TPU v7x, 32 devices: a whole 2x2x4 slice. The times are simulated.
32 devices in a mesh: dp: 8 (over z, y), tensor: 4 (over x, core).
Axes of the slice: x: 2, y: 2, z: 4, core: 2. Of those that a mesh axis runs over, the one named last changes fastest.
Arguments:
- tokens: bfloat16 [2, 8192, 1024], P(None, ('dp', 'tensor')), may hold values from -6 to 6
- cotangent: float32 [2, 8192, 1024], P(None, ('dp', 'tensor')), may hold values from -6 to 6
- slot_order: int32 [2, 8, 1024], P(None, 'dp'), may hold values from 0 to 1023, each once within a row
- lengths: int32 [2, 8, 3], P(None, 'dp'), may hold values from 1 to 512, 1024 in all within a row
- live_mask: int32 [2, 8, 1024], P(None, 'dp'), may hold values 0 or 1
- w_in: float32 [4, 1024, 1024], P(None, 'dp', 'tensor'), may hold values from -0.1875 to 0.1875
- w_out: float32 [1024, 1024], P('tensor', 'dp'), may hold values from -0.75 to 0.75
- w_ff: float32 [2, 1024, 2816], P(None, 'dp', 'tensor'), may hold values from -0.1875 to 0.1875
- w_down: float32 [2816, 1024], P('tensor', 'dp'), may hold values from -0.21875 to 0.21875
- norm_gains: float32 [2, 1024], replicated, may hold values from 0.5 to 1.5
- conv_taps: float32 [3, 4, 1024], P(None, None, 'tensor'), may hold values from -3 to 3
- decay_w: float32 [1024, 8], P(None, 'tensor'), may hold values from -0.09375 to 0.09375
- mesa_bias: float32 [2, 8], P(None, 'tensor'), may hold values from -7 to -3
- mom_in: float32 [4, 1024, 1024], P(None, 'dp', 'tensor'), may hold values from -12 to 12
- mom_out: float32 [1024, 1024], P('tensor', 'dp'), may hold values from -12 to 12
- mom_ff: float32 [2, 1024, 2816], P(None, 'dp', 'tensor'), may hold values from -12 to 12
- mom_down: float32 [2816, 1024], P('tensor', 'dp'), may hold values from -12 to 12
- mom_gains: float32 [2, 1024], replicated, may hold values from -96 to 96
- mom_conv: float32 [3, 4, 1024], P(None, None, 'tensor'), may hold values from -8 to 8
- mom_decay: float32 [1024, 8], P(None, 'tensor'), may hold values from -8 to 8
- mom_bias: float32 [2, 8], P(None, 'tensor'), may hold values from -8 to 8
- err_in: float32 [8, 4, 1024, 1024], P('dp', None, None, 'tensor'), may hold values from -14 to 14
- err_out: float32 [8, 1024, 1024], P('dp', 'tensor'), may hold values from -14 to 14
- err_ff: float32 [8, 2, 1024, 2816], P('dp', None, None, 'tensor'), may hold values from -14 to 14
- err_down: float32 [8, 2816, 1024], P('dp', 'tensor'), may hold values from -14 to 14
- basis_in: float32 [4, 1024, 8], P(None, 'tensor'), may hold values from -6 to 6
- basis_out: float32 [4, 1024, 8], P('tensor'), may hold values from -6 to 6
- basis_ff: float32 [2, 2816, 8], P(None, 'tensor'), may hold values from -6 to 6
- basis_down: float32 [4, 1024, 8], P('tensor'), may hold values from -6 to 6
Outputs:
- out_tokens: bfloat16 [2, 8192, 1024], P(None, ('dp', 'tensor'))
- d_tokens: float32 [2, 8192, 1024], P(None, ('dp', 'tensor'))
- w_in_new: float32 [4, 1024, 1024], P(None, 'dp', 'tensor')
- mom_in_new: float32 [4, 1024, 1024], P(None, 'dp', 'tensor')
- err_in_new: float32 [8, 4, 1024, 1024], P('dp', None, None, 'tensor')
- basis_in_new: float32 [4, 1024, 8], P(None, 'tensor')
- w_out_new: float32 [1024, 1024], P('tensor', 'dp')
- mom_out_new: float32 [1024, 1024], P('tensor', 'dp')
- err_out_new: float32 [8, 1024, 1024], P('dp', 'tensor')
- basis_out_new: float32 [4, 1024, 8], P('tensor')
- w_ff_new: float32 [2, 1024, 2816], P(None, 'dp', 'tensor')
- mom_ff_new: float32 [2, 1024, 2816], P(None, 'dp', 'tensor')
- err_ff_new: float32 [8, 2, 1024, 2816], P('dp', None, None, 'tensor')
- basis_ff_new: float32 [2, 2816, 8], P(None, 'tensor')
- w_down_new: float32 [2816, 1024], P('tensor', 'dp')
- mom_down_new: float32 [2816, 1024], P('tensor', 'dp')
- err_down_new: float32 [8, 2816, 1024], P('dp', 'tensor')
- basis_down_new: float32 [4, 1024, 8], P('tensor')
- gains_new: float32 [2, 1024], replicated
- mom_gains_new: float32 [2, 1024], replicated
- conv_new: float32 [3, 4, 1024], P(None, None, 'tensor')
- mom_conv_new: float32 [3, 4, 1024], P(None, None, 'tensor')
- decay_new: float32 [1024, 8], P(None, 'tensor')
- mom_decay_new: float32 [1024, 8], P(None, 'tensor')
- bias_new: float32 [2, 8], P(None, 'tensor')
- mom_bias_new: float32 [2, 8], P(None, 'tensor')
Inputs may be any that keep to these rules, and one draw needn't show every extreme that they name: `slot_order`: each row is a permutation of the pack's 1024 slots: entry j names the group slot placed at packed position j. Each row holds 3 lengths that sum to 1024; the largest is exactly 512.
All inputs are finite; a program needn't handle non-finite values. No bound on the sum of `live_mask` on one device may be relied on, other than what follows from the above.
Results may differ from a plain program's by a relative error of at most 0.033.
Values may be sent and summed in bfloat16 or wider, within the bound.
No kernel may reach another device: no remote copies, remote signals or barrier semaphores. Data moves between devices by JAX's collectives and lax.ppermute only.
A program may use at most 448 MiB of HBM per device.

v0:
```python
import jax
import jax.numpy as jnp
from jax import lax
from jax.sharding import PartitionSpec as P

D = 1024
CG_STEPS = 8
STRETCH = 64


precise = lax.Precision.HIGHEST
tiny_eps = 1e-06
solve_floor = 0.01
momentum_decay = 0.5
step_rate = 1.0
small_rate = 0.05
ridge_shift = 9.0


def rms_norm(values, gain):
    return values * lax.rsqrt(jnp.mean(values * values, axis=-1, keepdims=True) + tiny_eps) * gain


def shift_rows(matrix, offset):
    return jnp.pad(matrix, ((offset, 0), (0, 0)))[: matrix.shape[0]]


def shift_ids(seg_ids, offset):
    return jnp.concatenate(
        [jnp.full((offset,), -1, jnp.int32), seg_ids[: seg_ids.shape[0] - offset]]
    )


def short_conv(projected, tap_weights, seg_ids):
    result = projected * tap_weights[0]
    for offset in range(1, tap_weights.shape[0]):
        same_seg = (shift_ids(seg_ids, offset) == seg_ids)[:, None]
        result = (
            result + jnp.where(same_seg, shift_rows(projected, offset), 0.0) * tap_weights[offset]
        )
    return result


def segment_ids(length_row, total_rows):
    seq_ends = jnp.cumsum(length_row)
    places = jnp.arange(total_rows, dtype=jnp.int32)
    return jnp.sum((places[:, None] >= seq_ends[None, :]).astype(jnp.int32), axis=1)


def mesa_head(queries, key_rows, values, log_decay, ridge_term, seg_ids):
    row_count, head_width = queries.shape
    block_count = row_count // STRETCH
    queries = queries.reshape(block_count, STRETCH, head_width)
    key_rows = key_rows.reshape(block_count, STRETCH, head_width)
    values = values.reshape(block_count, STRETCH, head_width)
    cumulative = jnp.cumsum(log_decay.reshape(block_count, STRETCH), axis=1)
    seg_block = seg_ids.reshape(block_count, STRETCH)
    previous = jnp.concatenate([jnp.full((1,), -1, jnp.int32), seg_block[:-1, -1]])
    from_start = jnp.where(seg_block == previous[:, None], jnp.exp(cumulative), 0.0)
    causal = jnp.arange(STRETCH)[:, None] >= jnp.arange(STRETCH)[None, :]
    allowed = causal[None] & (seg_block[:, :, None] == seg_block[:, None, :])
    spread = jnp.where(allowed, cumulative[:, :, None] - cumulative[:, None, :], 0.0)
    within = jnp.where(allowed, jnp.exp(spread), 0.0)
    last_seg = seg_block[:, -1:]
    to_end = jnp.where(seg_block == last_seg, jnp.exp(cumulative[:, -1:] - cumulative), 0.0)
    keep_end = jnp.where(last_seg[:, 0] == previous, jnp.exp(cumulative[:, -1]), 0.0)
    key_sums = jnp.einsum("ncd,nc,nce->nde", key_rows, to_end, key_rows, precision=precise)
    value_sums = jnp.einsum("ncv,nc,ncd->nvd", values, to_end, key_rows, precision=precise)

    def advance(state_pair, pieces):
        key_state, value_state = state_pair
        keep_now, key_add, value_add = pieces
        new_pair = (keep_now * key_state + key_add, keep_now * value_state + value_add)
        return (new_pair, state_pair)

    zero_state = jnp.zeros((head_width, head_width), jnp.float32)
    unused, starts = lax.scan(advance, (zero_state, zero_state), (keep_end, key_sums, value_sums))
    key_start, value_start = starts

    def apply_ridge(vectors):
        scores = jnp.einsum("ncd,ntd->nct", vectors, key_rows, precision=precise) * within
        inside = jnp.einsum("nct,ntd->ncd", scores, key_rows, precision=precise)
        state_part = jnp.einsum("ncd,nde->nce", vectors, key_start, precision=precise)
        return ridge_term * vectors + from_start[:, :, None] * state_part + inside

    def solve_raw(state_now):
        solved, residual, direction, norm_now = state_now
        image = apply_ridge(direction)
        curvature = jnp.sum(direction * image, axis=2, keepdims=True)
        step_size = norm_now / (curvature + solve_floor)
        solved = solved + step_size * direction
        residual = residual - step_size * image
        norm_next = jnp.sum(residual * residual, axis=2, keepdims=True)
        direction = residual + norm_next / (norm_now + solve_floor) * direction
        return (solved, residual, direction, norm_next)

    solve_step = jax.checkpoint(solve_raw)
    state_now = (
        jnp.zeros_like(queries),
        queries,
        queries,
        jnp.sum(queries * queries, axis=2, keepdims=True),
    )
    for step_index in range(CG_STEPS):
        state_now = solve_step(state_now)
    solved = state_now[0]
    scores = jnp.einsum("ncd,ntd->nct", solved, key_rows, precision=precise) * within
    inside = jnp.einsum("nct,ntv->ncv", scores, values, precision=precise)
    state_part = jnp.einsum("ncd,nvd->ncv", solved, value_start, precision=precise)
    return (from_start[:, :, None] * state_part + inside).reshape(row_count, head_width)


def mixer_core(pre_q, pre_k, pre_v, pre_g, pre_a, tap_weights, head_rows, seg_ids, live_slots):
    row_count = pre_q.shape[0]
    head_count = pre_a.shape[1]
    head_width = pre_q.shape[1] // head_count

    def prepared(projected, taps_now):
        return jax.nn.silu(short_conv(projected, taps_now, seg_ids)).reshape(
            row_count, head_count, head_width
        )

    queries = prepared(pre_q, tap_weights[0])
    queries = queries * lax.rsqrt(jnp.sum(queries * queries, axis=2, keepdims=True) + tiny_eps)
    key_rows = prepared(pre_k, tap_weights[1])
    key_rows = (
        key_rows
        * lax.rsqrt(jnp.sum(key_rows * key_rows, axis=2, keepdims=True) + tiny_eps)
        * live_slots[:, None, None]
    )
    values = prepared(pre_v, tap_weights[2]) * live_slots[:, None, None]
    log_decay = -jax.nn.softplus(pre_a + head_rows[0])
    ridge_term = jax.nn.softplus(head_rows[1] + ridge_shift)
    solved = jax.vmap(mesa_head, in_axes=(1, 1, 1, 1, 0, None), out_axes=1)(
        queries, key_rows, values, log_decay, ridge_term, seg_ids
    )
    return solved.reshape(row_count, head_count * head_width) * jax.nn.sigmoid(pre_g)


def orthonormal(sketch):
    columns = []
    for position in range(sketch.shape[2]):
        column = sketch[:, :, position]
        for earlier in columns:
            column = column - jnp.sum(earlier * column, axis=1, keepdims=True) * earlier
        column = column * lax.rsqrt(jnp.sum(column * column, axis=1, keepdims=True) + tiny_eps)
        columns.append(column)
    return jnp.stack(columns, axis=2)


def project_left(merged, basis_now):
    return jnp.einsum("smn,snr->smr", merged, basis_now, precision=precise)


def project_right(merged, frame):
    return jnp.einsum("smn,smr->snr", merged, frame, precision=precise)


def rebuild(frame, basis_new):
    return jnp.einsum("smr,snr->smn", frame, basis_new, precision=precise)


def advance_weight(weight, moment, grad_now, rate):
    moment_new = momentum_decay * moment + grad_now
    return (weight - rate * moment_new, moment_new)


def on_device(
    tokens,
    cotangent,
    slot_order,
    lengths,
    live_mask,
    w_in,
    w_out,
    w_ff,
    w_down,
    norm_gains,
    conv_taps,
    decay_w,
    mesa_bias,
    mom_in,
    mom_out,
    mom_ff,
    mom_down,
    mom_gains,
    mom_conv,
    mom_decay,
    mom_bias,
    err_in,
    err_out,
    err_ff,
    err_down,
    basis_in,
    basis_out,
    basis_ff,
    basis_down,
):
    dp_count = lax.axis_size("dp")
    dp_index = lax.axis_index("dp")
    shard_count = lax.axis_size("tensor")
    low_in = w_in.astype(jnp.bfloat16)
    low_out = w_out.astype(jnp.bfloat16)
    low_ff = w_ff.astype(jnp.bfloat16)
    low_down = w_down.astype(jnp.bfloat16)
    decay_low = decay_w.astype(jnp.bfloat16)
    rows_group = tokens.shape[1] * shard_count
    grad_in = jnp.zeros((4, D, w_in.shape[2]), jnp.float32)
    grad_out = jnp.zeros((w_out.shape[0], D), jnp.float32)
    grad_ff = jnp.zeros((2, D, w_ff.shape[2]), jnp.float32)
    grad_down = jnp.zeros((w_down.shape[0], D), jnp.float32)
    grad_decay = jnp.zeros(decay_w.shape, jnp.float32)
    grad_conv = jnp.zeros(conv_taps.shape, jnp.float32)
    grad_bias = jnp.zeros(mesa_bias.shape, jnp.float32)
    grad_gains = jnp.zeros(norm_gains.shape, jnp.float32)
    out_list = []
    back_list = []
    for micro_index in range(tokens.shape[0]):
        weights_in, weights_out, weights_ff, weights_down = (
            lax.all_gather(low_in, "dp", axis=1, tiled=True),
            lax.all_gather(low_out, "dp", axis=1, tiled=True),
            lax.all_gather(low_ff, "dp", axis=1, tiled=True),
            lax.all_gather(low_down, "dp", axis=1, tiled=True),
        )
        order_now = slot_order[micro_index, 0]
        inverse = (
            jnp.zeros((rows_group,), jnp.int32)
            .at[order_now]
            .set(jnp.arange(rows_group, dtype=jnp.int32))
        )
        seg_ids = segment_ids(lengths[micro_index, 0], rows_group)
        live_slots = live_mask[micro_index, 0].astype(jnp.float32)
        token_rows = tokens[micro_index].astype(jnp.float32)
        normed_one, norm_one_pull = jax.vjp(rms_norm, token_rows, norm_gains[0])
        group_one = lax.all_gather(normed_one.astype(jnp.bfloat16), "tensor", axis=0, tiled=True)
        packed = group_one[order_now]
        projected = jnp.einsum(
            "td,jdc->jtc", packed, weights_in, preferred_element_type=jnp.float32
        )
        pre_decay = jnp.dot(packed, decay_low, preferred_element_type=jnp.float32)

        def core_local(pre_q, pre_k, pre_v, pre_g, pre_a, tap_weights, head_rows):
            return mixer_core(
                pre_q, pre_k, pre_v, pre_g, pre_a, tap_weights, head_rows, seg_ids, live_slots
            )

        gated, core_pull = jax.vjp(
            core_local,
            projected[0],
            projected[1],
            projected[2],
            projected[3],
            pre_decay,
            conv_taps,
            mesa_bias,
        )
        gated_low = gated.astype(jnp.bfloat16)
        mix_term = jnp.dot(gated_low, weights_out, preferred_element_type=jnp.float32)
        mixed = lax.psum_scatter(
            mix_term[inverse].astype(jnp.bfloat16), "tensor", scatter_dimension=0, tiled=True
        ).astype(jnp.float32)
        resid_one = token_rows + mixed
        normed_two, norm_two_pull = jax.vjp(rms_norm, resid_one, norm_gains[1])
        group_two = lax.all_gather(normed_two.astype(jnp.bfloat16), "tensor", axis=0, tiled=True)
        gate_up = jnp.einsum(
            "td,jdh->jth", group_two, weights_ff, preferred_element_type=jnp.float32
        )
        gate_sig = jax.nn.sigmoid(gate_up[0])
        gate_act = gate_up[0] * gate_sig
        hidden = (gate_act * gate_up[1]).astype(jnp.bfloat16)
        ffn_term = jnp.dot(hidden, weights_down, preferred_element_type=jnp.float32)
        ffn_total = lax.psum_scatter(
            ffn_term.astype(jnp.bfloat16), "tensor", scatter_dimension=0, tiled=True
        ).astype(jnp.float32)
        out_list.append((resid_one + ffn_total).astype(jnp.bfloat16))
        back_rows = cotangent[micro_index]
        d_ffn = lax.all_gather(back_rows.astype(jnp.bfloat16), "tensor", axis=0, tiled=True)
        grad_down = grad_down + jnp.einsum(
            "th,td->hd", hidden, d_ffn, preferred_element_type=jnp.float32
        )
        d_hidden = jnp.einsum("td,hd->th", d_ffn, weights_down, preferred_element_type=jnp.float32)
        d_gate = d_hidden * gate_up[1] * gate_sig * (1.0 + gate_up[0] * (1.0 - gate_sig))
        d_gate_up = jnp.stack([d_gate, d_hidden * gate_act]).astype(jnp.bfloat16)
        grad_ff = grad_ff + jnp.einsum(
            "td,jth->jdh", group_two, d_gate_up, preferred_element_type=jnp.float32
        )
        d_two = jnp.einsum("jth,jdh->td", d_gate_up, weights_ff, preferred_element_type=jnp.float32)
        d_two_rows = lax.psum_scatter(
            d_two.astype(jnp.bfloat16), "tensor", scatter_dimension=0, tiled=True
        ).astype(jnp.float32)
        d_resid_part, d_gain_two = norm_two_pull(d_two_rows)
        d_resid = back_rows + d_resid_part
        d_mix = lax.all_gather(d_resid.astype(jnp.bfloat16), "tensor", axis=0, tiled=True)[
            order_now
        ]
        grad_out = grad_out + jnp.einsum(
            "tc,td->cd", gated_low, d_mix, preferred_element_type=jnp.float32
        )
        d_gated = jnp.einsum("td,cd->tc", d_mix, weights_out, preferred_element_type=jnp.float32)
        d_query, d_key, d_value, d_gatepre, d_decay, d_taps, d_head = core_pull(d_gated)
        d_proj = jnp.stack([d_query, d_key, d_value, d_gatepre]).astype(jnp.bfloat16)
        d_decay_low = d_decay.astype(jnp.bfloat16)
        grad_in = grad_in + jnp.einsum(
            "td,jtc->jdc", packed, d_proj, preferred_element_type=jnp.float32
        )
        grad_decay = grad_decay + jnp.einsum(
            "td,th->dh", packed, d_decay_low, preferred_element_type=jnp.float32
        )
        d_packed = jnp.einsum(
            "jtc,jdc->td", d_proj, weights_in, preferred_element_type=jnp.float32
        ) + jnp.einsum("th,dh->td", d_decay_low, decay_low, preferred_element_type=jnp.float32)
        d_one_rows = lax.psum_scatter(
            d_packed[inverse].astype(jnp.bfloat16), "tensor", scatter_dimension=0, tiled=True
        ).astype(jnp.float32)
        d_token_part, d_gain_one = norm_one_pull(d_one_rows)
        back_list.append(d_resid + d_token_part)
        grad_conv = grad_conv + d_taps
        grad_bias = grad_bias + d_head
        grad_gains = grad_gains + jnp.stack([d_gain_one, d_gain_two])
    merged_in = grad_in + err_in[0]
    merged_out = grad_out[None] + err_out
    merged_ff = grad_ff + err_ff[0]
    merged_down = grad_down[None] + err_down
    summed = lax.psum(
        (
            project_left(merged_in, basis_in),
            project_left(merged_out, basis_out),
            project_left(merged_ff, basis_ff),
            project_left(merged_down, basis_down),
            grad_conv,
            grad_decay,
            grad_bias,
        ),
        "dp",
    )
    frame_in = orthonormal(summed[0] / dp_count)
    frame_out = orthonormal(summed[1] / dp_count)
    frame_ff = orthonormal(summed[2] / dp_count)
    frame_down = orthonormal(summed[3] / dp_count)
    basis_sums = lax.psum(
        (
            project_right(merged_in, frame_in),
            project_right(merged_out, frame_out),
            project_right(merged_ff, frame_ff),
            project_right(merged_down, frame_down),
        ),
        "dp",
    )
    basis_in_new = basis_sums[0] / dp_count
    basis_out_new = basis_sums[1] / dp_count
    basis_ff_new = basis_sums[2] / dp_count
    basis_down_new = basis_sums[3] / dp_count
    approx_in = rebuild(frame_in, basis_in_new)
    approx_out = rebuild(frame_out, basis_out_new)
    approx_ff = rebuild(frame_ff, basis_ff_new)
    approx_down = rebuild(frame_down, basis_down_new)
    err_in_new = (merged_in - approx_in)[None]
    err_out_new = merged_out - approx_out
    err_ff_new = (merged_ff - approx_ff)[None]
    err_down_new = merged_down - approx_down
    owned_in = lax.dynamic_slice_in_dim(approx_in, dp_index * w_in.shape[1], w_in.shape[1], 1)
    owned_out = lax.dynamic_slice_in_dim(
        approx_out[0], dp_index * w_out.shape[1], w_out.shape[1], 1
    )
    owned_ff = lax.dynamic_slice_in_dim(approx_ff, dp_index * w_ff.shape[1], w_ff.shape[1], 1)
    owned_down = lax.dynamic_slice_in_dim(
        approx_down[0], dp_index * w_down.shape[1], w_down.shape[1], 1
    )
    w_in_new, mom_in_new = advance_weight(w_in, mom_in, owned_in, step_rate)
    w_out_new, mom_out_new = advance_weight(w_out, mom_out, owned_out, step_rate)
    w_ff_new, mom_ff_new = advance_weight(w_ff, mom_ff, owned_ff, step_rate)
    w_down_new, mom_down_new = advance_weight(w_down, mom_down, owned_down, step_rate)
    gain_total = lax.psum(grad_gains, ("dp", "tensor")) / dp_count
    gains_new, mom_gains_new = advance_weight(norm_gains, mom_gains, gain_total, small_rate)
    conv_new, mom_conv_new = advance_weight(conv_taps, mom_conv, summed[4] / dp_count, small_rate)
    decay_new, mom_decay_new = advance_weight(decay_w, mom_decay, summed[5] / dp_count, small_rate)
    bias_new, mom_bias_new = advance_weight(mesa_bias, mom_bias, summed[6] / dp_count, small_rate)
    out_tokens = jnp.stack(out_list)
    d_tokens = jnp.stack(back_list)
    return (
        out_tokens,
        d_tokens,
        w_in_new,
        mom_in_new,
        err_in_new,
        basis_in_new,
        w_out_new,
        mom_out_new,
        err_out_new,
        basis_out_new,
        w_ff_new,
        mom_ff_new,
        err_ff_new,
        basis_ff_new,
        w_down_new,
        mom_down_new,
        err_down_new,
        basis_down_new,
        gains_new,
        mom_gains_new,
        conv_new,
        mom_conv_new,
        decay_new,
        mom_decay_new,
        bias_new,
        mom_bias_new,
    )


def solution(mesh):
    placed = (
        P(None, ("dp", "tensor"), None),
        P(None, ("dp", "tensor"), None),
        P(None, "dp", None),
        P(None, "dp", None),
        P(None, "dp", None),
        P(None, "dp", "tensor"),
        P("tensor", "dp"),
        P(None, "dp", "tensor"),
        P("tensor", "dp"),
        P(),
        P(None, None, "tensor"),
        P(None, "tensor"),
        P(None, "tensor"),
        P(None, "dp", "tensor"),
        P("tensor", "dp"),
        P(None, "dp", "tensor"),
        P("tensor", "dp"),
        P(),
        P(None, None, "tensor"),
        P(None, "tensor"),
        P(None, "tensor"),
        P("dp", None, None, "tensor"),
        P("dp", "tensor", None),
        P("dp", None, None, "tensor"),
        P("dp", "tensor", None),
        P(None, "tensor", None),
        P("tensor", None, None),
        P(None, "tensor", None),
        P("tensor", None, None),
    )
    return jax.shard_map(
        on_device,
        mesh=mesh,
        in_specs=placed,
        out_specs=(
            P(None, ("dp", "tensor"), None),
            P(None, ("dp", "tensor"), None),
            P(None, "dp", "tensor"),
            P(None, "dp", "tensor"),
            P("dp", None, None, "tensor"),
            P(None, "tensor", None),
            P("tensor", "dp"),
            P("tensor", "dp"),
            P("dp", "tensor", None),
            P("tensor", None, None),
            P(None, "dp", "tensor"),
            P(None, "dp", "tensor"),
            P("dp", None, None, "tensor"),
            P(None, "tensor", None),
            P("tensor", "dp"),
            P("tensor", "dp"),
            P("dp", "tensor", None),
            P("tensor", None, None),
            P(),
            P(),
            P(None, None, "tensor"),
            P(None, None, "tensor"),
            P(None, "tensor"),
            P(None, "tensor"),
            P(None, "tensor"),
            P(None, "tensor"),
        ),
        check_vma=False,
    )
```

profile of v0, /device:TPU:0, one launch (start us, length us, event | category | flops | bytes accessed | tf_op | source)
XLA Modules:
  0.0 2331.1 jit_solution(7056127156139961874)
XLA Ops:
  29.6 30.7 %all_gather.42 = bf16[256,1024]{1,0:T(8,128)(2,1)} all-gather(bf16[256,128]{1,0:T(8,128)(2,1)S(1)} %convert_element_type.183), channel_id=1, replica_groups=mesh['dp'=8,'tensor'=4] {'dp'}, dimensions={1}, use_global_device_ids=true | all-gather | bytes 589824 | tf_op jit(solution)/shard_map/all_gather | solution.py:221
  60.6 7.4 gather_fusion
  70.1 7.9 gather_fusion.2
  82.4 33.5 %all-gather.14.cloned.1.call-done = bf16[4,1024,256]{2,1,0:T(8,128)(2,1)} async-done(((bf16[4,128,256]{2,1,0:T(8,128)(2,1)}), bf16[4,1024,256]{2,1,0:T(8,128)(2,1)}) %all-gather.14.cloned.1.call-update) | async-done | bytes 2097168 | tf_op jit(solution)/shard_map/all_gather | solution.py:220
  136.5 6.1 fusion.444
  155.4 15.4 multiply_reduce_fusion.166
  185.0 115.5 %while.90 = (s32[]{:T(128)}, f32[2,128,128]{2,1,0:T(8,128)}, f32[2,128,128]{2,1,0:T(8,128)}, f32[16,2,128,128]{3,2,1,0:T(8,128)S(1)}, f32[16,2,128,128]{3,2,1,0:...) while((s32[]{:T(128)}, f32[2,128,128]{2,1,0:T(8,128)}, ...), condition=%wide.region_8.11_spmd.clone, body=%wide.region_7.10_spmd.clone.sunk | while | flops 262147 | bytes 1835696 | solution.py:77
  368.8 16.5 multiply_reduce_fusion.148
  392.6 5.2 convolution_bitcast_fusion.6
  400.9 116.6 %while.91 = (s32[]{:T(128)}, f32[2,128,128]{2,1,0:T(8,128)}, f32[2,128,128]{2,1,0:T(8,128)}, f32[16,2,128,128]{3,2,1,0:T(8,128)}, f32[16,2,128,128]{3,2,1,0:T(8,...) while((s32[]{:T(128)}, f32[2,128,128]{2,1,0:T(8,128)}, ...), condition=%wide.region_36.39_spmd.clone, body=%wide.region_35.38_spmd.clone.sunk | while | flops 262147 | bytes 1835696 | solution.py:77
  588.0 7.9 gather_fusion.1
  624.5 5.3 gather_fusion.3
  631.9 28.6 %reduce-scatter.13.cloned.1.call-done = bf16[256,1024]{1,0:T(8,128)(2,1)} async-done(((bf16[1024,1024]{1,0:T(8,128)(2,1)}), bf16[256,1024]{1,0:T(8,128)(2,1)}) %reduce-scatter.13.cloned.1.call-update) | async-done | bytes 524304 | tf_op jit(solution)/shard_map/reduce_scatter | solution.py:259
  669.5 53.6 %all-gather.18.cloned.1.call-done = bf16[2,1024,704]{1,2,0:T(8,128)(2,1)} async-done(((bf16[2,128,704]{1,2,0:T(8,128)(2,1)}), bf16[2,1024,704]{1,2,0:T(8,128)(2,1)}) %all-gather.18.cloned.1.call-update) | async-done | bytes 2883600 | tf_op jit(solution)/shard_map/all_gather | solution.py:222
  723.0 22.9 all-gather.16.cloned.1.call-done
  746.0 8.2 convolution_bitcast_fusion.1
  754.1 38.3 %all-gather.20.cloned.1.call-done = bf16[704,1024]{1,0:T(8,128)(2,1)} async-done(((bf16[704,128]{1,0:T(8,128)(2,1)}), bf16[704,1024]{1,0:T(8,128)(2,1)}) %all-gather.20.cloned.1.call-update) | async-done | bytes 1441808 | tf_op jit(solution)/shard_map/all_gather | solution.py:223
  792.5 23.1 all-gather.26.cloned.1.call-done
  815.6 7.7 fusion.117
  829.4 10.3 all-gather.24.cloned.1.call-done
  839.6 8.2 convolution_bitcast_fusion
  847.8 16.0 all-gather.30.cloned.1.call-done
  863.8 6.4 fusion.118
  885.9 5.4 copy.1748
  892.0 6.3 reduce-scatter.17.cloned.1.call-done
  898.3 34.7 %reduce-scatter.21.cloned.1.call-done = bf16[256,1024]{1,0:T(8,128)(2,1)} async-done(((bf16[1024,1024]{1,0:T(8,128)(2,1)}), bf16[256,1024]{1,0:T(8,128)(2,1)}) %reduce-scatter.21.cloned.1.call-update) | async-done | bytes 524304 | tf_op jit(solution)/shard_map/reduce_scatter | solution.py:288
  936.4 30.5 %reduce-scatter.15.cloned.1.call-done = bf16[256,1024]{1,0:T(8,128)(2,1)} async-done(((bf16[1024,1024]{1,0:T(8,128)(2,1)}), bf16[256,1024]{1,0:T(8,128)(2,1)}) %reduce-scatter.15.cloned.1.call-update) | async-done | bytes 524304 | tf_op jit(solution)/shard_map/reduce_scatter | solution.py:272
  966.8 34.0 %reduce-scatter.11.cloned.1.call-done = bf16[256,1024]{1,0:T(8,128)(2,1)} async-done(((bf16[1024,1024]{1,0:T(8,128)(2,1)}), bf16[256,1024]{1,0:T(8,128)(2,1)}) %reduce-scatter.11.cloned.1.call-update) | async-done | bytes 524304 | tf_op jit(solution)/shard_map/reduce_scatter | solution.py:272
  1000.8 5.7 fusion.828
  1007.1 5.8 fusion.19
  1012.9 5.5 bitcast_add_fusion.8
  1032.0 8.1 gather_fusion.4
  1196.5 5.2 fusion.414
  1201.7 5.6 fusion.417
  1217.4 5.3 fusion.426
  1233.0 8.1 gather_fusion.6
  1400.8 5.4 fusion.397
  1419.0 5.2 fusion.406
  1474.9 7.6 add_add_fusion.16
  1486.2 7.8 add_add_fusion.1
  1497.1 107.0 %while.92 = (s32[]{:T(128)}, f32[2,128,128]{2,1,0:T(8,128)}, f32[2,128,128]{2,1,0:T(8,128)}, f32[16,2]{1,0:T(8,128)S(1)}, f32[16,2,128,128]{3,2,1,0:T(8,128)}, /...) while((s32[]{:T(128)}, f32[2,128,128]{2,1,0:T(8,128)}, ...), condition=%wide.region_99.102_spmd.clone, body=%wide.region_96.101_spmd.clone.sunk | while | flops 393218 | bytes 2621728 | solution.py:77
  1640.0 6.0 fusion.157
  1652.6 7.0 fusion.185
  1691.6 7.8 add_add_fusion.4
  1702.9 7.8 add_add_fusion
  1713.9 82.7 %while.93 = (s32[]{:T(128)}, f32[2,128,128]{2,1,0:T(8,128)}, f32[2,128,128]{2,1,0:T(8,128)}, f32[16,2]{1,0:T(8,128)S(1)}, f32[16,2,128,128]{3,2,1,0:T(8,128)}, /...) while((s32[]{:T(128)}, f32[2,128,128]{2,1,0:T(8,128)}, ...), condition=%wide.region_159.162_spmd.clone, body=%wide.region_156.161_spmd.clone.sunk | while | flops 393218 | bytes 2097412 | solution.py:77
  1832.6 5.4 fusion.191
  1858.5 6.8 multiply_reduce_fusion.38
  1889.7 37.2 %all-reduce.79 = (f32[1,256,8]{1,2,0:T(8,128)S(1)}, f32[1,704,8]{1,2,0:T(8,128)S(1)}) all-reduce(f32[1,256,8]{1,2,0:T(8,128)S(1)} %convolution_bitcast_fusion.11, f32[1,704,8]{1,2,0:T(8,128)S(1)} %copy-done.418), channel_id=1, replica_groups=mesh['dp'=8,'tensor'=4] {'dp'}, use_global_device_ids=true, to_apply=%region_214.217 | all-reduce | flops 7680 | bytes 61440 | tf_op jit(solution)/shard_map/psum | solution.py:324
  1967.3 17.6 subtract_multiply_fusion.27
  2006.8 5.7 multiply_reduce_fusion.228
  2030.2 17.6 subtract_multiply_fusion.20
  2053.2 6.1 fusion.556
  2061.5 53.9 %all-reduce.86.cloned.1.call-done = (f32[4,1024,8]{1,0,2:T(4,128)}, f32[2,1024,8]{1,0,2:T(2,128)}) async-done(((f32[4,1024,8]{1,0,2:T(4,128)}, f32[2,1024,8]{1,0,2:T(2,128)}), (f32[4,1024,8]{1,0,2:T(4,128)}, f32[2,1024,8]{1,0,2:T(2,128)})) %all-reduce.86.cloned.1.call-update) | async-done | bytes 196624 | tf_op jit(solution)/shard_map/psum | solution.py:324
  2121.9 6.5 fusion.557
  2131.9 7.5 fusion.561
  2142.7 5.3 gather_fusion.5
  2155.0 5.4 gather_fusion.7
  2160.4 49.4 %all-reduce.84.cloned.1.call-done = (f32[4,256,8]{1,2,0:T(8,128)}, f32[1,1024,8]{1,2,0:T(8,128)}, f32[2,704,8]{1,2,0:T(8,128)}, f32[1,1024,8]{1,2,0:T(8,128)}, f...) async-done(((f32[4,256,8]{1,2,0:T(8,128)}, f32[1,1024,8]{1,2,0:T(8,128)}, f32[2,704,8]{1,2,0:T(8,128)}, f32[1,1024,8]{1,2,0:T(8,128)}, ...) | async-done | bytes 163872 | tf_op jit(solution)/shard_map/psum | solution.py:340
  2215.7 5.4 copy.1754
  2221.1 7.0 subtract_bitcast_fusion.1
  2228.1 5.7 copy.1758
  2256.3 22.2 reduce-scatter.23.cloned.1.call-done
  2280.7 39.4 %psum.92 = f32[2,1024]{1,0:T(2,128)S(1)} all-reduce(f32[2,1024]{1,0:T(2,128)S(1)} %maximum_add_fusion), channel_id=1, replica_groups=mesh['dp'=8,'tensor'=4] {'dp','tensor'}, use_global_device_ids=true, to_apply=%region_332.335 | all-reduce | flops 2048 | bytes 16384 | tf_op jit(solution)/shard_map/psum | solution.py:373
  (2322 shorter events, 1417.0 us)
Async XLA Ops:
  7.2 1011.2 %copy-start = (f32[2,704,8]{1,2,0:T(8,128)S(1)}, f32[2,704,8]{1,2,0:T(8,128)}, u32[]{:S(2)}) copy-start(f32[2,704,8]{1,2,0:T(8,128)} %param.66) | copy-start | bytes 135172
  7.2 53.4 %all-gather.12.cloned.1.call-start = ((), (), s32[]{:S(2)}) async-start(), calls=%async_computation.8 | async-start | bytes 2621440 | tf_op jit(solution)/shard_map/all_gather | solution.py:235
  13.4 56.7 %all-gather.22.cloned.1.call-start = ((), (), s32[]{:S(2)}) async-start(), calls=%async_computation.15 | async-start | bytes 2621440 | tf_op jit(solution)/shard_map/all_gather | solution.py:235
  14.2 101.7 %all-gather.14.cloned.1.call-start = ((), (), s32[]{:S(2)}) async-start(), calls=%async_computation.9 | async-start | bytes 2359296 | tf_op jit(solution)/shard_map/all_gather | solution.py:220
  15.0 616.8 %reduce-scatter.9.cloned.1.call-start = ((), (), s32[]{:S(2)}) async-start(), calls=%async_computation.10 | async-start | bytes 2621440 | tf_op jit(solution)/shard_map/reduce_scatter | solution.py:259
  16.6 51.4 %copy-start.477 = (s32[1024]{0:T(1024)}, s32[1024]{0:T(1024)S(1)}, u32[]{:S(2)}) copy-start(s32[1024]{0:T(1024)S(1)} %broadcast_clamp_fusion.1) | copy-start | bytes 12292
  16.6 53.4 %copy-start.475 = (s32[1024]{0:T(1024)}, s32[1024]{0:T(1024)S(1)}, u32[]{:S(2)}) copy-start(s32[1024]{0:T(1024)S(1)} %broadcast_clamp_fusion) | copy-start | bytes 12292
  16.8 52.6 %copy-start.532 = (pred[16]{0:T(512)(128)(4,1)}, pred[16]{0:T(512)(128)(4,1)S(1)}, u32[]{:S(2)}) copy-start(pred[16]{0:T(512)(128)(4,1)S(1)} %fusion.808) | copy-start | bytes 52
  16.8 61.1 %copy-start.414 = (bf16[1024,2]{0,1:T(2,128)(2,1)}, bf16[1024,2]{0,1:T(2,128)(2,1)S(1)}, u32[]{:S(2)}) copy-start(bf16[1024,2]{0,1:T(2,128)(2,1)S(1)} %convert_element_type.178) | copy-start | bytes 12292
  27.4 102.0 %copy-start.456 = (pred[1024]{0:T(1024)(128)(4,1)}, pred[1024]{0:T(1024)(128)(4,1)S(1)}, u32[]{:S(2)}) copy-start(pred[1024]{0:T(1024)(128)(4,1)S(1)} %get-tuple-element.2497) | copy-start | bytes 3076
  27.4 102.0 %copy-start.458 = (pred[1024]{0:T(1024)(128)(4,1)}, pred[1024]{0:T(1024)(128)(4,1)S(1)}, u32[]{:S(2)}) copy-start(pred[1024]{0:T(1024)(128)(4,1)S(1)} %get-tuple-element.2498) | copy-start | bytes 3076
  28.1 52.8 %copy-start.531 = (pred[16]{0:T(512)(128)(4,1)}, pred[16]{0:T(512)(128)(4,1)S(1)}, u32[]{:S(2)}) copy-start(pred[16]{0:T(512)(128)(4,1)S(1)} %fusion.809) | copy-start | bytes 52
  28.7 143.4 %copy-start.416 = (f32[1,1,1024]{2,1,0:T(1,128)}, f32[1,1,1024]{2,1,0:T(1,128)S(1)}, u32[]{:S(2)}) copy-start(f32[1,1,1024]{2,1,0:T(1,128)S(1)} %get-tuple-element.2483) | copy-start | bytes 12292
  28.8 52.8 %copy-start.489 = (pred[16,64]{1,0:T(8,128)(4,1)}, pred[16,64]{1,0:T(8,128)(4,1)S(1)}, u32[]{:S(2)}) copy-start(pred[16,64]{1,0:T(8,128)(4,1)S(1)} %get-tuple-element.2482) | copy-start | bytes 3076
  28.8 52.8 %copy-start.495 = (pred[16,64]{1,0:T(8,128)(4,1)}, pred[16,64]{1,0:T(8,128)(4,1)S(1)}, u32[]{:S(2)}) copy-start(pred[16,64]{1,0:T(8,128)(4,1)S(1)} %get-tuple-element.2481) | copy-start | bytes 3076
  28.9 53.4 %copy-start.488 = (pred[16,64]{1,0:T(8,128)(4,1)}, pred[16,64]{1,0:T(8,128)(4,1)S(1)}, u32[]{:S(2)}) copy-start(pred[16,64]{1,0:T(8,128)(4,1)S(1)} %get-tuple-element.2488) | copy-start | bytes 3076
  28.9 53.4 %copy-start.494 = (pred[16,64]{1,0:T(8,128)(4,1)}, pred[16,64]{1,0:T(8,128)(4,1)S(1)}, u32[]{:S(2)}) copy-start(pred[16,64]{1,0:T(8,128)(4,1)S(1)} %get-tuple-element.2487) | copy-start | bytes 3076
  68.0 47.9 %copy-start.134 = (bf16[1024,1024]{1,0:T(8,128)(2,1)}, bf16[1024,1024]{1,0:T(8,128)(2,1)S(1)}, u32[]{:S(2)}) copy-start(bf16[1024,1024]{1,0:T(8,128)(2,1)S(1)} %gather_fusion) | copy-start | bytes 6291460
  80.9 35.0 %copy-start.479 = (f32[2,16]{1,0:T(2,128)}, f32[2,16]{1,0:T(2,128)S(1)}, u32[]{:S(2)}) copy-start(f32[2,16]{1,0:T(2,128)S(1)} %slice_reduce_fusion) | copy-start | bytes 388
  82.4 310.2 %copy-start.325 = (f32[2,16,64]{2,1,0:T(8,128)}, f32[2,16,64]{2,1,0:T(8,128)S(1)}, u32[]{:S(2)}) copy-start(f32[2,16,64]{2,1,0:T(8,128)S(1)} %get-tuple-element.2464) | copy-start | bytes 24580
  82.4 535.2 %copy-start.132 = (f32[2,16,64]{2,1,0:T(8,128)}, f32[2,16,64]{2,1,0:T(8,128)S(1)}, u32[]{:S(2)}) copy-start(f32[2,16,64]{2,1,0:T(8,128)S(1)} %get-tuple-element.1044) | copy-start | bytes 24580
  135.7 36.5 %copy-start.207 = (f32[1024,2,128]{2,0,1:T(8,128)}, f32[1024,2,128]{2,0,1:T(8,128)S(1)}, u32[]{:S(2)}) copy-start(f32[1024,2,128]{2,0,1:T(8,128)S(1)} %copy.1552) | copy-start | bytes 3145732
  136.4 35.7 %copy-start.421 = (f32[1024,2]{0,1:T(2,128)}, f32[1024,2]{0,1:T(2,128)S(1)}, u32[]{:S(2)}) copy-start(f32[1024,2]{0,1:T(2,128)S(1)} %add_rsqrt_fusion.2) | copy-start | bytes 24580
  300.6 52.8 %copy-start.4 = (f32[16,2,128,128]{3,2,1,0:T(8,128)}, f32[16,2,128,128]{3,2,1,0:T(8,128)S(1)}, u32[]{:S(2)}) copy-start(f32[16,2,128,128]{3,2,1,0:T(8,128)S(1)} %get-tuple-element.949) | copy-start | bytes 6291460
  385.4 138.0 %copy-start.68 = (f32[2,1024,128]{2,1,0:T(8,128)}, f32[2,1024,128]{2,1,0:T(8,128)S(1)}, u32[]{:S(2)}) copy-start(f32[2,1024,128]{2,1,0:T(8,128)S(1)} %copy.1572) | copy-start | bytes 3145732
  387.4 224.0 %copy-start.2 = (f32[1024,2,128]{2,0,1:T(8,128)}, f32[1024,2,128]{2,0,1:T(8,128)S(1)}, u32[]{:S(2)}) copy-start(f32[1024,2,128]{2,0,1:T(8,128)S(1)} %get-tuple-element.2500) | copy-start | bytes 3145732
  533.9 73.7 %copy-start.29 = (f32[2,16,64,128]{3,2,1,0:T(8,128)}, f32[2,16,64,128]{3,2,1,0:T(8,128)S(1)}, u32[]{:S(2)}) copy-start(f32[2,16,64,128]{3,2,1,0:T(8,128)S(1)} %multiply_add_fusion.20) | copy-start | bytes 3145732
  560.8 39.2 %copy-start.347 = (f32[2,16,64]{2,1,0:T(8,128)}, f32[2,16,64]{2,1,0:T(8,128)S(1)}, u32[]{:S(2)}) copy-start(f32[2,16,64]{2,1,0:T(8,128)S(1)} %get-tuple-element.2295) | copy-start | bytes 24580
  595.9 64.6 %reduce-scatter.13.cloned.1.call-start = ((), (), s32[]{:S(2)}) async-start(), calls=%async_computation.16 | async-start | bytes 2621440 | tf_op jit(solution)/shard_map/reduce_scatter | solution.py:259
  629.9 30.6 %copy-start.82 = (bf16[2,256,1024]{2,1,0:T(8,128)(2,1)S(1)}, bf16[2,256,1024]{2,1,0:T(8,128)(2,1)}, u32[]{:S(2)}) copy-start(bf16[2,256,1024]{2,1,0:T(8,128)(2,1)} %param.39) | copy-start | bytes 3145732
  629.9 32.3 %copy-start.435 = (f32[1,1024]{1,0:T(1,128)S(1)}, f32[1,1024]{1,0:T(1,128)}, u32[]{:S(2)}) copy-start(f32[1,1024]{1,0:T(1,128)} %get-tuple-element.2477) | copy-start | bytes 12292
  629.9 93.1 %all-gather.18.cloned.1.call-start = ((), (), s32[]{:S(2)}) async-start(), calls=%async_computation.12 | async-start | bytes 3244032 | tf_op jit(solution)/shard_map/all_gather | solution.py:222
  631.8 114.2 %all-gather.16.cloned.1.call-start = ((), (), s32[]{:S(2)}) async-start(), calls=%async_computation.11 | async-start | bytes 2621440 | tf_op jit(solution)/shard_map/all_gather | solution.py:264
  631.9 30.4 %copy-start.254 = (bf16[256,1024]{1,0:T(8,128)(2,1)S(1)}, bf16[256,1024]{1,0:T(8,128)(2,1)}, u32[]{:S(2)}) copy-start(bf16[256,1024]{1,0:T(8,128)(2,1)} %reduce-scatter.9.cloned.1.call-done) | copy-start | bytes 1572868
  663.6 128.8 %all-gather.20.cloned.1.call-start = ((), (), s32[]{:S(2)}) async-start(), calls=%async_computation.13 | async-start | bytes 1622016 | tf_op jit(solution)/shard_map/all_gather | solution.py:223
  665.4 150.2 %all-gather.26.cloned.1.call-start = ((), (), s32[]{:S(2)}) async-start(), calls=%async_computation.19 | async-start | bytes 2621440 | tf_op jit(solution)/shard_map/all_gather | solution.py:277
  668.1 171.5 %all-gather.24.cloned.1.call-start = ((), (), s32[]{:S(2)}) async-start(), calls=%async_computation.17 | async-start | bytes 2621440 | tf_op jit(solution)/shard_map/all_gather | solution.py:264
  668.7 195.1 %all-gather.30.cloned.1.call-start = ((), (), s32[]{:S(2)}) async-start(), calls=%async_computation.23 | async-start | bytes 2621440 | tf_op jit(solution)/shard_map/all_gather | solution.py:277
  669.4 228.8 %reduce-scatter.17.cloned.1.call-start = ((), (), s32[]{:S(2)}) async-start(), calls=%async_computation.20 | async-start | bytes 2621440 | tf_op jit(solution)/shard_map/reduce_scatter | solution.py:288
  829.1 34.7 %copy-start.562 = (bf16[704,1024]{1,0:T(8,128)(2,1)S(1)}, bf16[704,1024]{1,0:T(8,128)(2,1)}, u32[]{:S(2)}) copy-start(bf16[704,1024]{1,0:T(8,128)(2,1)} %all-gather.20.cloned.1.call-done) | copy-start | bytes 4325380
  829.1 103.9 %reduce-scatter.21.cloned.1.call-start = ((), (), s32[]{:S(2)}) async-start(), calls=%async_computation.24 | async-start | bytes 2621440 | tf_op jit(solution)/shard_map/reduce_scatter | solution.py:288
  876.5 90.4 %reduce-scatter.15.cloned.1.call-start = ((), (), s32[]{:S(2)}) async-start(), calls=%async_computation.18 | async-start | bytes 2621440 | tf_op jit(solution)/shard_map/reduce_scatter | solution.py:272
  881.1 119.8 %reduce-scatter.11.cloned.1.call-start = ((), (), s32[]{:S(2)}) async-start(), calls=%async_computation.14 | async-start | bytes 2621440 | tf_op jit(solution)/shard_map/reduce_scatter | solution.py:272
  885.8 146.2 %all-gather.28.cloned.1.call-start = ((), (), s32[]{:S(2)}) async-start(), calls=%async_computation.21 | async-start | bytes 2621440 | tf_op jit(solution)/shard_map/all_gather | solution.py:293
  891.6 284.4 %copy-start.12 = (f32[2,16,64,64]{3,2,1,0:T(8,128)}, f32[2,16,64,64]{3,2,1,0:T(8,128)S(1)}, u32[]{:S(2)}) copy-start(f32[2,16,64,64]{3,2,1,0:T(8,128)S(1)} %fusion.441) | copy-start | bytes 1572868
  1006.5 226.5 %all-gather.32.cloned.1.call-start = ((), (), s32[]{:S(2)}) async-start(), calls=%async_computation.25 | async-start | bytes 2621440 | tf_op jit(solution)/shard_map/all_gather | solution.py:293
  1031.9 1083.6 %all-reduce.86.cloned.1.call-start = ((), (), s32[]{:S(2)}) async-start(), calls=%async_computation.28 | async-start | bytes 393216 | tf_op jit(solution)/shard_map/psum | solution.py:324
  1048.5 179.4 %copy-start.92 = (f32[2,1024,128]{2,1,0:T(8,128)}, f32[2,1024,128]{2,1,0:T(8,128)S(1)}, u32[]{:S(2)}) copy-start(f32[2,1024,128]{2,1,0:T(8,128)S(1)} %copy.1593) | copy-start | bytes 3145732
  1050.4 139.7 %copy-start.141 = (f32[2,16,64,64]{3,2,1,0:T(8,128)}, f32[2,16,64,64]{3,2,1,0:T(8,128)S(1)}, u32[]{:S(2)}) copy-start(f32[2,16,64,64]{3,2,1,0:T(8,128)S(1)} %fusion.854) | copy-start | bytes 1572868
  1054.5 124.4 %copy-start.16 = (f32[2,16,64,128]{3,2,1,0:T(8,128)}, f32[2,16,64,128]{3,2,1,0:T(8,128)S(1)}, u32[]{:S(2)}) copy-start(f32[2,16,64,128]{3,2,1,0:T(8,128)S(1)} %fusion.127) | copy-start | bytes 3145732
  1257.0 122.2 %copy-start.19 = (f32[2,16,64,128]{3,2,1,0:T(8,128)}, f32[2,16,64,128]{3,2,1,0:T(8,128)S(1)}, u32[]{:S(2)}) copy-start(f32[2,16,64,128]{3,2,1,0:T(8,128)S(1)} %fusion.130) | copy-start | bytes 3145732
  2048.4 161.4 %all-reduce.84.cloned.1.call-start = ((), (), s32[]{:S(2)}) async-start(), calls=%async_computation.27 | async-start | bytes 337920 | tf_op jit(solution)/shard_map/psum | solution.py:340
  2139.5 116.8 %reduce-scatter.19.cloned.1.call-start = ((), (), s32[]{:S(2)}) async-start(), calls=%async_computation.22 | async-start | bytes 2621440 | tf_op jit(solution)/shard_map/reduce_scatter | solution.py:312
  2148.1 130.4 %reduce-scatter.23.cloned.1.call-start = ((), (), s32[]{:S(2)}) async-start(), calls=%async_computation.26 | async-start | bytes 2621440 | tf_op jit(solution)/shard_map/reduce_scatter | solution.py:312
  2252.3 26.1 %copy-start.83 = (bf16[2,256,1024]{2,1,0:T(8,128)(2,1)S(1)}, bf16[2,256,1024]{2,1,0:T(8,128)(2,1)}, u32[]{:S(2)}) copy-start(bf16[2,256,1024]{2,1,0:T(8,128)(2,1)} %param.39) | copy-start | bytes 3145732
  2252.4 26.1 %copy-start.434 = (f32[1,1024]{1,0:T(1,128)S(1)}, f32[1,1024]{1,0:T(1,128)}, u32[]{:S(2)}) copy-start(f32[1,1024]{1,0:T(1,128)} %copy-done.433) | copy-start | bytes 12292
  2252.4 26.1 %copy-start.497 = (f32[256]{0:T(256)S(1)}, f32[256]{0:T(256)}, u32[]{:S(2)}) copy-start(f32[256]{0:T(256)} %copy-done.496) | copy-start | bytes 3076
  2252.4 26.1 %copy-start.499 = (f32[256]{0:T(256)S(1)}, f32[256]{0:T(256)}, u32[]{:S(2)}) copy-start(f32[256]{0:T(256)} %copy-done.498) | copy-start | bytes 3076
  2256.3 24.4 %copy-start.500 = (f32[1024]{0:T(1024)S(1)}, f32[1024]{0:T(1024)}, u32[]{:S(2)}) copy-start(f32[1024]{0:T(1024)} %get-tuple-element.1742) | copy-start | bytes 12292
  2256.3 24.4 %copy-start.501 = (f32[1024]{0:T(1024)S(1)}, f32[1024]{0:T(1024)}, u32[]{:S(2)}) copy-start(f32[1024]{0:T(1024)} %get-tuple-element.1755) | copy-start | bytes 12292
  2256.3 63.8 %copy-start.521 = (f32[256]{0:T(256)S(1)}, f32[256]{0:T(256)}, u32[]{:S(2)}) copy-start(f32[256]{0:T(256)} %copy-done.520) | copy-start | bytes 3076
  2256.3 63.8 %copy-start.523 = (f32[256]{0:T(256)S(1)}, f32[256]{0:T(256)}, u32[]{:S(2)}) copy-start(f32[256]{0:T(256)} %copy-done.522) | copy-start | bytes 3076
  2256.3 63.8 %copy-start.288 = (f32[256,1024]{1,0:T(8,128)S(1)}, f32[256,1024]{1,0:T(8,128)}, u32[]{:S(2)}) copy-start(f32[256,1024]{1,0:T(8,128)} %get-tuple-element.2260) | copy-start | bytes 3145732
  2256.3 63.8 %copy-start.289 = (f32[256,1024]{1,0:T(8,128)S(1)}, f32[256,1024]{1,0:T(8,128)}, u32[]{:S(2)}) copy-start(f32[256,1024]{1,0:T(8,128)} %get-tuple-element.2354) | copy-start | bytes 3145732
  (549 other events, 2547.6 us)
Sparse Core Ops, SparseCore 0:
  13.5 25.2 all-gather.11
  41.0 22.5 all-gather.21
  66.4 49.4 all-gather.13
  596.0 29.8 reduce-scatter.8
  630.0 30.4 reduce-scatter.12
  663.0 60.0 all-gather.17
  725.2 20.7 all-gather.15
  748.6 43.8 all-gather.19
  794.6 20.9 all-gather.25
  817.0 22.5 all-gather.23
  841.2 22.5 all-gather.29
  866.8 31.4 reduce-scatter.16
  901.5 31.4 reduce-scatter.20
  935.4 31.4 reduce-scatter.14
  969.4 31.4 reduce-scatter.10
  1006.6 22.5 all-gather.27
  1032.0 22.6 all-gather.31
  2048.5 66.8 all-reduce.85
  2139.6 70.2 all-reduce.83
  2212.8 31.4 reduce-scatter.18
  2247.0 31.3 reduce-scatter.22
where the time goes:
time: 2350 us; the launch traced here: 2330 us
  matrix products  752 us (32%)
  other arithmetic  565 us (24%)
  waiting for transfers between devices  460 us (20%)
  local copies, waits for them, and re-layouts  408 us (17%)
  blocking collectives  107 us (5%)
  between operations  34.8 us (1%)
    dot_general x64, matrix products, apply_ridge(): jnp.einsum('ncd,nde->nce', vectors, key_start, precision=precise)  231 us
    while x160, local copies, waits for them, and re-layouts  147 us
    dot_general x64, matrix products, apply_ridge(): inside = jnp.einsum('nct,ntd->ncd', scores, key_rows, precision=precise)  135 us
    dot_general x64, matrix products, apply_ridge(): jnp.einsum('ncd,ntd->nct', vectors, key_rows, precision=precise) * within  131 us
    dynamic_update_slice x64, other arithmetic, mesa_head(): lax.scan(advance, (zero_state, zero_state), (keep_end, key_sums, value_su...  86.2 us
    reduce_scatter x2, waiting for transfers between devices, on_device(): lax.psum_scatter(ffn_term.astype(jnp.bfloat16), 'tensor', scatter_dimensi...  64.5 us
    reduce_sum x32, other arithmetic, advance(): keep_now * key_state + key_add  62 us
    reduce_sum x37, other arithmetic, orthonormal(): column = column - jnp.sum(earlier * column, axis=1, keepdims=True) * earlier  60.6 us
  transfers between devices with their start and end apart: 21, of which 15 were waited for; matrix products, arithmetic and copies ran while one was open for 19% of the time, Pallas kernels for 0%

commit v1 on v0

v1 whole, which is shorter than its diff:
```python
import functools

import jax
import jax.numpy as jnp
from jax import lax
from jax.experimental import pallas as pl
from jax.experimental.pallas import tpu as pltpu
from jax.sharding import PartitionSpec as P

CG_STEPS = 8
BLK = 128
tiny_eps = 1e-06
solve_floor = 0.01
ridge_shift = 9.0
precise = lax.Precision.HIGHEST
F32 = jnp.float32
BF = jnp.bfloat16


def softplus(x):
    return jnp.maximum(x, 0.0) + jnp.log1p(jnp.exp(-jnp.abs(x)))


def mm(a, b):
    return jnp.dot(a, b, preferred_element_type=F32)


def nt(a, b):
    return lax.dot_general(a, b, (((1,), (1,)), ((), ())), preferred_element_type=F32)


def col_sum(x):
    return jnp.sum(x, axis=0, keepdims=True)


def start_of(lens_ref, places):
    begin = jnp.zeros_like(places)
    edge = jnp.int32(0)
    for item in range(lens_ref.shape[0] - 1):
        edge = edge + lens_ref[item]
        begin = jnp.where(places >= edge, edge, begin)
    return begin


def conv_masks(lens_ref, total, taps):
    places = lax.broadcasted_iota(jnp.int32, (1, total), 1)
    begin = start_of(lens_ref, places)
    return [(places - i >= begin).astype(F32) for i in range(taps)]


def conv_rows(rows, taps_now, masks):
    acc = rows * taps_now[:, 0:1]
    for i in range(1, len(masks)):
        acc = acc + (pltpu.roll(rows, i, 1) * masks[i]) * taps_now[:, i : i + 1]
    return acc


CHUNK = 16


def set_up(head, proj_ref, prea_ref, taps_ref, live_ref, lens_ref, bias_ref, sc):
    width, total = proj_ref.shape[1], proj_ref.shape[2]
    blocks = total // BLK
    taps = taps_ref.shape[2]
    masks = conv_masks(lens_ref, total, taps)
    live = live_ref[...]

    def squares(j, dst):
        def body(c, acc):
            at = pl.ds(pl.multiple_of(c * CHUNK, CHUNK), CHUNK)
            u = conv_rows(proj_ref[j, at, :], taps_ref[j, at, :], masks)
            x = u * jax.nn.sigmoid(u)
            dst[at, :] = x
            return acc + x * x

        acc = lax.fori_loop(0, width // CHUNK, body, jnp.zeros((CHUNK, total), F32))
        return lax.rsqrt(col_sum(acc) + tiny_eps)

    scale_q = squares(0, sc["q"])
    scale_k = squares(1, sc["x"])
    sc["scale"][0:1, :] = scale_q
    sc["scale"][1:2, :] = scale_k
    scale_k = scale_k * live
    for n in range(blocks):
        at = pl.ds(n * BLK, BLK)
        sc["q"][:, at] = sc["q"][:, at] * scale_q[:, n * BLK : (n + 1) * BLK]
        kt = sc["x"][:, at] * scale_k[:, n * BLK : (n + 1) * BLK]
        sc["kt"][:, at] = kt.astype(BF)
        sc["ks"][n, 0:BLK, :] = kt.T.astype(BF)
    squares(2, sc["x"])
    for n in range(blocks):
        at = pl.ds(n * BLK, BLK)
        vt = sc["x"][:, at] * live[:, n * BLK : (n + 1) * BLK]
        sc["vt"][:, at] = vt.astype(BF)
        if "vg" in sc:
            sc["vg"][n, 0:BLK, :] = vt.T.astype(BF)
    base = prea_ref[0, :, :] + jnp.full((1, total), bias_ref[0, head], F32)
    base = jnp.concatenate([base[:, n * BLK : (n + 1) * BLK] for n in range(blocks)], axis=0)
    forget = -softplus(base)
    row_i = lax.broadcasted_iota(jnp.int32, (BLK, BLK), 0)
    col_i = lax.broadcasted_iota(jnp.int32, (BLK, BLK), 1)
    cum = jnp.dot(forget, (row_i <= col_i).astype(F32), precision=precise, preferred_element_type=F32)
    first = lax.broadcasted_iota(jnp.int32, (blocks, BLK), 0) * BLK
    places = first + lax.broadcasted_iota(jnp.int32, (blocks, BLK), 1)
    begin = start_of(lens_ref, places)
    begin_last = start_of(lens_ref, first + (BLK - 1))
    end = jnp.broadcast_to(cum[:, BLK - 1 : BLK], cum.shape)
    from_start = jnp.where(begin < first, jnp.exp(cum), 0.0)
    to_end = jnp.where(places >= begin_last, jnp.exp(end - cum), 0.0)
    keep = jnp.where(begin_last < first, jnp.exp(end), 0.0)
    sc["dec"][0] = from_start
    sc["dec"][1] = to_end
    sc["dec"][2] = keep
    cum_col = jnp.transpose(cum)
    for n in range(blocks):
        spread = cum[n : n + 1, :] - cum_col[:, n : n + 1]
        allowed = (row_i <= col_i) & (row_i + n * BLK >= begin[n : n + 1, :])
        sc["dt"][n] = jnp.where(allowed, jnp.exp(jnp.where(allowed, spread, 0.0)), 0.0)
    state = jnp.zeros((2 * width, width), F32)
    for n in range(blocks):
        sc["ks"][n, BLK:, :] = state[:width].astype(BF)
        sc["g"][n] = state[width:].astype(BF)
        if "vg" in sc:
            sc["vg"][n, BLK:, :] = state[width:].T.astype(BF)
        if n + 1 < blocks:
            at = pl.ds(n * BLK, BLK)
            to_row = to_end[n : n + 1, :]
            scaled = jnp.concatenate(
                [sc["kt"][:, at].astype(F32) * to_row, sc["vt"][:, at].astype(F32) * to_row], axis=0
            ).astype(BF)
            state = keep[n : n + 1, :] * state + mm(scaled, sc["ks"][n, 0:BLK, :])
    return softplus(jnp.full((1, BLK), bias_ref[1, head], F32) + ridge_shift)


def apply_ridge(n, vec, lam, sc):
    at = pl.ds(n * BLK, BLK)
    both = mm(sc["ks"][n], vec.astype(BF))
    scores = (sc["dt"][n] * both[:BLK]).astype(BF)
    inside = mm(sc["kt"][:, at], scores)
    state_part = sc["dec"][0, n : n + 1, :] * both[BLK:]
    return lam * vec + state_part + inside, both, scores, state_part


def solve(lam, sc, keep_all):
    blocks = sc["dt"].shape[0]
    for n in range(blocks):
        at = pl.ds(n * BLK, BLK)
        q = sc["q"][:, at]
        sc["rho"][0:1, at] = col_sum(q * q)
        sc["z"][:, at] = jnp.zeros_like(q)
        if keep_all:
            sc["ph"][0, :, at] = q
        else:
            sc["p"][:, at] = q
            sc["r"][:, at] = q

    def step(i, last):
        for n in range(blocks):
            at = pl.ds(n * BLK, BLK)
            if keep_all:
                p = sc["ph"][i, :, at]
            else:
                p = sc["p"][:, at]
            rho = sc["rho"][0:1, at]
            w, both, scores, state_part = apply_ridge(n, p, lam, sc)
            inv_c = 1.0 / (col_sum(p * w) + solve_floor)
            s = rho * inv_c
            sc["z"][:, at] = sc["z"][:, at] + s * p
            if keep_all:
                sc["wh"][i, :, at] = w
                sc["bh"][i, n] = scores
                sc["sh"][i, 0:1, at] = s
                sc["sh"][i, 1:2, at] = inv_c
            if not last:
                if keep_all:
                    q = sc["q"][:, at]
                    r = jnp.where(i == 0, q, sc["rh"][jnp.maximum(i - 1, 0), :, at]) - s * w
                    sc["rh"][i, :, at] = r
                else:
                    r = sc["r"][:, at] - s * w
                    sc["r"][:, at] = r
                rho_next = col_sum(r * r)
                inv_rho = 1.0 / (rho + solve_floor)
                beta = rho_next * inv_rho
                p_next = r + beta * p
                sc["rho"][0:1, at] = rho_next
                if keep_all:
                    sc["ph"][i + 1, :, at] = p_next
                    sc["sh"][i, 2:3, at] = inv_rho
                    sc["sh"][i, 3:4, at] = beta
                else:
                    sc["p"][:, at] = p_next

    def body(i, carry):
        step(i, False)
        return carry

    lax.fori_loop(0, CG_STEPS - 1, body, 0)
    step(CG_STEPS - 1, True)


def forward_kernel(names, proj_ref, prea_ref, taps_ref, live_ref, lens_ref, bias_ref, out_ref, *scratch):
    sc = dict(zip(names, scratch))
    head = pl.program_id(0)
    lam = set_up(head, proj_ref, prea_ref, taps_ref, live_ref, lens_ref, bias_ref, sc)
    solve(lam, sc, False)
    for n in range(sc["dt"].shape[0]):
        at = pl.ds(n * BLK, BLK)
        z = sc["z"][:, at].astype(BF)
        scores = (sc["dt"][n] * mm(sc["ks"][n, 0:BLK, :], z)).astype(BF)
        o = mm(sc["vt"][:, at], scores) + sc["dec"][0, n : n + 1, :] * mm(sc["g"][n], z)
        out_ref[:, at] = (o * jax.nn.sigmoid(proj_ref[3, :, at])).astype(BF)


def backward_kernel(
    names, proj_ref, prea_ref, taps_ref, live_ref, dg_ref, lens_ref, bias_ref,
    dproj_ref, da_ref, dtaps_ref, dhead_ref, *scratch
):
    sc = dict(zip(names, scratch))
    head = pl.program_id(0)
    width, total = proj_ref.shape[1], proj_ref.shape[2]
    blocks = total // BLK
    lam = set_up(head, proj_ref, prea_ref, taps_ref, live_ref, lens_ref, bias_ref, sc)
    solve(lam, sc, True)
    row_i = lax.broadcasted_iota(jnp.int32, (BLK, BLK), 0)
    col_i = lax.broadcasted_iota(jnp.int32, (BLK, BLK), 1)
    dkt, dvt, zb, rb_s, pb_s = sc["dkt"], sc["dvt"], sc["zb"], sc["rb"], sc["pb"]
    dlam = jnp.zeros((1, BLK), F32)

    last = CG_STEPS - 1
    for n in range(blocks):
        at = pl.ds(n * BLK, BLK)
        dt = sc["dt"][n]
        from_row = sc["dec"][0, n : n + 1, :]
        z = sc["z"][:, at]
        z_low = z.astype(BF)
        scores = (dt * mm(sc["ks"][n, 0:BLK, :], z_low)).astype(BF)
        o = mm(sc["vt"][:, at], scores) + from_row * mm(sc["g"][n], z_low)
        sig = jax.nn.sigmoid(proj_ref[3, :, at])
        dg = dg_ref[:, at]
        dproj_ref[3, :, at] = (dg * o * sig * (1.0 - sig)).astype(BF)
        do = (dg * sig).astype(BF)
        both = mm(sc["vg"][n], do)
        d_scores = (dt * both[:BLK]).astype(BF)
        state_part = from_row * both[BLK:]
        zbar = state_part + mm(sc["kt"][:, at], d_scores)
        zb[:, at] = zbar
        dvt[:, at] = nt(do, scores)
        sc["dg0"][n] = nt(do, (from_row * z).astype(BF))
        p = sc["ph"][last, :, at]
        w = sc["wh"][last, :, at]
        s = sc["sh"][last, 0:1, at]
        inv_c = sc["sh"][last, 1:2, at]
        sbar = col_sum(zbar * p)
        cbar = -sbar * s * inv_c
        wb = (cbar * p).astype(BF)
        pb_s[:, at] = s * zbar + (2.0 * cbar) * w
        rb_s[:, at] = jnp.zeros_like(p)
        sc["rho"][0:1, at] = sbar * inv_c
        kept = sc["bh"][last, n]
        w_both = mm(sc["ks"][n], wb)
        w_scores = (dt * w_both[:BLK]).astype(BF)
        w_state = from_row * w_both[BLK:]
        p_low = p.astype(BF)
        dkt[:, at] = nt(z_low, d_scores) + nt(wb, kept) + nt(p_low, w_scores)
        sc["ds0"][n] = nt(wb, (from_row * p).astype(BF))
        sc["xm"][n] = scores.astype(F32) * both[:BLK] + kept.astype(F32) * w_both[:BLK]
        sc["fm"][0:1, at] = col_sum(z * state_part + p * w_state)
        sc["fm"][1:2, at] = col_sum(wb.astype(F32) * p)

    def body(it, carry):
        i = CG_STEPS - 2 - it
        for n in range(blocks):
            at = pl.ds(n * BLK, BLK)
            dt = sc["dt"][n]
            from_row = sc["dec"][0, n : n + 1, :]
            p = sc["ph"][i, :, at]
            w = sc["wh"][i, :, at]
            r_next = sc["rh"][i, :, at]
            s = sc["sh"][i, 0:1, at]
            inv_c = sc["sh"][i, 1:2, at]
            inv_rho = sc["sh"][i, 2:3, at]
            beta = sc["sh"][i, 3:4, at]
            zbar = zb[:, at]
            pb_next = pb_s[:, at]
            beta_bar = col_sum(pb_next * p)
            rho_next_bar = sc["rho"][0:1, at] + beta_bar * inv_rho
            rb = rb_s[:, at] + pb_next + (2.0 * rho_next_bar) * r_next
            sbar = col_sum(zbar * p - rb * w)
            cbar = -sbar * s * inv_c
            sc["rho"][0:1, at] = sbar * inv_c - beta_bar * beta * inv_rho
            wb32 = cbar * p - s * rb
            wb = wb32.astype(BF)
            image, w_both, w_scores, w_state = apply_ridge(n, wb32, lam, sc)
            pb_s[:, at] = beta * pb_next + s * zbar + cbar * w + image
            rb_s[:, at] = rb
            kept = sc["bh"][i, n]
            p_low = p.astype(BF)
            dkt[:, at] += nt(wb, kept) + nt(p_low, w_scores)
            sc["ds0"][n] += nt(wb, (from_row * p).astype(BF))
            sc["xm"][n] += kept.astype(F32) * w_both[:BLK]
            sc["fm"][0:1, at] += col_sum(p * w_state)
            sc["fm"][1:2, at] += col_sum(wb32 * p)
        return carry

    lax.fori_loop(0, CG_STEPS - 1, body, 0)

    d_sym = jnp.zeros((width, width), F32)
    d_g = jnp.zeros((width, width), F32)
    g_rows = [None] * blocks
    f_rows = [None] * blocks
    x_rows = [None] * blocks
    keep_rows = [None] * blocks
    lower = (row_i >= col_i).astype(BF)
    before = row_i < col_i
    for n in reversed(range(blocks)):
        at = pl.ds(n * BLK, BLK)
        kt = sc["kt"][:, at]
        to_row = sc["dec"][1, n : n + 1, :]
        keep = sc["dec"][2, n : n + 1, :]
        if n + 1 < blocks:
            vt = sc["vt"][:, at]
            g_low = d_g.astype(BF)
            part_s = to_row * mm(d_sym.astype(BF), kt)
            part_v = to_row * mm(g_low, kt)
            part_k = to_row * mm(d_g.T.astype(BF), vt)
            dkt[:, at] += part_s + part_k
            dvt[:, at] += part_v
            g_rows[n] = col_sum(0.5 * kt.astype(F32) * part_s + vt.astype(F32) * part_v)
            inner = 0.5 * d_sym * sc["ks"][n, BLK:, :].astype(F32) + d_g * sc["g"][n].astype(F32)
            keep_rows[n] = keep * jnp.sum(col_sum(inner), axis=1, keepdims=True)
        else:
            g_rows[n] = jnp.zeros((1, BLK), F32)
            keep_rows[n] = jnp.zeros((1, BLK), F32)
        ds0 = sc["ds0"][n]
        d_sym = keep * d_sym + ds0 + ds0.T
        d_g = keep * d_g + sc["dg0"][n]
        x = sc["xm"][n]
        high = x.astype(BF)
        low = (x - high.astype(F32)).astype(BF)
        summed = mm(high, lower) + mm(low, lower)
        x_rows[n] = col_sum(jnp.where(before, summed, 0.0))
        f_rows[n] = sc["fm"][0:1, at]
    f_all = jnp.concatenate(f_rows, axis=0)
    g_all = jnp.concatenate(g_rows, axis=0)
    da = (
        jnp.dot(f_all, (row_i >= col_i).astype(F32), precision=precise, preferred_element_type=F32)
        + jnp.dot(g_all, before.astype(F32), precision=precise, preferred_element_type=F32)
        + jnp.concatenate(x_rows, axis=0)
        + jnp.concatenate(keep_rows, axis=0)
    )
    da = jnp.concatenate([da[n : n + 1, :] for n in range(blocks)], axis=1)
    base = prea_ref[0, :, :] + jnp.full((1, total), bias_ref[0, head], F32)
    da = -jax.nn.sigmoid(base) * da
    da_ref[0, :, :] = da
    d_bias = jnp.sum(da, axis=1, keepdims=True)
    d_lam = jnp.sum(sc["fm"][1:2, :], axis=1, keepdims=True)
    d_lam = d_lam * jax.nn.sigmoid(jnp.full((1, BLK), bias_ref[1, head], F32) + ridge_shift)
    lane = lax.broadcasted_iota(jnp.int32, (1, BLK), 1)
    dhead_ref[0, :, :] = jnp.where(lane == 0, d_bias, d_lam)

    taps = taps_ref.shape[2]
    masks = conv_masks(lens_ref, total, taps)
    live = live_ref[...]
    scale_q = sc["scale"][0:1, :]
    scale_k = sc["scale"][1:2, :]

    def d_query(at):
        grad = rb_s[at, :] + pb_s[at, :] + (2.0 * sc["rho"][0:1, :]) * sc["q"][at, :]
        return grad

    def finish(j, grad_of, scale):
        def activated(at):
            u = conv_rows(proj_ref[j, at, :], taps_ref[j, at, :], masks)
            sig = jax.nn.sigmoid(u)
            return u, sig

        if scale is not None:

            def dots(c, acc):
                at = pl.ds(pl.multiple_of(c * CHUNK, CHUNK), CHUNK)
                u, sig = activated(at)
                return acc + (u * sig * scale) * grad_of(at)

            mean = col_sum(lax.fori_loop(0, width // CHUNK, dots, jnp.zeros((CHUNK, total), F32)))

        def body(c, carry):
            at = pl.ds(pl.multiple_of(c * CHUNK, CHUNK), CHUNK)
            u, sig = activated(at)
            grad = grad_of(at)
            if scale is not None:
                grad = scale * (grad - (u * sig * scale) * mean)
            du = grad * (sig * (1.0 + u * (1.0 - sig)))
            rows = proj_ref[j, at, :]
            taps_now = taps_ref[j, at, :]
            d_rows = du * taps_now[:, 0:1]
            sums = [jnp.sum(rows * du, axis=1, keepdims=True)]
            for i in range(1, taps):
                masked = du * masks[i]
                d_rows = d_rows + pltpu.roll(masked, total - i, 1) * taps_now[:, i : i + 1]
                sums.append(jnp.sum(pltpu.roll(rows, i, 1) * masked, axis=1, keepdims=True))
            dproj_ref[j, at, :] = d_rows.astype(BF)
            dtaps_ref[j, at, :] = jnp.concatenate(sums, axis=1)
            return carry

        lax.fori_loop(0, width // CHUNK, body, 0)

    finish(0, d_query, scale_q)
    finish(1, lambda at: dkt[at, :] * live, scale_k)
    finish(2, lambda at: dvt[at, :] * live, None)


def scratch_of(width, total, backward):
    blocks = total // BLK
    own = {
        "q": ((width, total), F32),
        "x": ((width, total), F32),
        "kt": ((width, total), BF),
        "vt": ((width, total), BF),
        "ks": ((blocks, 2 * BLK, width), BF),
        "g": ((blocks, width, width), BF),
        "dt": ((blocks, BLK, BLK), F32),
        "dec": ((3, blocks, BLK), F32),
        "scale": ((8, total), F32),
        "rho": ((8, total), F32),
        "z": ((width, total), F32),
    }
    if backward:
        own.update({
            "vg": ((blocks, 2 * BLK, width), BF),
            "ph": ((CG_STEPS, width, total), F32),
            "wh": ((CG_STEPS, width, total), F32),
            "rh": ((CG_STEPS, width, total), F32),
            "bh": ((CG_STEPS, blocks, BLK, BLK), BF),
            "sh": ((CG_STEPS, 8, total), F32),
            "dkt": ((width, total), F32),
            "dvt": ((width, total), F32),
            "zb": ((width, total), F32),
            "rb": ((width, total), F32),
            "pb": ((width, total), F32),
            "dg0": ((blocks, width, width), F32),
            "ds0": ((blocks, width, width), F32),
            "xm": ((blocks, BLK, BLK), F32),
            "fm": ((8, total), F32),
        })
    else:
        own.update({"p": ((width, total), F32), "r": ((width, total), F32)})
    return list(own), [pltpu.VMEM(shape, kind) for shape, kind in own.values()]


def mixer_forward(proj, pre_a, taps, live, lens, bias):
    slots, columns, total = proj.shape
    heads = pre_a.shape[0]
    width = columns // heads
    names, scratch = scratch_of(width, total, False)
    smem = pl.BlockSpec(memory_space=pltpu.SMEM)
    return pl.pallas_call(
        functools.partial(forward_kernel, names),
        grid=(heads,),
        in_specs=[
            pl.BlockSpec((slots, width, total), lambda h: (0, h, 0)),
            pl.BlockSpec((1, 1, total), lambda h: (h, 0, 0)),
            pl.BlockSpec((taps.shape[0], width, taps.shape[2]), lambda h: (0, h, 0)),
            pl.BlockSpec((1, total), lambda h: (0, 0)),
            smem,
            smem,
        ],
        out_specs=pl.BlockSpec((width, total), lambda h: (h, 0)),
        out_shape=jax.ShapeDtypeStruct((columns, total), BF),
        scratch_shapes=scratch,
        compiler_params=pltpu.CompilerParams(vmem_limit_bytes=56 * 2**20),
        name="mixer_forward",
    )(proj, pre_a, taps, live, lens, bias)


def mixer_backward(proj, pre_a, taps, live, d_gated, lens, bias):
    slots, columns, total = proj.shape
    heads = pre_a.shape[0]
    width = columns // heads
    names, scratch = scratch_of(width, total, True)
    smem = pl.BlockSpec(memory_space=pltpu.SMEM)
    kinds, count = taps.shape[0], taps.shape[2]
    return pl.pallas_call(
        functools.partial(backward_kernel, names),
        grid=(heads,),
        in_specs=[
            pl.BlockSpec((slots, width, total), lambda h: (0, h, 0)),
            pl.BlockSpec((1, 1, total), lambda h: (h, 0, 0)),
            pl.BlockSpec((kinds, width, count), lambda h: (0, h, 0)),
            pl.BlockSpec((1, total), lambda h: (0, 0)),
            pl.BlockSpec((width, total), lambda h: (h, 0)),
            smem,
            smem,
        ],
        out_specs=(
            pl.BlockSpec((slots, width, total), lambda h: (0, h, 0)),
            pl.BlockSpec((1, 1, total), lambda h: (h, 0, 0)),
            pl.BlockSpec((kinds, width, count), lambda h: (0, h, 0)),
            pl.BlockSpec((1, 1, BLK), lambda h: (h, 0, 0)),
        ),
        out_shape=(
            jax.ShapeDtypeStruct((slots, columns, total), BF),
            jax.ShapeDtypeStruct((heads, 1, total), F32),
            jax.ShapeDtypeStruct((kinds, columns, count), F32),
            jax.ShapeDtypeStruct((heads, 1, BLK), F32),
        ),
        scratch_shapes=scratch,
        compiler_params=pltpu.CompilerParams(vmem_limit_bytes=56 * 2**20),
        name="mixer_backward",
    )(proj, pre_a, taps, live, d_gated, lens, bias)


momentum_decay = 0.5
step_rate = 1.0
small_rate = 0.05


def rms_scale(values):
    return lax.rsqrt(jnp.mean(values * values, axis=-1, keepdims=True) + tiny_eps)


def rms_pull(values, scale, gain, grad):
    unit = values * scale
    scaled = grad * gain
    d_values = scale * (scaled - unit * jnp.mean(unit * scaled, axis=-1, keepdims=True))
    return d_values, jnp.sum(grad * unit, axis=0)


def swap(value, axis, flip):
    count = lax.axis_size(axis)
    return lax.ppermute(value, axis, [(i, i ^ flip) for i in range(count)])


def gather_rows(own):
    beside = swap(own, "tensor", 1)
    across = swap(own, "tensor", 2)
    corner = swap(across, "tensor", 1)
    return jnp.concatenate([own, beside, across, corner], axis=0)


def scatter_rows(terms):
    share = terms.shape[0] // 4
    low = terms.astype(jnp.bfloat16)
    from_beside = swap(jnp.concatenate([low[share : 2 * share], low[3 * share :]], axis=0), "tensor", 1)
    passed = terms[2 * share : 3 * share] + from_beside[share:].astype(jnp.float32)
    from_across = swap(passed.astype(jnp.bfloat16), "tensor", 2)
    mine = terms[:share] + from_beside[:share].astype(jnp.float32)
    return mine + from_across.astype(jnp.float32)


def total_over(values, axis):
    flip = 1
    while flip < lax.axis_size(axis):
        moved = [swap(v, axis, flip) for v in values]
        values = [a + b for a, b in zip(values, moved)]
        flip *= 2
    return values


def orthonormal_kernel(count, *refs):
    ranks = refs[0].shape[0]
    for source, target in zip(refs[:count], refs[count:]):
        columns = [source[r] for r in range(ranks)]
        for r in range(ranks):
            column = columns[r]
            column = column * lax.rsqrt(jnp.sum(column * column, axis=1, keepdims=True) + tiny_eps)
            target[r] = column
            for later in range(r + 1, ranks):
                dot = jnp.sum(column * columns[later], axis=1, keepdims=True)
                columns[later] = columns[later] - dot * column


def orthonormal(sketches):
    return pl.pallas_call(
        functools.partial(orthonormal_kernel, len(sketches)),
        out_shape=[jax.ShapeDtypeStruct(s.shape, s.dtype) for s in sketches],
        name="orthonormal",
    )(*sketches)


def project_left(merged, basis_now):
    return jnp.einsum("smn,snr->rsm", merged, basis_now, precision=precise)


def project_right(merged, frame):
    return jnp.einsum("smn,rsm->rsn", merged, frame, precision=precise)


def rebuild(frame, basis_new):
    return jnp.einsum("rsm,rsn->smn", frame, basis_new, precision=precise)


def advance_weight(weight, moment, grad_now, rate):
    moment_new = momentum_decay * moment + grad_now
    return (weight - rate * moment_new, moment_new)


def dot32(spec, a, b):
    return jnp.einsum(spec, a, b, preferred_element_type=jnp.float32)


def on_device(
    tokens,
    cotangent,
    slot_order,
    lengths,
    live_mask,
    w_in,
    w_out,
    w_ff,
    w_down,
    norm_gains,
    conv_taps,
    decay_w,
    mesa_bias,
    mom_in,
    mom_out,
    mom_ff,
    mom_down,
    mom_gains,
    mom_conv,
    mom_decay,
    mom_bias,
    err_in,
    err_out,
    err_ff,
    err_down,
    basis_in,
    basis_out,
    basis_ff,
    basis_down,
):
    dp_count = lax.axis_size("dp")
    dp_index = lax.axis_index("dp")
    mine = lax.axis_index("tensor")
    shard_count = lax.axis_size("tensor")
    micro_count, share, width = tokens.shape
    total = share * shard_count
    low_in = w_in.astype(jnp.bfloat16)
    low_out = w_out.astype(jnp.bfloat16)
    low_ff = w_ff.astype(jnp.bfloat16)
    low_down = w_down.astype(jnp.bfloat16)
    decay_low = decay_w.astype(jnp.bfloat16)
    weights_in = lax.all_gather(low_in, "dp", axis=1, tiled=True)
    weights_out = lax.all_gather(low_out, "dp", axis=1, tiled=True)
    weights_ff = lax.all_gather(low_ff, "dp", axis=1, tiled=True)
    weights_down = lax.all_gather(low_down, "dp", axis=1, tiled=True)
    taps_cols = jnp.transpose(conv_taps, (0, 2, 1))
    micros = range(micro_count)
    rows, scale_one, group_one, d_ffn, place, live, lens = [], [], [], [], [], [], []
    for m in micros:
        rows.append(tokens[m].astype(jnp.float32))
        scale_one.append(rms_scale(rows[m]))
        normed = rows[m] * scale_one[m] * norm_gains[0]
        group_one.append(gather_rows(normed.astype(jnp.bfloat16)))
        order_now = slot_order[m, 0]
        near = jnp.bitwise_xor(order_now // share, mine) * share + order_now % share
        slots = lax.broadcasted_iota(jnp.int32, (total, total), 1)
        place.append((near[:, None] == slots).astype(jnp.bfloat16))
        live.append(live_mask[m].astype(jnp.float32))
        lens.append(lengths[m, 0])
    for m in micros:
        d_ffn.append(gather_rows(cotangent[m].astype(jnp.bfloat16)))

    proj, pre_decay, gated_u, resid_one, scale_two, group_two = [], [], [], [], [], []
    for m in micros:
        packed = dot32("ji,id->jd", place[m], group_one[m]).astype(jnp.bfloat16)
        proj.append(dot32("jdc,td->jct", weights_in, packed))
        pre_decay.append(dot32("dh,td->ht", decay_low, packed)[:, None, :])
        gated = mixer_forward(proj[m], pre_decay[m], taps_cols, live[m], lens[m], mesa_bias)
        gated_u.append(dot32("cj,ji->ci", gated, place[m]).astype(jnp.bfloat16))
        mixed = scatter_rows(dot32("ci,cd->id", gated_u[m], weights_out))
        resid_one.append(rows[m] + mixed)
        scale_two.append(rms_scale(resid_one[m]))
        normed = resid_one[m] * scale_two[m] * norm_gains[1]
        group_two.append(gather_rows(normed.astype(jnp.bfloat16)))

    grad_down = jnp.zeros((w_down.shape[0], width), jnp.float32)
    grad_ff = jnp.zeros((2, width, w_ff.shape[2]), jnp.float32)
    out_list, d_two, d_resid, d_group = [], [], [], []
    grad_gains = []
    for m in micros:
        gate = dot32("td,dh->th", group_two[m], weights_ff[0])
        up = dot32("td,dh->th", group_two[m], weights_ff[1])
        gate_sig = jax.nn.sigmoid(gate)
        gate_act = gate * gate_sig
        hidden = (gate_act * up).astype(jnp.bfloat16)
        ffn = scatter_rows(dot32("th,hd->td", hidden, weights_down))
        out_list.append((resid_one[m] + ffn).astype(jnp.bfloat16))
        d_hidden = dot32("td,hd->th", d_ffn[m], weights_down)
        d_gate = (d_hidden * up * gate_sig * (1.0 + gate * (1.0 - gate_sig))).astype(jnp.bfloat16)
        d_up = (d_hidden * gate_act).astype(jnp.bfloat16)
        d_two = scatter_rows(
            dot32("th,dh->td", d_gate, weights_ff[0]) + dot32("th,dh->td", d_up, weights_ff[1])
        )
        grad_down = grad_down + dot32("th,td->hd", hidden, d_ffn[m])
        grad_ff = grad_ff + jnp.stack(
            [dot32("td,th->dh", group_two[m], d_gate), dot32("td,th->dh", group_two[m], d_up)]
        )
        d_part, d_gain = rms_pull(resid_one[m], scale_two[m], norm_gains[1], d_two)
        grad_gains.append(d_gain)
        d_resid.append(cotangent[m] + d_part)
        d_group.append(gather_rows(d_resid[m].astype(jnp.bfloat16)))

    grad_out = jnp.zeros((w_out.shape[0], width), jnp.float32)
    grad_in = jnp.zeros((4, width, w_in.shape[2]), jnp.float32)
    grad_decay = jnp.zeros(decay_w.shape, jnp.float32)
    grad_taps = jnp.zeros(taps_cols.shape, jnp.float32)
    grad_head = jnp.zeros((mesa_bias.shape[1], 1, BLK), jnp.float32)
    back_list = []
    gains_one = []
    for m in micros:
        grad_out = grad_out + dot32("ci,id->cd", gated_u[m], d_group[m])
        d_mix = dot32("ji,id->jd", place[m], d_group[m]).astype(jnp.bfloat16)
        d_gated = dot32("cd,td->ct", weights_out, d_mix)
        d_proj, d_decay, d_taps, d_head = mixer_backward(
            proj[m], pre_decay[m], taps_cols, live[m], d_gated, lens[m], mesa_bias
        )
        grad_taps = grad_taps + d_taps
        grad_head = grad_head + d_head
        d_proj = dot32("kcj,ji->kci", d_proj, place[m]).astype(jnp.bfloat16)
        d_decay = dot32("hj,ji->hi", d_decay[:, 0].astype(jnp.bfloat16), place[m]).astype(jnp.bfloat16)
        d_one = scatter_rows(
            dot32("kci,kdc->id", d_proj, weights_in) + dot32("hi,dh->id", d_decay, decay_low)
        )
        grad_in = grad_in + dot32("id,kci->kdc", group_one[m], d_proj)
        grad_decay = grad_decay + dot32("id,hi->dh", group_one[m], d_decay)
        d_part, d_gain = rms_pull(rows[m], scale_one[m], norm_gains[0], d_one)
        gains_one.append(d_gain)
        back_list.append(d_resid[m] + d_part)

    merged_in = grad_in + err_in[0]
    merged_out = grad_out[None] + err_out
    merged_ff = grad_ff + err_ff[0]
    merged_down = grad_down[None] + err_down
    merged = (merged_in, merged_out, merged_ff, merged_down)
    bases = (basis_in, basis_out, basis_ff, basis_down)
    early = total_over([project_left(merged[i], bases[i]) for i in (1, 2, 3)], "dp")
    frame_out, frame_ff, frame_down = orthonormal([s / dp_count for s in early])
    basis_early = total_over(
        [
            project_right(merged_out, frame_out),
            project_right(merged_ff, frame_ff),
            project_right(merged_down, frame_down),
        ],
        "dp",
    )
    late = total_over(
        [project_left(merged_in, basis_in), grad_taps, grad_decay, grad_head], "dp"
    )
    (frame_in,) = orthonormal([late[0] / dp_count])
    (basis_late,) = total_over([project_right(merged_in, frame_in)], "dp")
    grad_conv = jnp.transpose(late[1], (0, 2, 1))
    grad_decay = late[2]
    grad_bias = jnp.transpose(late[3][:, 0, :2])
    (gain_total,) = total_over([jnp.stack([sum(gains_one), sum(grad_gains)])], "tensor")
    (gain_total,) = total_over([gain_total], "dp")
    gain_total = gain_total / dp_count
    frames = (frame_in, frame_out, frame_ff, frame_down)
    sums = (basis_late, basis_early[0], basis_early[1], basis_early[2])
    basis_rows = [s / dp_count for s in sums]
    basis_in_new, basis_out_new, basis_ff_new, basis_down_new = (
        jnp.transpose(b, (1, 2, 0)) for b in basis_rows
    )
    approx_in, approx_out, approx_ff, approx_down = (
        rebuild(f, b) for f, b in zip(frames, basis_rows)
    )
    err_in_new = (merged_in - approx_in)[None]
    err_out_new = merged_out - approx_out
    err_ff_new = (merged_ff - approx_ff)[None]
    err_down_new = merged_down - approx_down

    def part(rows_of, count, axis):
        return lax.dynamic_slice_in_dim(rows_of, dp_index * count, count, axis)

    owned_in = rebuild(part(frame_in, w_in.shape[1], 2), basis_rows[0])
    owned_ff = rebuild(part(frame_ff, w_ff.shape[1], 2), basis_rows[2])
    owned_out = rebuild(frame_out, part(basis_rows[1], w_out.shape[1], 2))[0]
    owned_down = rebuild(frame_down, part(basis_rows[3], w_down.shape[1], 2))[0]
    w_in_new, mom_in_new = advance_weight(w_in, mom_in, owned_in, step_rate)
    w_out_new, mom_out_new = advance_weight(w_out, mom_out, owned_out, step_rate)
    w_ff_new, mom_ff_new = advance_weight(w_ff, mom_ff, owned_ff, step_rate)
    w_down_new, mom_down_new = advance_weight(w_down, mom_down, owned_down, step_rate)
    gains_new, mom_gains_new = advance_weight(norm_gains, mom_gains, gain_total, small_rate)
    conv_new, mom_conv_new = advance_weight(conv_taps, mom_conv, grad_conv / dp_count, small_rate)
    decay_new, mom_decay_new = advance_weight(decay_w, mom_decay, grad_decay / dp_count, small_rate)
    bias_new, mom_bias_new = advance_weight(mesa_bias, mom_bias, grad_bias / dp_count, small_rate)
    out_tokens = jnp.stack(out_list)
    d_tokens = jnp.stack(back_list)
    return (
        out_tokens,
        d_tokens,
        w_in_new,
        mom_in_new,
        err_in_new,
        basis_in_new,
        w_out_new,
        mom_out_new,
        err_out_new,
        basis_out_new,
        w_ff_new,
        mom_ff_new,
        err_ff_new,
        basis_ff_new,
        w_down_new,
        mom_down_new,
        err_down_new,
        basis_down_new,
        gains_new,
        mom_gains_new,
        conv_new,
        mom_conv_new,
        decay_new,
        mom_decay_new,
        bias_new,
        mom_bias_new,
    )


def solution(mesh):
    placed = (
        P(None, ("dp", "tensor"), None),
        P(None, ("dp", "tensor"), None),
        P(None, "dp", None),
        P(None, "dp", None),
        P(None, "dp", None),
        P(None, "dp", "tensor"),
        P("tensor", "dp"),
        P(None, "dp", "tensor"),
        P("tensor", "dp"),
        P(),
        P(None, None, "tensor"),
        P(None, "tensor"),
        P(None, "tensor"),
        P(None, "dp", "tensor"),
        P("tensor", "dp"),
        P(None, "dp", "tensor"),
        P("tensor", "dp"),
        P(),
        P(None, None, "tensor"),
        P(None, "tensor"),
        P(None, "tensor"),
        P("dp", None, None, "tensor"),
        P("dp", "tensor", None),
        P("dp", None, None, "tensor"),
        P("dp", "tensor", None),
        P(None, "tensor", None),
        P("tensor", None, None),
        P(None, "tensor", None),
        P("tensor", None, None),
    )
    return jax.shard_map(
        on_device,
        mesh=mesh,
        in_specs=placed,
        out_specs=(
            P(None, ("dp", "tensor"), None),
            P(None, ("dp", "tensor"), None),
            P(None, "dp", "tensor"),
            P(None, "dp", "tensor"),
            P("dp", None, None, "tensor"),
            P(None, "tensor", None),
            P("tensor", "dp"),
            P("tensor", "dp"),
            P("dp", "tensor", None),
            P("tensor", None, None),
            P(None, "dp", "tensor"),
            P(None, "dp", "tensor"),
            P("dp", None, None, "tensor"),
            P(None, "tensor", None),
            P("tensor", "dp"),
            P("tensor", "dp"),
            P("dp", "tensor", None),
            P("tensor", None, None),
            P(),
            P(),
            P(None, None, "tensor"),
            P(None, None, "tensor"),
            P(None, "tensor"),
            P(None, "tensor"),
            P(None, "tensor"),
            P(None, "tensor"),
        ),
        check_vma=False,
    )
```

time: 2350 us -> 819 us (0.35)
  matrix products: 752 us -> 176 us
  other arithmetic: 565 us -> 63.5 us
  local copies, waits for them, and re-layouts: 408 us -> 30.6 us
  waiting for transfers between devices: 460 us -> 155 us
  Pallas kernels: 0 us -> 274 us
  blocking collectives: 107 us -> 33.1 us
  starting transfers between devices: 2.12 us -> 62.9 us
    dot_general x264 -> x60, matrix products: 752 us -> 176 us  [the longest x44 127 us: dot32(): return jnp.einsum(spec, a, b, preferred_element_type=jnp.float32)]
    pallas_call x0 -> x6, Pallas kernels: none -> 274 us  [the longest x2 192 us: mixer_backward(): pl.pallas_call(functools.partial(backward_kernel, names), grid=(heads,),...]
    reduce_sum x176 -> x5, other arithmetic: 266 us -> 10.5 us  [the longest x3 6.2 us: rms_pull(): return (d_values, jnp.sum(grad * unit, axis=0))]
    all_gather x11 -> x3, waiting for transfers between devices: 198 us -> 0.02 us  [the longest x1 0.02 us: on_device(): weights_down = lax.all_gather(low_down, 'dp', axis=1, tiled=True)]
    reduce_scatter x8 -> x0, waiting for transfers between devices: 156 us -> none  [the longest x2 64.5 us: on_device(): lax.psum_scatter(ffn_term.astype(jnp.bfloat16), 'tensor', scatter_dimensi...]
    ppermute x0 -> x78, waiting for transfers between devices: none -> 155 us  [swap(): return lax.ppermute(value, axis, [(i, i ^ flip) for i in range(count)])]
    while x162 -> x0, local copies, waits for them, and re-layouts: 150 us -> none
    psum x2 -> x0, waiting for transfers between devices: 103 us -> none  [the longest x1 53.9 us: on_device(): lax.psum((project_left(merged_in, basis_in), project_left(merged_out, bas...]
  transfers between devices with their start and end apart: 21 -> 81, of which waited for: 15 -> 26; matrix products, arithmetic and copies ran while one was open for 19% -> 29% of each run, Pallas kernels for 0% -> 22%
where the time goes in v1:
time: 819 us; the launch traced here: 810 us
  Pallas kernels  274 us (33%)
  matrix products  176 us (21%)
  waiting for transfers between devices  155 us (19%)
  other arithmetic  63.5 us (8%)
  starting transfers between devices  62.9 us (8%)
  blocking collectives  33.1 us (4%)
  local copies, waits for them, and re-layouts  30.6 us (4%)
  between operations  15.9 us (2%)
    pallas_call x2, Pallas kernels, mixer_backward(): pl.pallas_call(functools.partial(backward_kernel, names), grid=(heads,),...  192 us
    ppermute x78, waiting for transfers between devices, swap(): return lax.ppermute(value, axis, [(i, i ^ flip) for i in range(count)])  155 us
    dot_general x44, matrix products, dot32(): return jnp.einsum(spec, a, b, preferred_element_type=jnp.float32)  127 us
    pallas_call x2, Pallas kernels, mixer_forward(): pl.pallas_call(functools.partial(forward_kernel, names), grid=(heads,), i...  75.8 us
    ppermute x78, starting transfers between devices, swap(): return lax.ppermute(value, axis, [(i, i ^ flip) for i in range(count)])  62.8 us
    all_gather x1, blocking collectives, on_device(): weights_out = lax.all_gather(low_out, 'dp', axis=1, tiled=True)  33.1 us
    unnamed x237, local copies, waits for them, and re-layouts  24.9 us
    dot_general x8, matrix products, rebuild(): return jnp.einsum('rsm,rsn->smn', frame, basis_new, precision=precise)  24.8 us
  transfers between devices with their start and end apart: 81, of which 26 were waited for; matrix products, arithmetic and copies ran while one was open for 29% of the time, Pallas kernels for 22%

profile of v1, /device:TPU:0, one launch (start us, length us, event | category | flops | bytes accessed | tf_op | source)
XLA Modules:
  0.0 810.4 jit_solution(12893198522931816413)
XLA Ops:
  13.1 3.0 collective-permute-start.11
  17.6 11.3 %collective-permute-done.11 = bf16[256,1024]{1,0:T(8,128)(2,1)S(1)} collective-permute-done((bf16[256,1024]{1,0:T(8,128)(2,1)S(1)}, bf16[256,1024]{1,0:T(8,128)(2,1)S(1)}, u32[]{:S(2)}, u32[]{:S(2)}) %collective-permute-start.11) | collective-permute-done | bytes 524320 | tf_op jit(solution)/shard_map/ppermute | solution.py:531
  31.1 33.1 %all_gather.13 = bf16[256,1024]{1,0:T(8,128)(2,1)S(1)} all-gather(bf16[256,128]{1,0:T(8,128)(2,1)S(1)} %convert_element_type.258), channel_id=1, replica_groups=mesh['dp'=8,'tensor'=4] {'dp'}, dimensions={1}, use_global_device_ids=true | all-gather | bytes 589824 | tf_op jit(solution)/shard_map/all_gather | solution.py:645
  64.2 3.8 fusion.48
  69.3 3.8 fusion.47
  74.4 6.6 convolution_bitcast_fusion.proj_ref
  81.0 37.8 %mixer_forward.3 = bf16[256,1024]{1,0:T(8,128)(2,1)} custom-call(f32[4,256,1024]{2,1,0:T(8,128)} %convolution_bitcast_fusion.proj_ref, f32[2,1,1024]{2,1,0:T(1,128)} %broadcast_in_dim.13.prea_ref, f32[3,256,4]{2,1,0:T(8,128)} %bitcast.283, f32[1,1024]{1,0:T(1,128)} %get-tuple-element.189.live_ref, s32[3]{0:T(128)} %get-tuple-element.196.lens_ref, ...), custom_call_target="tpu_custom_call" | custom-call | tf_op jit(solution)/shard_map/mixer_forward/pallas_call | solution.py:457
  124.8 4.4 convolution_bitcast_fusion.1.proj_ref
  129.2 38.0 %mixer_forward.2 = bf16[256,1024]{1,0:T(8,128)(2,1)} custom-call(f32[4,256,1024]{2,1,0:T(8,128)} %convolution_bitcast_fusion.1.proj_ref, f32[2,1,1024]{2,1,0:T(1,128)} %broadcast_in_dim.12.prea_ref, f32[3,256,4]{2,1,0:T(8,128)} %bitcast.284, f32[1,1024]{1,0:T(1,128)} %get-tuple-element.188.live_ref, s32[3]{0:T(128)} %get-tuple-element.195.lens_ref, ...), custom_call_target="tpu_custom_call" | custom-call | tf_op jit(solution)/shard_map/mixer_forward/pallas_call | solution.py:457
  170.7 2.6 fusion.106
  177.0 11.0 %collective-permute-done.14 = bf16[256,1024]{1,0:T(8,128)(2,1)S(1)} collective-permute-done((bf16[256,1024]{1,0:T(8,128)(2,1)S(1)}, bf16[256,1024]{1,0:T(8,128)(2,1)S(1)}, u32[]{:S(2)}, u32[]{:S(2)}) %collective-permute-start.14) | collective-permute-done | bytes 524320 | tf_op jit(solution)/shard_map/ppermute | solution.py:531
  188.8 10.0 %collective-permute-done.4 = bf16[256,1024]{1,0:T(8,128)(2,1)} collective-permute-done((bf16[256,1024]{1,0:T(8,128)(2,1)S(1)}, bf16[256,1024]{1,0:T(8,128)(2,1)}, u32[]{:S(2)}, u32[]{:S(2)}) %collective-permute-start.4) | collective-permute-done | bytes 524320 | tf_op jit(solution)/shard_map/ppermute | solution.py:531
  198.8 2.8 multiply_reduce_fusion.5
  205.0 12.9 %collective-permute-done.6 = bf16[256,1024]{1,0:T(8,128)(2,1)} collective-permute-done((bf16[256,1024]{1,0:T(8,128)(2,1)}, bf16[256,1024]{1,0:T(8,128)(2,1)}, u32[]{:S(2)}, u32[]{:S(2)}) %collective-permute-start.6) | collective-permute-done | bytes 524320 | tf_op jit(solution)/shard_map/ppermute | solution.py:531
  218.4 9.2 %collective-permute-done.21 = bf16[256,1024]{1,0:T(8,128)(2,1)} collective-permute-done((bf16[256,1024]{1,0:T(8,128)(2,1)S(1)}, bf16[256,1024]{1,0:T(8,128)(2,1)}, u32[]{:S(2)}, u32[]{:S(2)}) %collective-permute-start.21) | collective-permute-done | bytes 524320 | tf_op jit(solution)/shard_map/ppermute | solution.py:531
  227.7 5.4 fusion.121
  233.1 4.8 fusion.119
  238.0 6.4 multiply_convert_fusion.2
  257.4 10.5 %collective-permute-done.9 = bf16[256,1024]{1,0:T(8,128)(2,1)S(1)} collective-permute-done((bf16[256,1024]{1,0:T(8,128)(2,1)S(1)}, bf16[256,1024]{1,0:T(8,128)(2,1)S(1)}, u32[]{:S(2)}, u32[]{:S(2)}) %collective-permute-start.9) | collective-permute-done | bytes 524320 | tf_op jit(solution)/shard_map/ppermute | solution.py:531
  267.9 11.2 %collective-permute-done.24 = bf16[256,1024]{1,0:T(8,128)(2,1)S(1)} collective-permute-done((bf16[256,1024]{1,0:T(8,128)(2,1)S(1)}, bf16[256,1024]{1,0:T(8,128)(2,1)S(1)}, u32[]{:S(2)}, u32[]{:S(2)}) %collective-permute-start.24) | collective-permute-done | bytes 524320 | tf_op jit(solution)/shard_map/ppermute | solution.py:531
  282.1 8.2 %collective-permute-done.31 = bf16[256,1024]{1,0:T(8,128)(2,1)S(1)} collective-permute-done((bf16[256,1024]{1,0:T(8,128)(2,1)S(1)}, bf16[256,1024]{1,0:T(8,128)(2,1)S(1)}, u32[]{:S(2)}, u32[]{:S(2)}) %collective-permute-start.31) | collective-permute-done | bytes 524320 | tf_op jit(solution)/shard_map/ppermute | solution.py:531
  290.3 3.2 convolution_bitcast_fusion.5
  294.1 6.5 collective-permute-done.16
  300.7 3.2 convolution_bitcast_fusion.4
  305.6 3.3 fusion.118
  308.8 6.4 multiply_convert_fusion
  315.3 3.9 fusion.208
  327.7 3.1 bitcast_add_fusion.3
  335.7 3.7 convolution_bitcast_fusion.2
  339.4 3.6 fusion
  348.3 3.1 fusion.218
  353.0 6.5 collective-permute-done.34
  361.6 8.2 %collective-permute-done.19 = bf16[256,1024]{1,0:T(8,128)(2,1)S(1)} collective-permute-done((bf16[256,1024]{1,0:T(8,128)(2,1)S(1)}, bf16[256,1024]{1,0:T(8,128)(2,1)S(1)}, u32[]{:S(2)}, u32[]{:S(2)}) %collective-permute-start.19) | collective-permute-done | bytes 524320 | tf_op jit(solution)/shard_map/ppermute | solution.py:531
  369.9 3.6 fusion.192
  375.1 3.8 collective-permute-done.53
  383.8 5.4 copy.120
  392.9 2.6 collective-permute-done.51
  399.1 6.3 collective-permute-done.26
  405.5 5.4 fusion.62.dg_ref
  410.9 95.7 %mixer_backward.3 = (bf16[4,256,1024]{2,1,0:T(8,128)(2,1)}, f32[2,1,1024]{2,1,0:T(1,128)}, f32[3,256,4]{2,1,0:T(8,128)}, f32[2,1,128]{2,1,0:T(1,128)}) custom-call(f32[4,256,1024]{2,1,0:T(8,128)} %convolution_bitcast_fusion.proj_ref, f32[2,1,1024]{2,1,0:T(1,128)} %broadcast_in_dim.13.prea_ref, f32[3,256,4]{2,1,0:T(8,128)} %bitcast.285, ...), custom_call_target="tpu_custom_call" | custom-call | tf_op jit(solution)/shard_map/mixer_backward/pallas_call | solution.py:483
  506.6 5.4 fusion.59.dg_ref
  512.1 96.3 %mixer_backward.2 = (bf16[4,256,1024]{2,1,0:T(8,128)(2,1)}, f32[2,1,1024]{2,1,0:T(1,128)}, f32[3,256,4]{2,1,0:T(8,128)}, f32[2,1,128]{2,1,0:T(1,128)}) custom-call(f32[4,256,1024]{2,1,0:T(8,128)} %convolution_bitcast_fusion.1.proj_ref, f32[2,1,1024]{2,1,0:T(1,128)} %broadcast_in_dim.12.prea_ref, f32[3,256,4]{2,1,0:T(8,128)} %bitcast.286, ...), custom_call_target="tpu_custom_call" | custom-call | tf_op jit(solution)/shard_map/mixer_backward/pallas_call | solution.py:483
  623.5 2.8 fusion.210
  633.1 3.0 fusion.209
  636.2 3.5 fusion.21
  639.8 3.5 bitcast_add_fusion
  668.2 3.1 collective-permute-done.70
  674.6 2.9 orthonormal.3
  680.2 7.1 convolution_bitcast_fusion.7
  697.4 2.6 collective-permute-start.63
  711.7 4.0 bitcast_subtract_fusion
  722.1 6.9 subtract_bitcast_fusion
  732.2 4.6 collective-permute-done.42
  737.5 2.9 orthonormal.2
  740.4 5.9 convolution_bitcast_fusion.9
  750.3 3.9 collective-permute-done.44
  759.2 5.1 subtract_bitcast_fusion.1
  765.9 4.4 collective-permute-done.39
  770.4 6.9 collective-permute-done.29
  777.3 2.6 fusion.84
  780.7 5.5 copy.136
  786.9 3.1 collective-permute-done.65
  790.3 3.4 collective-permute-done.66
  795.2 2.9 fusion.83
  (518 shorter events, 187.6 us)
Async XLA Ops:
  7.3 67.1 %all-gather.4.cloned.1.call-start = ((), (), s32[]{:S(2)}) async-start(), calls=%async_computation | async-start | bytes 2359296 | tf_op jit(solution)/shard_map/all_gather | solution.py:644
  9.2 218.5 %all-gather.6.cloned.1.call-start = ((), (), s32[]{:S(2)}) async-start(), calls=%async_computation.1 | async-start | bytes 3244032 | tf_op jit(solution)/shard_map/all_gather | solution.py:646
  13.1 15.8 %collective-permute-start.11 = (bf16[256,1024]{1,0:T(8,128)(2,1)S(1)}, bf16[256,1024]{1,0:T(8,128)(2,1)S(1)}, u32[]{:S(2)}, u32[]{:S(2)}) collective-permute-start(bf16[256,1024]{1,0:T(8,128)(2,1)S(1)} %get-tuple-element.183), channel_id=1, source_target_pairs={{0,2},{1,3},{2,0},{3,1},{4,6},{5,7},{6,4},{7,5},{8,10},{9,11},{10,... | collective-permute-start | bytes 1572872 | tf_op jit(solution)/shard_map/ppermute | solution.py:531
  16.1 48.1 %collective-permute-start.10 = (bf16[256,1024]{1,0:T(8,128)(2,1)S(1)}, bf16[256,1024]{1,0:T(8,128)(2,1)S(1)}, u32[]{:S(2)}, u32[]{:S(2)}) collective-permute-start(bf16[256,1024]{1,0:T(8,128)(2,1)S(1)} %get-tuple-element.183), channel_id=1, source_target_pairs={{0,1},{1,0},{2,3},{3,2},{4,5},{5,4},{6,7},{7,6},{8,9},{9,8},{10,11... | collective-permute-start | bytes 1572872 | tf_op jit(solution)/shard_map/ppermute | solution.py:531
  16.1 48.1 %collective-permute-start.1 = (bf16[256,1024]{1,0:T(8,128)(2,1)S(1)}, bf16[256,1024]{1,0:T(8,128)(2,1)}, u32[]{:S(2)}, u32[]{:S(2)}) collective-permute-start(bf16[256,1024]{1,0:T(8,128)(2,1)S(1)} %get-tuple-element.182), channel_id=1, source_target_pairs={{0,2},{1,3},{2,0},{3,1},{4,6},{5,7},{6,4},{7,5},{8,10},{9,11},{10,... | collective-permute-start | bytes 1572872 | tf_op jit(solution)/shard_map/ppermute | solution.py:531
  16.2 53.0 %collective-permute-start = (bf16[256,1024]{1,0:T(8,128)(2,1)S(1)}, bf16[256,1024]{1,0:T(8,128)(2,1)}, u32[]{:S(2)}, u32[]{:S(2)}) collective-permute-start(bf16[256,1024]{1,0:T(8,128)(2,1)S(1)} %get-tuple-element.182), channel_id=1, source_target_pairs={{0,1},{1,0},{2,3},{3,2},{4,5},{5,4},{6,7},{7,6},{8,9},{9,8},{10,11... | collective-permute-start | bytes 1572872 | tf_op jit(solution)/shard_map/ppermute | solution.py:531
  17.4 220.5 %all-gather.8.cloned.1.call-start = ((), (), s32[]{:S(2)}) async-start(), calls=%async_computation.2 | async-start | bytes 1622016 | tf_op jit(solution)/shard_map/all_gather | solution.py:647
  28.8 35.3 %collective-permute-start.12 = (bf16[256,1024]{1,0:T(8,128)(2,1)S(1)}, bf16[256,1024]{1,0:T(8,128)(2,1)}, u32[]{:S(2)}, u32[]{:S(2)}) collective-permute-start(bf16[256,1024]{1,0:T(8,128)(2,1)S(1)} %collective-permute-done.11), channel_id=1, source_target_pairs={{0,1},{1,0},{2,3},{3,2},{4,5},{5,4},{6,7},{7,6},{8,9},{9,8},{10,11... | collective-permute-start | bytes 1572872 | tf_op jit(solution)/shard_map/ppermute | solution.py:531
  122.8 47.9 %collective-permute-start.13 = (bf16[512,1024]{1,0:T(8,128)(2,1)}, bf16[512,1024]{1,0:T(8,128)(2,1)}, u32[]{:S(2)}, u32[]{:S(2)}) collective-permute-start(bf16[512,1024]{1,0:T(8,128)(2,1)} %pad_maximum_fusion.11), channel_id=1, source_target_pairs={{0,1},{1,0},{2,3},{3,2},{4,5},{5,4},{6,7},{7,6},{8,9},{9,8},{10,11... | collective-permute-start | bytes 3145736 | tf_op jit(solution)/shard_map/ppermute | solution.py:531
  173.2 14.8 %collective-permute-start.14 = (bf16[256,1024]{1,0:T(8,128)(2,1)S(1)}, bf16[256,1024]{1,0:T(8,128)(2,1)S(1)}, u32[]{:S(2)}, u32[]{:S(2)}) collective-permute-start(bf16[256,1024]{1,0:T(8,128)(2,1)S(1)} %fusion.106), channel_id=1, source_target_pairs={{0,2},{1,3},{2,0},{3,1},{4,6},{5,7},{6,4},{7,5},{8,10},{9,11},{10,... | collective-permute-start | bytes 1572872 | tf_op jit(solution)/shard_map/ppermute | solution.py:531
  175.8 23.0 %collective-permute-start.4 = (bf16[256,1024]{1,0:T(8,128)(2,1)S(1)}, bf16[256,1024]{1,0:T(8,128)(2,1)}, u32[]{:S(2)}, u32[]{:S(2)}) collective-permute-start(bf16[256,1024]{1,0:T(8,128)(2,1)S(1)} %fusion.112), channel_id=1, source_target_pairs={{0,2},{1,3},{2,0},{3,1},{4,6},{5,7},{6,4},{7,5},{8,10},{9,11},{10,... | collective-permute-start | bytes 1572872 | tf_op jit(solution)/shard_map/ppermute | solution.py:531
  202.8 15.2 %collective-permute-start.6 = (bf16[256,1024]{1,0:T(8,128)(2,1)}, bf16[256,1024]{1,0:T(8,128)(2,1)}, u32[]{:S(2)}, u32[]{:S(2)}) collective-permute-start(bf16[256,1024]{1,0:T(8,128)(2,1)} %multiply_convert_fusion.7), channel_id=1, source_target_pairs={{0,2},{1,3},{2,0},{3,1},{4,6},{5,7},{6,4},{7,5},{8,10},{9,11},{10,... | collective-permute-start | bytes 1572872 | tf_op jit(solution)/shard_map/ppermute | solution.py:531
  204.4 23.2 %collective-permute-start.21 = (bf16[256,1024]{1,0:T(8,128)(2,1)S(1)}, bf16[256,1024]{1,0:T(8,128)(2,1)}, u32[]{:S(2)}, u32[]{:S(2)}) collective-permute-start(bf16[256,1024]{1,0:T(8,128)(2,1)S(1)} %get-tuple-element.168), channel_id=1, source_target_pairs={{0,2},{1,3},{2,0},{3,1},{4,6},{5,7},{6,4},{7,5},{8,10},{9,11},{10,... | collective-permute-start | bytes 1572872 | tf_op jit(solution)/shard_map/ppermute | solution.py:531
  205.0 22.7 %collective-permute-start.5 = (bf16[256,1024]{1,0:T(8,128)(2,1)}, bf16[256,1024]{1,0:T(8,128)(2,1)}, u32[]{:S(2)}, u32[]{:S(2)}) collective-permute-start(bf16[256,1024]{1,0:T(8,128)(2,1)} %multiply_convert_fusion.7), channel_id=1, source_target_pairs={{0,1},{1,0},{2,3},{3,2},{4,5},{5,4},{6,7},{7,6},{8,9},{9,8},{10,11... | collective-permute-start | bytes 1572872 | tf_op jit(solution)/shard_map/ppermute | solution.py:531
  217.9 9.8 %collective-permute-start.7 = (bf16[256,1024]{1,0:T(8,128)(2,1)}, bf16[256,1024]{1,0:T(8,128)(2,1)}, u32[]{:S(2)}, u32[]{:S(2)}) collective-permute-start(bf16[256,1024]{1,0:T(8,128)(2,1)} %collective-permute-done.6), channel_id=1, source_target_pairs={{0,1},{1,0},{2,3},{3,2},{4,5},{5,4},{6,7},{7,6},{8,9},{9,8},{10,11... | collective-permute-start | bytes 1572872 | tf_op jit(solution)/shard_map/ppermute | solution.py:531
  217.9 20.0 %collective-permute-start.20 = (bf16[256,1024]{1,0:T(8,128)(2,1)S(1)}, bf16[256,1024]{1,0:T(8,128)(2,1)}, u32[]{:S(2)}, u32[]{:S(2)}) collective-permute-start(bf16[256,1024]{1,0:T(8,128)(2,1)S(1)} %get-tuple-element.168), channel_id=1, source_target_pairs={{0,1},{1,0},{2,3},{3,2},{4,5},{5,4},{6,7},{7,6},{8,9},{9,8},{10,11... | collective-permute-start | bytes 1572872 | tf_op jit(solution)/shard_map/ppermute | solution.py:531
  227.7 10.3 %collective-permute-start.22 = (bf16[256,1024]{1,0:T(8,128)(2,1)}, bf16[256,1024]{1,0:T(8,128)(2,1)}, u32[]{:S(2)}, u32[]{:S(2)}) collective-permute-start(bf16[256,1024]{1,0:T(8,128)(2,1)} %collective-permute-done.21), channel_id=1, source_target_pairs={{0,1},{1,0},{2,3},{3,2},{4,5},{5,4},{6,7},{7,6},{8,9},{9,8},{10,11... | collective-permute-start | bytes 1572872 | tf_op jit(solution)/shard_map/ppermute | solution.py:531
  246.4 6.4 collective-permute-start.8
  253.0 14.8 %collective-permute-start.9 = (bf16[256,1024]{1,0:T(8,128)(2,1)S(1)}, bf16[256,1024]{1,0:T(8,128)(2,1)S(1)}, u32[]{:S(2)}, u32[]{:S(2)}) collective-permute-start(bf16[256,1024]{1,0:T(8,128)(2,1)S(1)} %fusion.108), channel_id=1, source_target_pairs={{0,2},{1,3},{2,0},{3,1},{4,6},{5,7},{6,4},{7,5},{8,10},{9,11},{10,... | collective-permute-start | bytes 1572872 | tf_op jit(solution)/shard_map/ppermute | solution.py:531
  255.3 23.8 %collective-permute-start.24 = (bf16[256,1024]{1,0:T(8,128)(2,1)S(1)}, bf16[256,1024]{1,0:T(8,128)(2,1)S(1)}, u32[]{:S(2)}, u32[]{:S(2)}) collective-permute-start(bf16[256,1024]{1,0:T(8,128)(2,1)S(1)} %fusion.100), channel_id=1, source_target_pairs={{0,2},{1,3},{2,0},{3,1},{4,6},{5,7},{6,4},{7,5},{8,10},{9,11},{10,... | collective-permute-start | bytes 1572872 | tf_op jit(solution)/shard_map/ppermute | solution.py:531
  256.9 33.4 %collective-permute-start.31 = (bf16[256,1024]{1,0:T(8,128)(2,1)S(1)}, bf16[256,1024]{1,0:T(8,128)(2,1)S(1)}, u32[]{:S(2)}, u32[]{:S(2)}) collective-permute-start(bf16[256,1024]{1,0:T(8,128)(2,1)S(1)} %get-tuple-element.169), channel_id=1, source_target_pairs={{0,2},{1,3},{2,0},{3,1},{4,6},{5,7},{6,4},{7,5},{8,10},{9,11},{10,... | collective-permute-start | bytes 1572872 | tf_op jit(solution)/shard_map/ppermute | solution.py:531
  280.6 20.1 %collective-permute-start.16 = (bf16[256,1024]{1,0:T(8,128)(2,1)S(1)}, bf16[256,1024]{1,0:T(8,128)(2,1)S(1)}, u32[]{:S(2)}, u32[]{:S(2)}) collective-permute-start(bf16[256,1024]{1,0:T(8,128)(2,1)S(1)} %get-tuple-element.194), channel_id=1, source_target_pairs={{0,2},{1,3},{2,0},{3,1},{4,6},{5,7},{6,4},{7,5},{8,10},{9,11},{10,... | collective-permute-start | bytes 1572872 | tf_op jit(solution)/shard_map/ppermute | solution.py:531
  282.1 26.7 %collective-permute-start.30 = (bf16[256,1024]{1,0:T(8,128)(2,1)S(1)}, bf16[256,1024]{1,0:T(8,128)(2,1)S(1)}, u32[]{:S(2)}, u32[]{:S(2)}) collective-permute-start(bf16[256,1024]{1,0:T(8,128)(2,1)S(1)} %get-tuple-element.169), channel_id=1, source_target_pairs={{0,1},{1,0},{2,3},{3,2},{4,5},{5,4},{6,7},{7,6},{8,9},{9,8},{10,11... | collective-permute-start | bytes 1572872 | tf_op jit(solution)/shard_map/ppermute | solution.py:531
  290.3 18.5 %collective-permute-start.32 = (bf16[256,1024]{1,0:T(8,128)(2,1)S(1)}, bf16[256,1024]{1,0:T(8,128)(2,1)S(1)}, u32[]{:S(2)}, u32[]{:S(2)}) collective-permute-start(bf16[256,1024]{1,0:T(8,128)(2,1)S(1)} %collective-permute-done.31), channel_id=1, source_target_pairs={{0,1},{1,0},{2,3},{3,2},{4,5},{5,4},{6,7},{7,6},{8,9},{9,8},{10,11... | collective-permute-start | bytes 1572872 | tf_op jit(solution)/shard_map/ppermute | solution.py:531
  293.5 10.3 %collective-permute-start.15 = (bf16[256,1024]{1,0:T(8,128)(2,1)S(1)}, bf16[256,1024]{1,0:T(8,128)(2,1)S(1)}, u32[]{:S(2)}, u32[]{:S(2)}) collective-permute-start(bf16[256,1024]{1,0:T(8,128)(2,1)S(1)} %get-tuple-element.194), channel_id=1, source_target_pairs={{0,1},{1,0},{2,3},{3,2},{4,5},{5,4},{6,7},{7,6},{8,9},{9,8},{10,11... | collective-permute-start | bytes 1572872 | tf_op jit(solution)/shard_map/ppermute | solution.py:531
  320.3 25.9 %collective-permute-start.18 = (bf16[512,1024]{1,0:T(8,128)(2,1)}, bf16[512,1024]{1,0:T(8,128)(2,1)}, u32[]{:S(2)}, u32[]{:S(2)}) collective-permute-start(bf16[512,1024]{1,0:T(8,128)(2,1)} %pad_maximum_fusion.12), channel_id=1, source_target_pairs={{0,1},{1,0},{2,3},{3,2},{4,5},{5,4},{6,7},{7,6},{8,9},{9,8},{10,11... | collective-permute-start | bytes 3145736 | tf_op jit(solution)/shard_map/ppermute | solution.py:531
  325.9 17.2 %collective-permute-start.33 = (bf16[512,1024]{1,0:T(8,128)(2,1)}, bf16[512,1024]{1,0:T(8,128)(2,1)}, u32[]{:S(2)}, u32[]{:S(2)}) collective-permute-start(bf16[512,1024]{1,0:T(8,128)(2,1)} %pad_maximum_fusion.16), channel_id=1, source_target_pairs={{0,1},{1,0},{2,3},{3,2},{4,5},{5,4},{6,7},{7,6},{8,9},{9,8},{10,11... | collective-permute-start | bytes 3145736 | tf_op jit(solution)/shard_map/ppermute | solution.py:531
  333.4 41.6 %collective-permute-start.52 = (f32[8,1,704]{2,1,0:T(1,128)S(1)}, f32[8,1,704]{2,1,0:T(1,128)S(1)}, u32[]{:S(2)}, u32[]{:S(2)}) collective-permute-start(f32[8,1,704]{2,1,0:T(1,128)S(1)} %transpose.86), channel_id=1, source_target_pairs={{0,4},{4,0},{8,12},{12,8},{16,20},{20,16},{24,28},{28,24},{1,5},{5... | collective-permute-start | bytes 67592 | tf_op jit(solution)/shard_map/ppermute | solution.py:531
  344.7 14.8 %collective-permute-start.34 = (bf16[256,1024]{1,0:T(8,128)(2,1)S(1)}, bf16[256,1024]{1,0:T(8,128)(2,1)S(1)}, u32[]{:S(2)}, u32[]{:S(2)}) collective-permute-start(bf16[256,1024]{1,0:T(8,128)(2,1)S(1)} %fusion.96), channel_id=1, source_target_pairs={{0,2},{1,3},{2,0},{3,1},{4,6},{5,7},{6,4},{7,5},{8,10},{9,11},{10,... | collective-permute-start | bytes 1572872 | tf_op jit(solution)/shard_map/ppermute | solution.py:531
  347.7 22.1 %collective-permute-start.19 = (bf16[256,1024]{1,0:T(8,128)(2,1)S(1)}, bf16[256,1024]{1,0:T(8,128)(2,1)S(1)}, u32[]{:S(2)}, u32[]{:S(2)}) collective-permute-start(bf16[256,1024]{1,0:T(8,128)(2,1)S(1)} %fusion.102), channel_id=1, source_target_pairs={{0,2},{1,3},{2,0},{3,1},{4,6},{5,7},{6,4},{7,5},{8,10},{9,11},{10,... | collective-permute-start | bytes 1572872 | tf_op jit(solution)/shard_map/ppermute | solution.py:531
  351.5 27.9 %collective-permute-start.49 = (f32[8,2,1024]{2,1,0:T(2,128)S(1)}, f32[8,2,1024]{2,1,0:T(2,128)S(1)}, u32[]{:S(2)}, u32[]{:S(2)}) collective-permute-start(f32[8,2,1024]{2,1,0:T(2,128)S(1)} %bitcast.299), channel_id=1, source_target_pairs={{0,4},{4,0},{8,12},{12,8},{16,20},{20,16},{24,28},{28,24},{1,5},{5... | collective-permute-start | bytes 196616 | tf_op jit(solution)/shard_map/ppermute | solution.py:531
  373.5 17.8 %collective-permute-start.36 = (bf16[256,1024]{1,0:T(8,128)(2,1)}, bf16[256,1024]{1,0:T(8,128)(2,1)}, u32[]{:S(2)}, u32[]{:S(2)}) collective-permute-start(bf16[256,1024]{1,0:T(8,128)(2,1)} %get-tuple-element.160), channel_id=1, source_target_pairs={{0,2},{1,3},{2,0},{3,1},{4,6},{5,7},{6,4},{7,5},{8,10},{9,11},{10,... | collective-permute-start | bytes 1572872 | tf_op jit(solution)/shard_map/ppermute | solution.py:531
  379.0 12.6 %collective-permute-start.54 = (f32[8,1,704]{2,1,0:T(1,128)S(1)}, f32[8,1,704]{2,1,0:T(1,128)}, u32[]{:S(2)}, u32[]{:S(2)}) collective-permute-start(f32[8,1,704]{2,1,0:T(1,128)S(1)} %add.472), channel_id=1, source_target_pairs={{0,16},{4,20},{8,24},{12,28},{16,0},{20,4},{24,8},{28,12},{1,17},{... | collective-permute-start | bytes 67592 | tf_op jit(solution)/shard_map/ppermute | solution.py:531
  379.5 9.8 %collective-permute-start.50 = (f32[8,2,1024]{2,1,0:T(2,128)S(1)}, f32[8,2,1024]{2,1,0:T(2,128)}, u32[]{:S(2)}, u32[]{:S(2)}) collective-permute-start(f32[8,2,1024]{2,1,0:T(2,128)S(1)} %fusion.188), channel_id=1, source_target_pairs={{0,8},{4,12},{8,0},{12,4},{16,24},{20,28},{24,16},{28,20},{1,9},{5... | collective-permute-start | bytes 196616 | tf_op jit(solution)/shard_map/ppermute | solution.py:531
  390.2 5.4 collective-permute-start.51
  390.8 14.7 %collective-permute-start.35 = (bf16[256,1024]{1,0:T(8,128)(2,1)}, bf16[256,1024]{1,0:T(8,128)(2,1)}, u32[]{:S(2)}, u32[]{:S(2)}) collective-permute-start(bf16[256,1024]{1,0:T(8,128)(2,1)} %get-tuple-element.160), channel_id=1, source_target_pairs={{0,1},{1,0},{2,3},{3,2},{4,5},{5,4},{6,7},{7,6},{8,9},{9,8},{10,11... | collective-permute-start | bytes 1572872 | tf_op jit(solution)/shard_map/ppermute | solution.py:531
  390.8 14.7 %collective-permute-start.26 = (bf16[256,1024]{1,0:T(8,128)(2,1)}, bf16[256,1024]{1,0:T(8,128)(2,1)}, u32[]{:S(2)}, u32[]{:S(2)}) collective-permute-start(bf16[256,1024]{1,0:T(8,128)(2,1)} %get-tuple-element.148), channel_id=1, source_target_pairs={{0,2},{1,3},{2,0},{3,1},{4,6},{5,7},{6,4},{7,5},{8,10},{9,11},{10,... | collective-permute-start | bytes 1572872 | tf_op jit(solution)/shard_map/ppermute | solution.py:531
  391.3 14.1 %collective-permute-start.37 = (bf16[256,1024]{1,0:T(8,128)(2,1)}, bf16[256,1024]{1,0:T(8,128)(2,1)}, u32[]{:S(2)}, u32[]{:S(2)}) collective-permute-start(bf16[256,1024]{1,0:T(8,128)(2,1)} %collective-permute-done.36), channel_id=1, source_target_pairs={{0,1},{1,0},{2,3},{3,2},{4,5},{5,4},{6,7},{7,6},{8,9},{9,8},{10,11... | collective-permute-start | bytes 1572872 | tf_op jit(solution)/shard_map/ppermute | solution.py:531
  396.2 110.4 %collective-permute-start.25 = (bf16[256,1024]{1,0:T(8,128)(2,1)}, bf16[256,1024]{1,0:T(8,128)(2,1)}, u32[]{:S(2)}, u32[]{:S(2)}) collective-permute-start(bf16[256,1024]{1,0:T(8,128)(2,1)} %get-tuple-element.148), channel_id=1, source_target_pairs={{0,1},{1,0},{2,3},{3,2},{4,5},{5,4},{6,7},{7,6},{8,9},{9,8},{10,11... | collective-permute-start | bytes 1572872 | tf_op jit(solution)/shard_map/ppermute | solution.py:531
  405.5 101.2 %collective-permute-start.27 = (bf16[256,1024]{1,0:T(8,128)(2,1)}, bf16[256,1024]{1,0:T(8,128)(2,1)}, u32[]{:S(2)}, u32[]{:S(2)}) collective-permute-start(bf16[256,1024]{1,0:T(8,128)(2,1)} %collective-permute-done.26), channel_id=1, source_target_pairs={{0,1},{1,0},{2,3},{3,2},{4,5},{5,4},{6,7},{7,6},{8,9},{9,8},{10,11... | collective-permute-start | bytes 1572872 | tf_op jit(solution)/shard_map/ppermute | solution.py:531
  609.1 43.7 %collective-permute-start.75 = (f32[2,1,128]{2,1,0:T(1,128)S(1)}, f32[2,1,128]{2,1,0:T(1,128)S(1)}, u32[]{:S(2)}, u32[]{:S(2)}) collective-permute-start(f32[2,1,128]{2,1,0:T(1,128)S(1)} %add.506), channel_id=1, source_target_pairs={{0,4},{4,0},{8,12},{12,8},{16,20},{20,16},{24,28},{28,24},{1,5},{5... | collective-permute-start | bytes 3080 | tf_op jit(solution)/shard_map/ppermute | solution.py:531
  616.4 44.7 %collective-permute-start.72 = (f32[1024,2]{0,1:T(2,128)S(1)}, f32[1024,2]{0,1:T(2,128)S(1)}, u32[]{:S(2)}, u32[]{:S(2)}) collective-permute-start(f32[1024,2]{0,1:T(2,128)S(1)} %convolution_add_fusion.7), channel_id=1, source_target_pairs={{0,4},{4,0},{8,12},{12,8},{16,20},{20,16},{24,28},{28,24},{1,5},{5... | collective-permute-start | bytes 24584 | tf_op jit(solution)/shard_map/ppermute | solution.py:531
  617.0 45.9 %collective-permute-start.69 = (f32[3,256,4]{2,1,0:T(8,128)S(1)}, f32[3,256,4]{2,1,0:T(8,128)S(1)}, u32[]{:S(2)}, u32[]{:S(2)}) collective-permute-start(f32[3,256,4]{2,1,0:T(8,128)S(1)} %add.496), channel_id=1, source_target_pairs={{0,4},{4,0},{8,12},{12,8},{16,20},{20,16},{24,28},{28,24},{1,5},{5... | collective-permute-start | bytes 36872 | tf_op jit(solution)/shard_map/ppermute | solution.py:531
  627.3 126.8 %collective-permute-start.38 = (bf16[512,1024]{1,0:T(8,128)(2,1)}, bf16[512,1024]{1,0:T(8,128)(2,1)}, u32[]{:S(2)}, u32[]{:S(2)}) collective-permute-start(bf16[512,1024]{1,0:T(8,128)(2,1)} %pad_maximum_fusion.17), channel_id=1, source_target_pairs={{0,1},{1,0},{2,3},{3,2},{4,5},{5,4},{6,7},{7,6},{8,9},{9,8},{10,11... | collective-permute-start | bytes 3145736 | tf_op jit(solution)/shard_map/ppermute | solution.py:531
  652.1 6.6 collective-permute-start.46
  661.0 5.8 collective-permute-start.73
  663.0 8.4 %collective-permute-start.70 = (f32[3,256,4]{2,1,0:T(8,128)S(1)}, f32[3,256,4]{2,1,0:T(8,128)}, u32[]{:S(2)}, u32[]{:S(2)}) collective-permute-start(f32[3,256,4]{2,1,0:T(8,128)S(1)} %add.497), channel_id=1, source_target_pairs={{0,8},{4,12},{8,0},{12,4},{16,24},{20,28},{24,16},{28,20},{1,9},{5... | collective-permute-start | bytes 36872 | tf_op jit(solution)/shard_map/ppermute | solution.py:531
  663.3 10.7 %collective-permute-start.48 = (f32[8,1,256]{2,1,0:T(1,128)S(1)}, f32[8,1,256]{2,1,0:T(1,128)S(1)}, u32[]{:S(2)}, u32[]{:S(2)}) collective-permute-start(f32[8,1,256]{2,1,0:T(1,128)S(1)} %add.462), channel_id=1, source_target_pairs={{0,16},{4,20},{8,24},{12,28},{16,0},{20,4},{24,8},{28,12},{1,17},{... | collective-permute-start | bytes 24584 | tf_op jit(solution)/shard_map/ppermute | solution.py:531
  667.4 22.1 %collective-permute-start.74 = (f32[1024,2]{0,1:T(2,128)}, f32[1024,2]{0,1:T(2,128)}, u32[]{:S(2)}, u32[]{:S(2)}) collective-permute-start(f32[1024,2]{0,1:T(2,128)} %add.503), channel_id=1, source_target_pairs={{0,16},{4,20},{8,24},{12,28},{16,0},{20,4},{24,8},{28,12},{1,17},{... | collective-permute-start | bytes 24584 | tf_op jit(solution)/shard_map/ppermute | solution.py:531
  672.5 24.9 %collective-permute-start.71 = (f32[3,256,4]{2,1,0:T(8,128)S(1)}, f32[3,256,4]{2,1,0:T(8,128)}, u32[]{:S(2)}, u32[]{:S(2)}) collective-permute-start(f32[3,256,4]{2,1,0:T(8,128)S(1)} %add.498), channel_id=1, source_target_pairs={{0,16},{4,20},{8,24},{12,28},{16,0},{20,4},{24,8},{28,12},{1,17},{... | collective-permute-start | bytes 36872 | tf_op jit(solution)/shard_map/ppermute | solution.py:531
  679.7 11.6 %collective-permute-start.61 = (f32[8,1,1024]{2,0,1:T(8,128)S(1)}, f32[8,1,1024]{2,0,1:T(8,128)S(1)}, u32[]{:S(2)}, u32[]{:S(2)}) collective-permute-start(f32[8,1,1024]{2,0,1:T(8,128)S(1)} %fusion.70), channel_id=1, source_target_pairs={{0,4},{4,0},{8,12},{12,8},{16,20},{20,16},{24,28},{28,24},{1,5},{5... | collective-permute-start | bytes 98312 | tf_op jit(solution)/shard_map/ppermute | solution.py:531
  687.3 6.8 collective-permute-start.58
  693.5 62.6 %collective-permute-start.28 = (bf16[512,1024]{1,0:T(8,128)(2,1)}, bf16[512,1024]{1,0:T(8,128)(2,1)}, u32[]{:S(2)}, u32[]{:S(2)}) collective-permute-start(bf16[512,1024]{1,0:T(8,128)(2,1)} %pad_maximum_fusion.15), channel_id=1, source_target_pairs={{0,1},{1,0},{2,3},{3,2},{4,5},{5,4},{6,7},{7,6},{8,9},{9,8},{10,11... | collective-permute-start | bytes 3145736 | tf_op jit(solution)/shard_map/ppermute | solution.py:531
  694.1 11.4 %collective-permute-start.56 = (f32[8,1,1024]{2,0,1:T(8,128)}, f32[8,1,1024]{2,0,1:T(8,128)}, u32[]{:S(2)}, u32[]{:S(2)}) collective-permute-start(f32[8,1,1024]{2,0,1:T(8,128)} %add.474), channel_id=1, source_target_pairs={{0,8},{4,12},{8,0},{12,4},{16,24},{20,28},{24,16},{28,20},{1,9},{5... | collective-permute-start | bytes 98312 | tf_op jit(solution)/shard_map/ppermute | solution.py:531
  696.0 10.8 %collective-permute-start.59 = (f32[8,2,704]{2,0,1:T(8,128)}, f32[8,2,704]{2,0,1:T(8,128)}, u32[]{:S(2)}, u32[]{:S(2)}) collective-permute-start(f32[8,2,704]{2,0,1:T(8,128)} %add.478), channel_id=1, source_target_pairs={{0,8},{4,12},{8,0},{12,4},{16,24},{20,28},{24,16},{28,20},{1,9},{5... | collective-permute-start | bytes 135176 | tf_op jit(solution)/shard_map/ppermute | solution.py:531
  697.4 11.5 %collective-permute-start.63 = (f32[8,1,1024]{2,0,1:T(8,128)}, f32[8,1,1024]{2,0,1:T(8,128)}, u32[]{:S(2)}, u32[]{:S(2)}) collective-permute-start(f32[8,1,1024]{2,0,1:T(8,128)} %add.483), channel_id=1, source_target_pairs={{0,16},{4,20},{8,24},{12,28},{16,0},{20,4},{24,8},{28,12},{1,17},{... | collective-permute-start | bytes 98312 | tf_op jit(solution)/shard_map/ppermute | solution.py:531
  705.5 15.0 %collective-permute-start.40 = (f32[8,4,1024]{2,1,0:T(4,128)}, f32[8,4,1024]{2,1,0:T(4,128)S(1)}, u32[]{:S(2)}, u32[]{:S(2)}) collective-permute-start(f32[8,4,1024]{2,1,0:T(4,128)} %bitcast.291), channel_id=1, source_target_pairs={{0,4},{4,0},{8,12},{12,8},{16,20},{20,16},{24,28},{28,24},{1,5},{5... | collective-permute-start | bytes 393224 | tf_op jit(solution)/shard_map/ppermute | solution.py:531
  706.7 10.6 %collective-permute-start.57 = (f32[8,1,1024]{2,0,1:T(8,128)S(1)}, f32[8,1,1024]{2,0,1:T(8,128)S(1)}, u32[]{:S(2)}, u32[]{:S(2)}) collective-permute-start(f32[8,1,1024]{2,0,1:T(8,128)S(1)} %add.475), channel_id=1, source_target_pairs={{0,16},{4,20},{8,24},{12,28},{16,0},{20,4},{24,8},{28,12},{1,17},{... | collective-permute-start | bytes 98312 | tf_op jit(solution)/shard_map/ppermute | solution.py:531
  708.9 13.2 %collective-permute-start.60 = (f32[8,2,704]{2,0,1:T(8,128)S(1)}, f32[8,2,704]{2,0,1:T(8,128)S(1)}, u32[]{:S(2)}, u32[]{:S(2)}) collective-permute-start(f32[8,2,704]{2,0,1:T(8,128)S(1)} %add.479), channel_id=1, source_target_pairs={{0,16},{4,20},{8,24},{12,28},{16,0},{20,4},{24,8},{28,12},{1,17},{... | collective-permute-start | bytes 135176 | tf_op jit(solution)/shard_map/ppermute | solution.py:531
  720.6 8.4 %collective-permute-start.41 = (f32[8,4,1024]{2,1,0:T(4,128)S(1)}, f32[8,4,1024]{2,1,0:T(4,128)S(1)}, u32[]{:S(2)}, u32[]{:S(2)}) collective-permute-start(f32[8,4,1024]{2,1,0:T(4,128)S(1)} %fusion.189), channel_id=1, source_target_pairs={{0,8},{4,12},{8,0},{12,4},{16,24},{20,28},{24,16},{28,20},{1,9},{5... | collective-permute-start | bytes 393224 | tf_op jit(solution)/shard_map/ppermute | solution.py:531
  729.1 7.7 collective-permute-start.42
  755.4 14.9 %collective-permute-start.39 = (bf16[256,1024]{1,0:T(8,128)(2,1)S(1)}, bf16[256,1024]{1,0:T(8,128)(2,1)S(1)}, u32[]{:S(2)}, u32[]{:S(2)}) collective-permute-start(bf16[256,1024]{1,0:T(8,128)(2,1)S(1)} %fusion.94), channel_id=1, source_target_pairs={{0,2},{1,3},{2,0},{3,1},{4,6},{5,7},{6,4},{7,5},{8,10},{9,11},{10,... | collective-permute-start | bytes 1572872 | tf_op jit(solution)/shard_map/ppermute | solution.py:531
  757.7 19.6 %collective-permute-start.29 = (bf16[256,1024]{1,0:T(8,128)(2,1)S(1)}, bf16[256,1024]{1,0:T(8,128)(2,1)S(1)}, u32[]{:S(2)}, u32[]{:S(2)}) collective-permute-start(bf16[256,1024]{1,0:T(8,128)(2,1)S(1)} %fusion.98), channel_id=1, source_target_pairs={{0,2},{1,3},{2,0},{3,1},{4,6},{5,7},{6,4},{7,5},{8,10},{9,11},{10,... | collective-permute-start | bytes 1572872 | tf_op jit(solution)/shard_map/ppermute | solution.py:531
  780.0 6.2 collective-permute-start.64
  (131 other events, 2753.6 us)
Sparse Core Ops, SparseCore 0:
  10.9 58.4 all-gather.3
  72.0 60.3 all-gather.5
  177.1 42.3 all-gather.7

commit v2 on v0

v2 whole, which is shorter than its diff:
```python
import functools
from types import SimpleNamespace

import jax
import jax.numpy as jnp
from jax import lax
from jax.experimental import pallas as pl
from jax.experimental.pallas import tpu as pltpu
from jax.sharding import PartitionSpec as P

CG_STEPS = 8
BLK = 128
tiny_eps = 1e-06
solve_floor = 0.01
ridge_shift = 9.0
precise = lax.Precision.HIGHEST
F32 = jnp.float32
BF = jnp.bfloat16


def softplus(x):
    return jnp.maximum(x, 0.0) + jnp.log1p(jnp.exp(-jnp.abs(x)))


def spot_of(i):
    return pl.ds(i * BLK, BLK)


def sigmoid(x):
    return 0.5 * jnp.tanh(0.5 * x) + 0.5


def mm(a, b):
    return jnp.dot(a, b, preferred_element_type=F32)


def nt(a, b):
    return lax.dot_general(a, b, (((1,), (1,)), ((), ())), preferred_element_type=F32)


def high_low(x, axis=0):
    high = x.astype(BF).astype(F32)
    return jnp.concatenate([high, x - high], axis=axis).astype(BF)


def halves(x):
    count = x.shape[0] // 2
    return x[:count] + x[count:]


def col_sum(x):
    return jnp.sum(x, axis=0, keepdims=True)


def start_of(lens_ref, places):
    begin = jnp.zeros_like(places)
    edge = jnp.int32(0)
    for item in range(lens_ref.shape[0] - 1):
        edge = edge + lens_ref[item]
        begin = jnp.where(places >= edge, edge, begin)
    return begin


def conv_masks(lens_ref, total, taps):
    places = lax.broadcasted_iota(jnp.int32, (1, total), 1)
    begin = start_of(lens_ref, places)
    return [(places - i >= begin).astype(F32) for i in range(taps)]


def conv_rows(rows, taps_now, sc):
    acc = rows * taps_now[:, 0:1]
    for i in range(1, taps_now.shape[1]):
        acc = acc + (pltpu.roll(rows, i, 1) * sc.mask[i]) * taps_now[:, i : i + 1]
    return acc


CHUNK = 16
TOGETHER = 8


def by_chunks(width, fn, init):
    def body(c, carry):
        for k in range(TOGETHER):
            carry = fn(pl.ds(pl.multiple_of((c * TOGETHER + k) * CHUNK, CHUNK), CHUNK), carry)
        return carry

    return lax.fori_loop(0, width // (CHUNK * TOGETHER), body, init)


def set_up(head, proj_ref, prea_ref, taps_ref, live_ref, lens_ref, bias_ref, sc, keep_all):
    width, total = proj_ref.shape[1], proj_ref.shape[2]
    blocks = total // BLK
    taps = taps_ref.shape[2]
    for i, mask in enumerate(conv_masks(lens_ref, total, taps)):
        sc.mask[i] = jnp.broadcast_to(mask, (CHUNK, total))
    live = live_ref[...]

    def squares(j, dst):
        def body(at, acc):
            u = conv_rows(proj_ref[j, at, :], taps_ref[j, at, :], sc)
            sig = sigmoid(u)
            x = u * sig
            dst[at, :] = x
            if keep_all:
                sc.slope[j, at, :] = sig + x * (1.0 - sig)
            return acc + x * x

        acc = by_chunks(width, body, jnp.zeros((CHUNK, total), F32))
        return lax.rsqrt(col_sum(acc) + tiny_eps)

    keys, values = (sc.xk, sc.xv) if keep_all else (sc.x, sc.x)

    scale_q = squares(0, sc.q)
    scale_k = squares(1, keys)
    sc.scale[0:1, :] = scale_q
    sc.scale[1:2, :] = scale_k
    scale_k = scale_k * live
    for n in range(blocks):
        at = pl.ds(n * BLK, BLK)
        sc.q[:, at] = sc.q[:, at] * scale_q[:, n * BLK : (n + 1) * BLK]
        kt = keys[:, at] * scale_k[:, n * BLK : (n + 1) * BLK]
        sc.kt[:, at] = kt.astype(BF)
        sc.ks[n, 0:BLK, :] = kt.T.astype(BF)
    squares(2, values)
    for n in range(blocks):
        at = pl.ds(n * BLK, BLK)
        vt = values[:, at] * live[:, n * BLK : (n + 1) * BLK]
        sc.vt[:, at] = vt.astype(BF)
        if keep_all:
            sc.vg[n, 0:BLK, :] = vt.T.astype(BF)
    base = prea_ref[0, :, :] + jnp.full((1, total), bias_ref[0, head], F32)
    base = jnp.concatenate([base[:, n * BLK : (n + 1) * BLK] for n in range(blocks)], axis=0)
    forget = -softplus(base)
    row_i = lax.broadcasted_iota(jnp.int32, (BLK, BLK), 0)
    col_i = lax.broadcasted_iota(jnp.int32, (BLK, BLK), 1)
    cum = jnp.dot(forget, (row_i <= col_i).astype(F32), precision=precise, preferred_element_type=F32)
    first = lax.broadcasted_iota(jnp.int32, (blocks, BLK), 0) * BLK
    places = first + lax.broadcasted_iota(jnp.int32, (blocks, BLK), 1)
    begin = start_of(lens_ref, places)
    begin_last = start_of(lens_ref, first + (BLK - 1))
    end = jnp.broadcast_to(cum[:, BLK - 1 : BLK], cum.shape)
    from_start = jnp.where(begin < first, jnp.exp(cum), 0.0)
    to_end = jnp.where(places >= begin_last, jnp.exp(end - cum), 0.0)
    keep = jnp.where(begin_last < first, jnp.exp(end), 0.0)
    sc.dec[0] = from_start
    sc.dec[1] = to_end
    sc.dec[2] = keep
    cum_col = jnp.transpose(cum)
    for n in range(blocks):
        spread = cum[n : n + 1, :] - cum_col[:, n : n + 1]
        allowed = (row_i <= col_i) & (row_i + n * BLK >= begin[n : n + 1, :])
        sc.dt[n] = jnp.where(allowed, jnp.exp(jnp.where(allowed, spread, 0.0)), 0.0)
    state = jnp.zeros((2 * width, width), F32)
    for n in range(blocks):
        sc.ks[n, BLK:, :] = state[:width].astype(BF)
        sc.g[n] = state[width:].astype(BF)
        if keep_all:
            sc.vg[n, BLK:, :] = state[width:].T.astype(BF)
        if n + 1 < blocks:
            at = pl.ds(n * BLK, BLK)
            to_row = to_end[n : n + 1, :]
            scaled = jnp.concatenate(
                [sc.kt[:, at].astype(F32) * to_row, sc.vt[:, at].astype(F32) * to_row], axis=0
            ).astype(BF)
            state = keep[n : n + 1, :] * state + mm(scaled, sc.ks[n, 0:BLK, :])
    return softplus(jnp.full((1, BLK), bias_ref[1, head], F32) + ridge_shift)


def solve(lam, sc, keep_all):
    blocks = sc.dt.shape[0]
    spans = [pl.ds(n * BLK, BLK) for n in range(blocks)]
    row = sc.row
    for n, at in enumerate(spans):
        q = sc.q[:, at]
        row[0, n : n + 1, :] = col_sum(q * q)
        sc.z[:, at] = jnp.zeros_like(q)
        sc.p[:, at] = q
        sc.r[:, at] = q
        sc.pl[:, at] = q.astype(BF)

    def step(i, last):
        spot = spot_of(i)
        for n, at in enumerate(spans):
            both = mm(sc.ks[n], sc.pl[:, at])
            scores = (sc.dt[n] * both[:BLK]).astype(BF)
            sc.sl[n] = scores
            sc.w[:, at] = sc.dec[0, n : n + 1, :] * both[BLK:]
            if keep_all:
                far = spot_of(CG_STEPS + i)
                sc.rh[n, :, spot] = scores
                sc.lh[n, :, far] = sc.pl[:, at]
        for n, at in enumerate(spans):
            p = sc.p[:, at]
            w = mm(sc.kt[:, at], sc.sl[n]) + sc.w[:, at] + lam * p
            rho = row[0, n : n + 1, :]
            inv_c = 1.0 / (col_sum(p * w) + solve_floor)
            s = rho * inv_c
            sc.z[:, at] = sc.z[:, at] + s * p
            if keep_all:
                sc.ph[i, :, at] = p
                sc.wh[i, :, at] = w
                sc.fh[n, :, spot] = (sc.dec[0, n : n + 1, :] * p).astype(BF)
                sc.sh[i, 0, n : n + 1, :] = s
                sc.sh[i, 1, n : n + 1, :] = inv_c
            if not last:
                r = sc.r[:, at] - s * w
                sc.r[:, at] = r
                rho_next = col_sum(r * r)
                inv_rho = 1.0 / (rho + solve_floor)
                beta = rho_next * inv_rho
                row[0, n : n + 1, :] = rho_next
                if keep_all:
                    sc.nh[i, :, at] = r
                    sc.sh[i, 2, n : n + 1, :] = inv_rho
                    sc.sh[i, 3, n : n + 1, :] = beta
                p = r + beta * p
                sc.p[:, at] = p
                sc.pl[:, at] = p.astype(BF)

    for i in range(CG_STEPS):
        step(i, i == CG_STEPS - 1)


def forward_kernel(names, head, proj_ref, prea_ref, taps_ref, live_ref, lens_ref, bias_ref, out_ref, *scratch):
    sc = SimpleNamespace(**dict(zip(names, scratch)))
    lam = set_up(head, proj_ref, prea_ref, taps_ref, live_ref, lens_ref, bias_ref, sc, False)
    solve(lam, sc, False)
    spans = [pl.ds(n * BLK, BLK) for n in range(sc.dt.shape[0])]
    for n, at in enumerate(spans):
        z = sc.z[:, at].astype(BF)
        sc.sl[n] = (sc.dt[n] * mm(sc.ks[n, 0:BLK, :], z)).astype(BF)
        sc.w[:, at] = sc.dec[0, n : n + 1, :] * mm(sc.g[n], z)
    for n, at in enumerate(spans):
        o = mm(sc.vt[:, at], sc.sl[n]) + sc.w[:, at]
        out_ref[:, at] = (o * sigmoid(proj_ref[3, :, at])).astype(BF)


def backward_kernel(
    names, head, proj_ref, prea_ref, taps_ref, live_ref, dg_ref, basis_ref, packed_ref, left_ref, lens_ref, bias_ref,
    dproj_ref, da_ref, dtaps_ref, dhead_ref, sketch_ref, *scratch
):
    sc = SimpleNamespace(**dict(zip(names, scratch)))
    width, total = proj_ref.shape[1], proj_ref.shape[2]
    blocks = total // BLK
    lam = set_up(head, proj_ref, prea_ref, taps_ref, live_ref, lens_ref, bias_ref, sc, True)
    solve(lam, sc, True)
    row_i = lax.broadcasted_iota(jnp.int32, (BLK, BLK), 0)
    col_i = lax.broadcasted_iota(jnp.int32, (BLK, BLK), 1)
    dkt, dvt, zb, rb_s, pb_s = sc.dkt, sc.dvt, sc.zb, sc.rb, sc.pb

    spans = [pl.ds(n * BLK, BLK) for n in range(blocks)]
    row = sc.row
    last = CG_STEPS - 1

    for n, at in enumerate(spans):
        z_low = sc.z[:, at].astype(BF)
        sc.pl[:, at] = z_low
        sc.sl[n] = (sc.dt[n] * mm(sc.ks[n, 0:BLK, :], z_low)).astype(BF)
        sc.w[:, at] = sc.dec[0, n : n + 1, :] * mm(sc.g[n], z_low)
    for n, at in enumerate(spans):
        o = mm(sc.vt[:, at], sc.sl[n]) + sc.w[:, at]
        sig = sigmoid(proj_ref[3, :, at])
        dg = dg_ref[:, at]
        dproj_ref[3, :, at] = (dg * o * sig * (1.0 - sig)).astype(BF)
        sc.do[:, at] = (dg * sig).astype(BF)
    for n, at in enumerate(spans):
        from_row = sc.dec[0, n : n + 1, :]
        z = sc.z[:, at]
        both = mm(sc.vg[n], sc.do[:, at])
        state_part = from_row * both[BLK:]
        zb[:, at] = state_part
        sc.sl2[n] = (sc.dt[n] * both[:BLK]).astype(BF)
        sc.xm[n] = sc.sl[n].astype(F32) * both[:BLK]
        sc.fm[0, n : n + 1, :] = col_sum(z * state_part)
        sc.p[:, at] = from_row * z
    for n, at in enumerate(spans):
        do = sc.do[:, at]
        zb[:, at] = zb[:, at] + mm(sc.kt[:, at], sc.sl2[n])
        dvt[:, at] = nt(do, sc.sl[n])
        sc.dg0[n] = nt(do, sc.p[:, at].astype(BF))
        dkt[:, at] = nt(sc.pl[:, at], sc.sl2[n])
    for at in spans:
        zero = jnp.zeros((width, BLK), F32)
        rb_s[:, at] = zero
        pb_s[:, at] = zero
        sc.nh[last, :, at] = zero
    sc.sh[last, 2] = jnp.zeros((blocks, BLK), F32)
    sc.sh[last, 3] = jnp.zeros((blocks, BLK), F32)
    row[0] = jnp.zeros((blocks, BLK), F32)
    sc.fm[1] = jnp.zeros((blocks, BLK), F32)

    def reverse_step(i):
        spot = spot_of(i)
        far = spot_of(CG_STEPS + i)
        s_all, inv_c, inv_rho, beta = sc.sh[i, 0], sc.sh[i, 1], sc.sh[i, 2], sc.sh[i, 3]
        for n, at in enumerate(spans):
            row[1, n : n + 1, :] = col_sum(pb_s[:, at] * sc.ph[i, :, at])
        beta_bar = row[1]
        row[2] = 2.0 * (row[0] + beta_bar * inv_rho)
        for n, at in enumerate(spans):
            rb = rb_s[:, at] + pb_s[:, at] + row[2, n : n + 1, :] * sc.nh[i, :, at]
            rb_s[:, at] = rb
            row[3, n : n + 1, :] = col_sum(zb[:, at] * sc.ph[i, :, at] - rb * sc.wh[i, :, at])
        sbar = row[3]
        row[4] = -sbar * s_all * inv_c
        row[0] = sbar * inv_c - beta_bar * beta * inv_rho
        for n, at in enumerate(spans):
            p = sc.ph[i, :, at]
            cbar = row[4, n : n + 1, :]
            s = sc.sh[i, 0, n : n + 1, :]
            wb = cbar * p - s * rb_s[:, at]
            low = wb.astype(BF)
            sc.pl[:, at] = low
            sc.lh[n, :, spot] = low
            sc.fm[1, n : n + 1, :] += col_sum(wb * p)
            pb_s[:, at] = (
                sc.sh[i, 3, n : n + 1, :] * pb_s[:, at]
                + s * zb[:, at]
                + cbar * sc.wh[i, :, at]
                + lam * wb
            )
        for n, at in enumerate(spans):
            both = mm(sc.ks[n], sc.pl[:, at])
            scores = (sc.dt[n] * both[:BLK]).astype(BF)
            sc.sl[n] = scores
            sc.rh[n, :, far] = scores
            sc.xm[n] += sc.rh[n, :, spot].astype(F32) * both[:BLK]
            state_part = sc.dec[0, n : n + 1, :] * both[BLK:]
            pb_s[:, at] = pb_s[:, at] + state_part
            sc.fm[0, n : n + 1, :] += col_sum(sc.ph[i, :, at] * state_part)
        for n, at in enumerate(spans):
            pb_s[:, at] = pb_s[:, at] + mm(sc.kt[:, at], sc.sl[n])

    for i in reversed(range(CG_STEPS)):
        reverse_step(i)
    half = CG_STEPS * BLK
    for n, at in enumerate(spans):
        dkt[:, at] += nt(sc.lh[n], sc.rh[n])
        sc.ds0[n] = nt(sc.lh[n, :, 0:half], sc.fh[n])

    d_sym = jnp.zeros((width, width), F32)
    d_g = jnp.zeros((width, width), F32)
    g_rows = [None] * blocks
    f_rows = [None] * blocks
    x_rows = [None] * blocks
    keep_rows = [None] * blocks
    lower = (row_i >= col_i).astype(BF)
    before = row_i < col_i
    for n in reversed(range(blocks)):
        at = pl.ds(n * BLK, BLK)
        kt = sc.kt[:, at]
        to_row = sc.dec[1, n : n + 1, :]
        keep = sc.dec[2, n : n + 1, :]
        if n + 1 < blocks:
            vt = sc.vt[:, at]
            g_low = d_g.astype(BF)
            part_s = to_row * mm(d_sym.astype(BF), kt)
            part_v = to_row * mm(g_low, kt)
            part_k = to_row * mm(d_g.T.astype(BF), vt)
            dkt[:, at] += part_s + part_k
            dvt[:, at] += part_v
            g_rows[n] = col_sum(0.5 * kt.astype(F32) * part_s + vt.astype(F32) * part_v)
            inner = 0.5 * d_sym * sc.ks[n, BLK:, :].astype(F32) + d_g * sc.g[n].astype(F32)
            keep_rows[n] = keep * jnp.sum(col_sum(inner), axis=1, keepdims=True)
        else:
            g_rows[n] = jnp.zeros((1, BLK), F32)
            keep_rows[n] = jnp.zeros((1, BLK), F32)
        ds0 = sc.ds0[n]
        d_sym = keep * d_sym + ds0 + ds0.T
        d_g = keep * d_g + sc.dg0[n]
        x = sc.xm[n]
        high = x.astype(BF)
        low = (x - high.astype(F32)).astype(BF)
        summed = mm(high, lower) + mm(low, lower)
        x_rows[n] = col_sum(jnp.where(before, summed, 0.0))
        f_rows[n] = sc.fm[0, n : n + 1, :]
    f_all = jnp.concatenate(f_rows, axis=0)
    g_all = jnp.concatenate(g_rows, axis=0)
    da = (
        jnp.dot(f_all, (row_i >= col_i).astype(F32), precision=precise, preferred_element_type=F32)
        + jnp.dot(g_all, before.astype(F32), precision=precise, preferred_element_type=F32)
        + jnp.concatenate(x_rows, axis=0)
        + jnp.concatenate(keep_rows, axis=0)
    )
    da = jnp.concatenate([da[n : n + 1, :] for n in range(blocks)], axis=1)
    base = prea_ref[0, :, :] + jnp.full((1, total), bias_ref[0, head], F32)
    da = -sigmoid(base) * da
    da_ref[0, :, :] = da
    d_bias = jnp.sum(da, axis=1, keepdims=True)
    d_lam = jnp.sum(col_sum(sc.fm[1]), axis=1, keepdims=True)
    d_lam = d_lam * sigmoid(jnp.full((1, BLK), bias_ref[1, head], F32) + ridge_shift)
    lane = lax.broadcasted_iota(jnp.int32, (1, BLK), 1)
    dhead_ref[0, :, :] = jnp.where(lane == 0, d_bias, d_lam)

    taps = taps_ref.shape[2]
    live = live_ref[...]
    scale_k = sc.scale[1:2, :]
    rho_bar = jnp.concatenate([row[0, n : n + 1, :] for n in range(blocks)], axis=1)
    sc.wide[0] = jnp.broadcast_to(2.0 * rho_bar, (CHUNK, total))
    sc.wide[1] = jnp.broadcast_to(sc.scale[0:1, :], (CHUNK, total))
    sc.wide[2] = jnp.broadcast_to(live, (CHUNK, total))
    sc.wide[3] = jnp.broadcast_to(scale_k, (CHUNK, total))

    def query_grad(at, acc):
        q = sc.q[at, :]
        grad = rb_s[at, :] + pb_s[at, :] + sc.wide[0] * q
        pb_s[at, :] = grad
        return acc + q * grad

    def key_grad(at, acc):
        grad = dkt[at, :] * sc.wide[2]
        dkt[at, :] = grad
        return acc + (sc.xk[at, :] * sc.wide[3]) * grad

    zero = jnp.zeros((CHUNK, total), F32)
    mean_q = col_sum(by_chunks(width, query_grad, zero))
    mean_k = col_sum(by_chunks(width, key_grad, zero))
    sc.wide[0] = jnp.broadcast_to(mean_q, (CHUNK, total))
    sc.wide[4] = jnp.broadcast_to(mean_k, (CHUNK, total))

    def through(j, at, du):
        taps_now = taps_ref[j, at, :]
        rows = proj_ref[j, at, :]
        d_rows = du * taps_now[:, 0:1]
        sums = [jnp.sum(rows * du, axis=1, keepdims=True)]
        for i in range(1, taps):
            moved = pltpu.roll(du * sc.mask[i], total - i, 1)
            d_rows = d_rows + moved * taps_now[:, i : i + 1]
            sums.append(jnp.sum(rows * moved, axis=1, keepdims=True))
        dproj_ref[j, at, :] = d_rows.astype(BF)
        dtaps_ref[j, at, :] = jnp.concatenate(sums, axis=1)

    def query_rows(at, carry):
        grad = sc.wide[1] * (pb_s[at, :] - sc.q[at, :] * sc.wide[0])
        through(0, at, grad * sc.slope[0, at, :])
        return carry

    def key_rows(at, carry):
        scale = sc.wide[3]
        grad = scale * (dkt[at, :] - (sc.xk[at, :] * scale) * sc.wide[4])
        through(1, at, grad * sc.slope[1, at, :])
        return carry

    def value_rows(at, carry):
        through(2, at, (dvt[at, :] * sc.wide[2]) * sc.slope[2, at, :])
        return carry

    for fn in (query_rows, key_rows, value_rows):
        by_chunks(width, fn, 0)

    slots, rank = basis_ref.shape[0], basis_ref.shape[1]
    inner = jnp.concatenate(
        [high_low(halves(mm(high_low(basis_ref[j]), dproj_ref[j]))) for j in range(slots)], axis=0
    )
    both = mm(inner, packed_ref[...])
    deep = packed_ref.shape[1]
    for j in range(slots):
        at = slice(j * deep, (j + 1) * deep)
        sketch_ref[:, at] = left_ref[:, at] + halves(both[2 * rank * j : 2 * rank * (j + 1)])
    if left_ref.shape[1] > slots * deep:
        sketch_ref[:, slots * deep :] = left_ref[:, slots * deep :]


def scratch_of(width, total, backward):
    blocks = total // BLK
    flat = ((width, total), F32)
    flat_low = ((width, total), BF)
    square = ((blocks, BLK, BLK), F32)
    square_low = ((blocks, BLK, BLK), BF)
    own = dict(
        q=flat,
        mask=((4, CHUNK, total), F32),
        kt=flat_low,
        vt=flat_low,
        ks=((blocks, 2 * BLK, width), BF),
        g=square_low,
        dt=square,
        dec=((3, blocks, BLK), F32),
        scale=((8, total), F32),
        row=((5, blocks, BLK), F32),
        z=flat,
        p=flat,
        r=flat,
        w=flat,
        pl=flat_low,
        sl=square_low,
    )
    if backward:
        history = ((CG_STEPS, width, total), F32)
        own.update(
            xk=flat,
            xv=flat,
            slope=((3, width, total), F32),
            wide=((5, CHUNK, total), F32),
            vg=((blocks, 2 * BLK, width), BF),
            ph=history,
            wh=history,
            nh=history,
            lh=((blocks, width, 2 * CG_STEPS * BLK), BF),
            rh=((blocks, BLK, 2 * CG_STEPS * BLK), BF),
            fh=((blocks, width, CG_STEPS * BLK), BF),
            sh=((CG_STEPS, 4, blocks, BLK), F32),
            do=flat_low,
            sl2=square_low,
            dkt=flat,
            dvt=flat,
            zb=flat,
            rb=flat,
            pb=flat,
            dg0=square,
            ds0=square,
            xm=square,
            fm=((2, blocks, BLK), F32),
        )
    else:
        own.update(x=flat)
    return list(own), [pltpu.VMEM(shape, kind) for shape, kind in own.values()]


def mixer_call(kernel, backward, head, arrays, lens, bias, deps, cost):
    proj, pre_a, taps, live = arrays[:4]
    slots, columns, total = proj.shape
    heads = pre_a.shape[0]
    width = columns // heads
    names, scratch = scratch_of(width, total, backward)
    smem = pl.BlockSpec(memory_space=pltpu.SMEM)
    kinds, count = taps.shape[0], taps.shape[2]
    in_specs = [
        pl.BlockSpec((slots, width, total), lambda g: (0, head, 0)),
        pl.BlockSpec((1, 1, total), lambda g: (head, 0, 0)),
        pl.BlockSpec((kinds, width, count), lambda g: (0, head, 0)),
        pl.BlockSpec((1, total), lambda g: (0, 0)),
    ]
    if backward:
        basis, packed, left = arrays[5:]
        in_specs += [
            pl.BlockSpec((width, total), lambda g: (head, 0)),
            pl.BlockSpec((slots, basis.shape[1], width), lambda g: (0, 0, head)),
            pl.BlockSpec(packed.shape, lambda g: (0, 0)),
            pl.BlockSpec(left.shape, lambda g: (0, 0)),
        ]
        out_specs = (
            pl.BlockSpec((slots, width, total), lambda g: (0, 0, 0)),
            pl.BlockSpec((1, 1, total), lambda g: (0, 0, 0)),
            pl.BlockSpec((kinds, width, count), lambda g: (0, 0, 0)),
            pl.BlockSpec((1, 1, BLK), lambda g: (0, 0, 0)),
            pl.BlockSpec(left.shape, lambda g: (0, 0)),
        )
        out_shape = (
            jax.ShapeDtypeStruct((slots, width, total), BF),
            jax.ShapeDtypeStruct((1, 1, total), F32),
            jax.ShapeDtypeStruct((kinds, width, count), F32),
            jax.ShapeDtypeStruct((1, 1, BLK), F32),
            jax.ShapeDtypeStruct(left.shape, F32),
        )
    else:
        out_specs = pl.BlockSpec((width, total), lambda g: (0, 0))
        out_shape = jax.ShapeDtypeStruct((width, total), BF)
    in_specs += [smem, smem] + [pl.BlockSpec(memory_space=pl.ANY)] * len(deps)
    own = len(arrays) + 2

    def body(*refs):
        kernel(names, head, *refs[:own], *refs[own + len(deps) :])

    return pl.pallas_call(
        body,
        grid=(1,),
        in_specs=in_specs,
        out_specs=out_specs,
        out_shape=out_shape,
        scratch_shapes=scratch,
        compiler_params=pltpu.CompilerParams(vmem_limit_bytes=56 * 2**20),
        cost_estimate=pl.CostEstimate(flops=cost * 10**9, bytes_accessed=cost * 3 * 10**6, transcendentals=0),
        name="mixer_backward" if backward else "mixer_forward",
    )(*arrays, lens, bias, *deps)


def mixer_forward(head, proj, pre_a, taps, live, lens, bias, deps=()):
    return mixer_call(forward_kernel, False, head, (proj, pre_a, taps, live), lens, bias, deps, 11)


def mixer_backward(head, proj, pre_a, taps, live, d_gated, basis, packed, left, lens, bias, deps=()):
    arrays = (proj, pre_a, taps, live, d_gated, basis, packed, left)
    return mixer_call(backward_kernel, True, head, arrays, lens, bias, deps, 28)


def any_specs(deps):
    return [pl.BlockSpec(memory_space=pl.ANY)] * len(deps)


def row_of(pair, k):
    return pair, pl.BlockSpec((pl.squeezed,) + pair.shape[1:], lambda g: (k, 0, 0))


def call(body, name, inputs, outs, deps=(), cost=1):
    whole = pl.BlockSpec(memory_space=pltpu.VMEM)
    count = len(inputs)

    def kernel(*refs):
        body(*refs[:count], *refs[count + len(deps) :])

    kinds = [i[1] if isinstance(i, tuple) else whole for i in inputs]
    inputs = [i[0] if isinstance(i, tuple) else i for i in inputs]
    return pl.pallas_call(
        kernel,
        grid=(1,),
        in_specs=kinds + any_specs(deps),
        out_specs=[whole] * len(outs),
        out_shape=[jax.ShapeDtypeStruct(*o) for o in outs],
        compiler_params=pltpu.CompilerParams(vmem_limit_bytes=56 * 2**20),
        cost_estimate=pl.CostEstimate(flops=cost * 10**9, bytes_accessed=cost * 3 * 10**6, transcendentals=0),
        name=name,
    )(*inputs, *deps)


def pass_on(keep, received, deps=()):
    def body(keep_ref, got_ref, out_ref):
        out_ref[...] = (keep_ref[...].astype(F32) + got_ref[...].astype(F32)).astype(BF)

    return call(body, "pass_on", [row_of(keep, 1), row_of(received, 1)], [(keep.shape[1:], BF)], deps)[0]


def second_norm(tokens, keep, beside, across, gain, deps=()):
    def body(x_ref, keep_ref, beside_ref, across_ref, gain_ref, resid_ref, normed_ref):
        x = x_ref[...].astype(F32)
        x = x + (keep_ref[...].astype(F32) + beside_ref[...].astype(F32) + across_ref[...].astype(F32))
        resid_ref[...] = x
        scale = lax.rsqrt(jnp.mean(x * x, axis=1, keepdims=True) + tiny_eps)
        normed_ref[...] = (x * scale * gain_ref[...]).astype(BF)

    return call(
        body, "second_norm", [tokens, row_of(keep, 0), row_of(beside, 0), across, gain],
        [(tokens.shape, F32), (tokens.shape, BF)], deps,
    )


def pulled_back(x, keep, beside, across, gain):
    grad = keep.astype(F32) + beside.astype(F32) + across.astype(F32)
    x = x.astype(F32)
    scale = lax.rsqrt(jnp.mean(x * x, axis=1, keepdims=True) + tiny_eps)
    unit = x * scale
    scaled = grad * gain
    return scale * (scaled - unit * jnp.mean(unit * scaled, axis=1, keepdims=True)), grad, unit


def norm_back(base, x, keep, beside, across, gain, deps=()):
    def body(base_ref, x_ref, keep_ref, beside_ref, across_ref, gain_ref, out_ref, low_ref, gain_out_ref):
        back, grad, unit = pulled_back(x_ref[...], keep_ref[...], beside_ref[...], across_ref[...], gain_ref[...])
        out = base_ref[...] + back
        out_ref[...] = out
        low_ref[...] = out.astype(BF)
        gain_out_ref[...] = col_sum(grad * unit)

    return call(
        body, "norm_back", [base, x, row_of(keep, 0), row_of(beside, 0), across, gain],
        [(x.shape, F32), (x.shape, BF), (gain.shape, F32)], deps,
    )


def norm_back_into(target, m, count, base, x, keep, beside, across, gain):
    share, width = base.shape

    def body(base_ref, x_ref, keep_ref, beside_ref, across_ref, gain_ref, *refs):
        back, grad, unit = pulled_back(x_ref[...], keep_ref[...], beside_ref[...], across_ref[...], gain_ref[...])
        refs[-1][...] = base_ref[...] + back

    inputs = [base, row_of(x, m), row_of(keep, 0), row_of(beside, 0), across, gain]
    whole = pl.BlockSpec(memory_space=pltpu.VMEM)
    old = [] if target is None else [target]
    return pl.pallas_call(
        body,
        grid=(1,),
        in_specs=[i[1] if isinstance(i, tuple) else whole for i in inputs] + any_specs(old),
        out_specs=pl.BlockSpec((pl.squeezed, share, width), lambda g: (m, 0, 0)),
        out_shape=jax.ShapeDtypeStruct((count, share, width), F32),
        input_output_aliases={len(inputs): 0} if old else {},
        name="norm_back_into",
    )(*[i[0] if isinstance(i, tuple) else i for i in inputs], *old)


def add_rows(resid, parts, across, deps=()):
    count = len(resid)
    shape = (count,) + resid[0].shape

    def body(*refs):
        out_ref = refs[-1]
        for m in range(count):
            x, keep, beside, far = (r[...] for r in refs[4 * m : 4 * m + 4])
            out_ref[m] = (x + (keep.astype(F32) + beside.astype(F32) + far.astype(F32))).astype(BF)

    inputs = []
    for x, (keep, beside), far in zip(resid, parts, across):
        inputs += [x, row_of(keep, 0), row_of(beside, 0), far]
    return call(body, "add_rows", inputs, [(shape, BF)], deps)[0]


def ffn_pass(rows, grads, w_ff, basis_ff, basis_down, deps=()):
    share, width = rows[0].shape
    total = 4 * share
    hidden_width = w_ff.shape[2]
    rank = basis_ff.shape[1]
    tile = 2 * share

    def body(*refs):
        row_refs, grad_refs = refs[:4], refs[4:8]
        ff_ref, bff_ref, bdown_ref = refs[8:11]
        hidden_ref, dgu_ref, two_keep, two_send, ffn_keep, ffn_send, left_ff, left_down, x_s, dy_s = refs[11:]
        for k in range(4):
            x_s[k * share : (k + 1) * share, :] = row_refs[k][...]
            dy_s[k * share : (k + 1) * share, :] = grad_refs[k][...]
        left_ff[...] = jnp.zeros_like(left_ff)
        left_down[...] = jnp.zeros_like(left_down)

        def step(i, carry):
            at = pl.ds(pl.multiple_of(i * tile, tile), tile)
            x, dy = x_s[at, :], dy_s[at, :]
            gate = mm(x, ff_ref[0])
            up = mm(x, ff_ref[1])
            sig = jax.nn.sigmoid(gate)
            act = gate * sig
            hidden = (act * up).astype(BF)
            d_hidden = mm(dy, ff_ref[2])
            d_gate = (d_hidden * up * sig * (1.0 + gate * (1.0 - sig))).astype(BF)
            d_up = (d_hidden * act).astype(BF)
            hidden_ref[at, :] = hidden
            dgu_ref[0, at, :] = d_gate
            dgu_ref[1, at, :] = d_up
            two = (nt(d_gate, ff_ref[0]) + nt(d_up, ff_ref[1])).astype(BF)
            two_keep[i] = two[:share]
            two_send[i] = two[share:]
            ffn = nt(hidden, ff_ref[2]).astype(BF)
            ffn_keep[i] = ffn[:share]
            ffn_send[i] = ffn[share:]
            for j, d in enumerate((d_gate, d_up)):
                inner = halves(nt(high_low(bff_ref[j]), d))
                left_ff[j] += halves(mm(high_low(inner), x))
            inner = halves(nt(high_low(bdown_ref[...]), dy))
            left_down[...] += halves(mm(high_low(inner), hidden))
            return carry

        lax.fori_loop(0, 2, step, 0)

    pair = ((2, share, width), BF)
    return call(
        body, "ffn_pass", [*rows, *grads, w_ff, basis_ff, basis_down],
        [
            ((total, hidden_width), BF), ((2, total, hidden_width), BF), pair, pair, pair, pair,
            ((2, rank, width), F32), ((rank, hidden_width), F32), ((total, width), BF), ((total, width), BF),
        ],
        deps, cost=12,
    )


def add_steps(values, axis):
    flip, count = 1, lax.axis_size(axis)
    moved, deps = [jnp.zeros_like(v) for v in values], ()
    while flip < count:
        moved = [swap(v, axis, flip) for v in values]
        deps = yield values
        flip *= 2
        if flip < count:
            values = add_after(values, moved, deps)
    return values, moved, deps


def add_after(left, right, deps=()):
    count = len(left)

    def body(*refs):
        for k in range(count):
            refs[2 * count + k][...] = refs[k][...] + refs[count + k][...]

    return call(body, "add_after", [*left, *right], [(v.shape, v.dtype) for v in left], deps)


def finish_steps(steps, deps=None):
    try:
        if deps is None:
            next(steps)
        while True:
            steps.send(deps or ())
    except StopIteration as end:
        return end.value


def gate(value, deps):
    return pl.pallas_call(
        lambda *refs: None,
        in_specs=any_specs((value, *deps)),
        out_specs=pl.BlockSpec(memory_space=pl.ANY),
        out_shape=jax.ShapeDtypeStruct(value.shape, value.dtype),
        input_output_aliases={0: 0},
        name="gate",
    )(value, *deps)


def each_block(groups):
    out = []
    for k, (array, flipped) in enumerate(groups):
        count, m, n = array.shape
        m, n = (n, m) if flipped else (m, n)
        out += [(k, j, flipped, m, n) for j in range(count)]
    return out


def frames_and_basis(left, right, groups, count, deps=()):
    rank = left.shape[0]
    blocks = each_block(groups)

    def body(left_ref, right_ref, *refs):
        frame_ref, right_out = refs[len(groups) :]
        edge, edge_n = 0, 0
        for k, j, flipped, m, n in blocks:
            sketch = (left_ref[:, edge : edge + m] + right_ref[:, edge : edge + m]) * (1.0 / count)
            done = []
            for r in range(rank):
                column = sketch[0:1]
                column = column * lax.rsqrt(jnp.sum(column * column, axis=1, keepdims=True) + tiny_eps)
                done.append(column)
                if r + 1 < rank:
                    sketch = sketch[1:]
                    sketch = sketch - jnp.sum(column * sketch, axis=1, keepdims=True) * column
            frame = jnp.concatenate(done, axis=0)
            frame_ref[:, edge : edge + m] = frame
            right_out[:, edge_n : edge_n + n] = times_block(frame, refs[k][j], flipped)
            edge, edge_n = edge + m, edge_n + n

    return call(
        body, "frames_and_basis", [left, right] + [a for a, f in groups],
        [(left.shape, F32), ((rank, sum(b[4] for b in blocks)), F32)], deps,
    )


def times_block(few, block, transposed):
    both = high_low(few)
    high = block.astype(BF)
    low = (block - high.astype(F32)).astype(BF)
    by = nt if transposed else mm
    return halves(by(both, high)) + by(both, low)[: few.shape[0]]


def basis_and_errors(frame, left, right, groups, count, deps=()):
    blocks = each_block(groups)

    def body(frame_ref, left_ref, right_ref, *refs):
        basis_ref = refs[len(groups)]
        out_refs = refs[len(groups) + 1 :]
        edge, edge_n = 0, 0
        for k, j, flipped, m, n in blocks:
            basis = (left_ref[:, edge_n : edge_n + n] + right_ref[:, edge_n : edge_n + n]) * (1.0 / count)
            basis_ref[:, edge_n : edge_n + n] = basis
            frame = frame_ref[:, edge : edge + m]
            high_f, high_b = frame.astype(BF).astype(F32), basis.astype(BF).astype(F32)
            f = jnp.concatenate([high_f, frame - high_f, high_f, jnp.zeros_like(frame)], axis=0)
            b = jnp.concatenate([high_b, high_b, basis - high_b, jnp.zeros_like(basis)], axis=0)
            if flipped:
                f, b = b, f
            out_refs[k][j] = refs[k][j] - mm(f.T.astype(BF), b.astype(BF))
            edge, edge_n = edge + m, edge_n + n

    arrays = [a for a, f in groups]
    return call(
        body, "basis_and_errors", [frame, left, right, *arrays],
        [(left.shape, F32)] + [(a.shape, F32) for a in arrays], deps,
    )


def sketches(groups, bases, deps=()):
    rank = bases[0].shape[1]
    blocks = each_block(groups)

    def body(*refs):
        edge = 0
        for k, j, flipped, m, n in blocks:
            refs[-1][:, edge : edge + m] = times_block(refs[len(groups) + k][j], refs[k][j], not flipped)
            edge += m

    return call(
        body, "sketches", [a for a, f in groups] + bases, [((rank, sum(b[3] for b in blocks)), F32)], deps
    )[0]


momentum_decay = 0.5
step_rate = 1.0
small_rate = 0.05


def swap(value, axis, flip):
    count = lax.axis_size(axis)
    return lax.ppermute(value, axis, [(i, i ^ flip) for i in range(count)])


def gather_rows(own):
    beside = swap(own, "tensor", 1)
    across = swap(own, "tensor", 2)
    return [own, beside, across, swap(across, "tensor", 1)]


def advance_weight(weight, moment, grad_now, rate):
    moment_new = momentum_decay * moment + grad_now
    return (weight - rate * moment_new, moment_new)


def dot32(spec, a, b):
    return jnp.einsum(spec, a, b, preferred_element_type=jnp.float32)


def on_device(
    tokens,
    cotangent,
    slot_order,
    lengths,
    live_mask,
    w_in,
    w_out,
    w_ff,
    w_down,
    norm_gains,
    conv_taps,
    decay_w,
    mesa_bias,
    mom_in,
    mom_out,
    mom_ff,
    mom_down,
    mom_gains,
    mom_conv,
    mom_decay,
    mom_bias,
    err_in,
    err_out,
    err_ff,
    err_down,
    basis_in,
    basis_out,
    basis_ff,
    basis_down,
):
    dp_count = lax.axis_size("dp")
    dp_index = lax.axis_index("dp")
    mine = lax.axis_index("tensor")
    shard_count = lax.axis_size("tensor")
    micro_count, share, width = tokens.shape
    total = share * shard_count
    decay_low = decay_w.astype(BF)
    first = jnp.concatenate([w_in.astype(BF), jnp.transpose(w_out.astype(BF))[None]], axis=0)
    second = jnp.concatenate([w_ff.astype(BF), jnp.transpose(w_down.astype(BF))[None]], axis=0)
    weights_first = lax.all_gather(first, "dp", axis=1, tiled=True)
    weights_in = weights_first[:4]
    weights_out = weights_first[4]
    weights_ff = lax.all_gather(second, "dp", axis=1, tiled=True)
    taps_cols = jnp.transpose(conv_taps, (0, 2, 1))
    gain_one, gain_two = norm_gains[0:1], norm_gains[1:2]
    bases = [jnp.swapaxes(b, 1, 2) for b in (basis_in, basis_out, basis_ff, basis_down)]
    micros = range(micro_count)
    heads = range(mesa_bias.shape[1])
    last = micro_count - 1
    pieces_one, group_one, pieces_dy, place, live, lens = [], [], [], [], [], []
    for m in micros:
        row = tokens[m].astype(F32)
        scale = lax.rsqrt(jnp.mean(row * row, axis=1, keepdims=True) + tiny_eps)
        pieces_one.append(gather_rows((row * scale * gain_one).astype(BF)))
        group_one.append(jnp.concatenate(pieces_one[m], axis=0))
        order_now = slot_order[m, 0]
        near = jnp.bitwise_xor(order_now // share, mine) * share + order_now % share
        slots = lax.broadcasted_iota(jnp.int32, (total, total), 1)
        place.append((near[:, None] == slots).astype(BF))
        live.append(live_mask[m].astype(F32))
        lens.append(lengths[m, 0])

    packed, proj, pre_decay, gated_u = [], [], [], []
    resid, group_two, passed_mix, send_two, keep_mix, beside_mix = [], [], [], [], [], []

    def project(m):
        packed.append(dot32("ji,id->jd", place[m], group_one[m]).astype(BF))
        proj.append(dot32("jdc,td->jct", weights_in, packed[m]))
        pre_decay.append(dot32("dh,td->ht", decay_low, packed[m])[:, None, :])

    def forward(m, h, deps):
        return mixer_forward(h, proj[m], pre_decay[m], taps_cols, live[m], lens[m], mesa_bias, deps)

    def mix_out(m, gated):
        gated_u.append(dot32("cj,ji->ci", jnp.concatenate(gated, axis=0), place[m]).astype(BF))
        terms = dot32("ci,dc->id", gated_u[m], weights_out).astype(BF).reshape(2, 2, share, width)
        keep_mix.append(terms[:, 0])
        send = terms[:, 1]
        beside_mix.append(swap(send, "tensor", 1))
        return send

    def pass_mix(m, deps):
        passed_mix.append(pass_on(keep_mix[m], beside_mix[m], deps))

    def norm_two(m, deps):
        across = swap(passed_mix[m], "tensor", 2)
        own, low = second_norm(tokens[m], keep_mix[m], beside_mix[m], across, gain_two, deps)
        resid.append(own)
        send_two.append(low)
        group_two.append(gather_rows(low))

    err_ff_t = jnp.swapaxes(err_ff[0], 1, 2)
    err_left = sketches([(err_ff_t, True), (err_down, False)], [bases[2], bases[3]])
    left_in = sketches([(err_in[0], False)], [bases[0]])
    project(0)
    gated = [forward(0, h, (err_left, left_in)) for h in heads]
    for m in micros:
        pieces_dy.append(gather_rows(gate(cotangent[m].astype(BF), (gated[min(m, 1)],))))
    sent = mix_out(0, gated)
    project(1)
    pass_mix(0, (proj[1],))
    gated = [forward(1, 0, (passed_mix[0],))]
    norm_two(0, (gated[0],))
    gated.append(forward(1, 1, (send_two[0],)))
    sent = mix_out(1, gated)

    hidden, d_gate_up, two_keep, two_beside, two_passed, ffn_parts, left_ff, left_down = [[] for i in range(8)]
    rows_of_two, rows_of_dy = [], []

    def feed_forward(m, deps):
        h, dgu, keep, send, ffn_keep, ffn_send, lf, ld, rows_two, rows_dy = ffn_pass(
            group_two[m], pieces_dy[m], weights_ff, bases[2], bases[3][0], deps
        )
        hidden.append(h)
        d_gate_up.append(dgu)
        two_keep.append(keep)
        two_beside.append(swap(send, "tensor", 1))
        ffn_parts.append((ffn_keep, swap(ffn_send, "tensor", 1)))
        left_ff.append(lf)
        left_down.append(ld)
        rows_of_two.append(rows_two)
        rows_of_dy.append(rows_dy)
        return send

    d_resid, send_back, gains_two, d_group = [], [], [], []

    def back_two(m, deps):
        across = swap(two_passed[m], "tensor", 2)
        out, low, gain = norm_back(
            cotangent[m], resid[m], two_keep[m], two_beside[m], across, gain_two, deps
        )
        d_resid.append(out)
        send_back.append(low)
        gains_two.append(gain)
        d_group.append(gather_rows(low))

    def pass_two(m, deps):
        two_passed.append(pass_on(two_keep[m], two_beside[m], deps))

    def weight_grads(m):
        return dot32("jth,td->jhd", d_gate_up[m], rows_of_two[m]), dot32("th,td->hd", hidden[m], rows_of_dy[m])

    sent = feed_forward(0, (sent,))
    pass_mix(1, (sent,))
    grads_first = weight_grads(0)
    norm_two(1, grads_first)
    pass_two(0, (group_two[1][2],))
    sent = feed_forward(1, (two_passed[0],))
    back_two(0, (sent,))
    pass_two(1, (send_back[0],))
    grads_last = weight_grads(1)
    merged_early = [
        (grads_first[0] + grads_last[0] + err_ff_t, True),
        ((grads_first[1] + grads_last[1])[None] + err_down, False),
    ]
    left_ff = sum(left_ff)
    early = jnp.concatenate([left_ff[0], left_ff[1], sum(left_down)], axis=1) + err_left

    def factor_steps():
        (left,), (right,), deps = yield from add_steps([early], "dp")
        frame, own = frames_and_basis(left, right, merged_early, dp_count, deps)
        (left,), (right,), deps = yield from add_steps([own], "dp")
        return (frame,) + tuple(basis_and_errors(frame, left, right, merged_early, dp_count, deps))

    steps = factor_steps()
    next(steps)
    (waiting,) = steps.send((merged_early[0][0], merged_early[1][0]))
    grad_out, grad_in, grad_decay, grad_taps, grad_head = 0.0, 0.0, 0.0, 0.0, 0.0
    back_parts, ffn_passed, before_last = [], [], []
    for m in micros:
        grad_out = grad_out + dot32("ci,id->cd", gated_u[m], jnp.concatenate(d_group[m], axis=0))
        d_mix = dot32("ji,id->jd", place[m], jnp.concatenate(d_group[m], axis=0)).astype(BF)
        d_gated = dot32("dc,td->ct", weights_out, d_mix)
        pieces = []
        if m == last:
            merged_out = grad_out[None] + err_out
            left_in = jnp.concatenate([left_in, sketches([(merged_out, False)], [bases[1]])], axis=1)
        for h in heads:
            deps = [waiting] + before_last * (m == last and h == heads[-1])
            if m == 0 and h == 0:
                deps.append(two_passed[1])
            if m == 0 and h == 1:
                back_two(1, (pieces[0][3],))
                deps.append(send_back[1])
            pieces.append(
                mixer_backward(
                    h, proj[m], pre_decay[m], taps_cols, live[m], d_gated, bases[0], packed[m], left_in,
                    lens[m], mesa_bias, deps,
                )
            )
            left_in = pieces[-1][4]
            done = (pieces[-1][3],)
            if m < last:
                keep, beside = ffn_parts[h]
                ffn_passed.append(pass_on(keep, beside, done))
            if (m, h) != (last, heads[-1]):
                (waiting,) = steps.send(done)
        d_heads = [p[0] for p in pieces]
        d_proj = jnp.concatenate(d_heads, axis=1)
        d_decay = jnp.concatenate([p[1][0] for p in pieces], axis=0).astype(BF)
        grad_taps = grad_taps + jnp.concatenate([p[2] for p in pieces], axis=1)
        grad_head = grad_head + jnp.concatenate([p[3] for p in pieces], axis=0)[:, 0]
        d_proj = dot32("kcj,ji->kci", d_proj, place[m]).astype(BF)
        if m == last:
            late = add_steps([left_in], "dp")
            next(late)
            (summed,) = late.send((d_proj,))
            d_proj = gate(d_proj, (summed,))
        grad_in = grad_in + dot32("id,kci->kdc", group_one[m], d_proj)
        if m == last:
            merged = [(grad_in + err_in[0], False), (merged_out, False)]
            (summed,) = late.send((merged[0][0],))
            d_proj = gate(d_proj, (summed,))
        d_decay = dot32("hj,ji->hi", d_decay, place[m]).astype(BF)
        d_one = dot32("kci,kdc->id", d_proj, weights_in) + dot32("hi,dh->id", d_decay, decay_low)
        d_one = d_one.astype(BF).reshape(2, 2, share, width)
        back_parts.append((d_one[:, 0], swap(d_one[:, 1], "tensor", 1)))
        grad_decay = grad_decay + dot32("hi,id->hd", d_decay, group_one[m])
        before_last = [grad_in, d_one]

    gain_grad = jnp.sum(weights_in.astype(F32) * grad_in, axis=(0, 2)) + jnp.sum(
        decay_low.astype(F32).T * grad_decay, axis=0
    )
    gains = jnp.concatenate([gain_grad[None] / gain_one, sum(gains_two)], axis=0)
    (left,), (right,), unused = finish_steps(add_steps([gains.reshape(-1, BLK)], "tensor"))
    gains = (left + right).reshape(gains.shape)
    small = [jnp.transpose(grad_taps, (0, 2, 1)), grad_decay, grad_head, gains]
    flat = jnp.concatenate([s.reshape(-1, BLK) for s in small], axis=0)

    (left,), (right,), unused = finish_steps(late, (d_one,))
    frame_late, own = frames_and_basis(left, right, merged, dp_count, (d_one,))
    try:
        while True:
            steps.send((own,))
    except StopIteration as end:
        frame_early, basis_early, *errors_early = end.value
    back_passed = [pass_on(*back_parts[m], (own,) if m == last else ()) for m in micros]
    (left, flat), (right, flat_moved), unused = finish_steps(add_steps([own, flat], "dp"))
    flat = (flat + flat_moved) / dp_count

    across = [swap(v, "tensor", 2) for v in ffn_passed]
    out_tokens = add_rows(resid, ffn_parts, across, (own,))
    back_across = [swap(v, "tensor", 2) for v in back_passed]
    d_tokens = None
    for m in micros:
        if m == last:
            deps = (back_passed[last], d_tokens, out_tokens)
            basis_late, *errors_late = basis_and_errors(frame_late, left, right, merged, dp_count, deps)
        keep, beside = back_parts[m]
        d_tokens = norm_back_into(
            d_tokens, m, micro_count, d_resid[m], tokens, keep, beside, back_across[m], gain_one
        )
    parts, edge = [], 0
    for s in small:
        parts.append(flat[edge : edge + s.size // BLK].reshape(s.shape))
        edge += s.size // BLK
    grad_conv, grad_decay, grad_bias, gain_total = parts
    grad_decay = jnp.transpose(grad_decay)
    grad_bias = jnp.transpose(grad_bias[:, :2])

    def part(rows_of, count, axis):
        return lax.dynamic_slice_in_dim(rows_of, dp_index * count, count, axis)

    def cut(rows_of, sizes):
        edge, out = 0, []
        for size in sizes:
            out.append(rows_of[:, edge : edge + size])
            edge += size
        return out

    def outer(frame, basis):
        return jnp.einsum("rm,rn->mn", frame, basis, precision=precise)

    hidden_width = w_ff.shape[2]
    columns = w_in.shape[2]
    frames = cut(frame_late, [width] * 4 + [columns]) + cut(frame_early, [width] * 2 + [hidden_width])
    rights = cut(basis_late, [columns] * 4 + [width]) + cut(basis_early, [hidden_width] * 2 + [width])
    basis_in_new = jnp.stack([b.T for b in rights[:4]])
    basis_out_new = rights[4].T[None]
    basis_ff_new = jnp.stack([b.T for b in rights[5:7]])
    basis_down_new = rights[7].T[None]
    err_in_new, err_out_new = errors_late[0][None], errors_late[1]
    err_ff_new, err_down_new = jnp.swapaxes(errors_early[0], 1, 2)[None], errors_early[1]
    owned_in = jnp.stack([outer(part(f, w_in.shape[1], 1), b) for f, b in zip(frames[:4], rights[:4])])
    owned_ff = jnp.stack([outer(part(f, w_ff.shape[1], 1), b) for f, b in zip(frames[5:7], rights[5:7])])
    owned_out = outer(frames[4], part(rights[4], w_out.shape[1], 1))
    owned_down = outer(frames[7], part(rights[7], w_down.shape[1], 1))
    w_in_new, mom_in_new = advance_weight(w_in, mom_in, owned_in, step_rate)
    w_out_new, mom_out_new = advance_weight(w_out, mom_out, owned_out, step_rate)
    w_ff_new, mom_ff_new = advance_weight(w_ff, mom_ff, owned_ff, step_rate)
    w_down_new, mom_down_new = advance_weight(w_down, mom_down, owned_down, step_rate)
    gains_new, mom_gains_new = advance_weight(norm_gains, mom_gains, gain_total, small_rate)
    conv_new, mom_conv_new = advance_weight(conv_taps, mom_conv, grad_conv, small_rate)
    decay_new, mom_decay_new = advance_weight(decay_w, mom_decay, grad_decay, small_rate)
    bias_new, mom_bias_new = advance_weight(mesa_bias, mom_bias, grad_bias, small_rate)
    return (
        out_tokens,
        d_tokens,
        w_in_new,
        mom_in_new,
        err_in_new,
        basis_in_new,
        w_out_new,
        mom_out_new,
        err_out_new,
        basis_out_new,
        w_ff_new,
        mom_ff_new,
        err_ff_new,
        basis_ff_new,
        w_down_new,
        mom_down_new,
        err_down_new,
        basis_down_new,
        gains_new,
        mom_gains_new,
        conv_new,
        mom_conv_new,
        decay_new,
        mom_decay_new,
        bias_new,
        mom_bias_new,
    )


def solution(mesh):
    placed = (
        P(None, ("dp", "tensor"), None),
        P(None, ("dp", "tensor"), None),
        P(None, "dp", None),
        P(None, "dp", None),
        P(None, "dp", None),
        P(None, "dp", "tensor"),
        P("tensor", "dp"),
        P(None, "dp", "tensor"),
        P("tensor", "dp"),
        P(),
        P(None, None, "tensor"),
        P(None, "tensor"),
        P(None, "tensor"),
        P(None, "dp", "tensor"),
        P("tensor", "dp"),
        P(None, "dp", "tensor"),
        P("tensor", "dp"),
        P(),
        P(None, None, "tensor"),
        P(None, "tensor"),
        P(None, "tensor"),
        P("dp", None, None, "tensor"),
        P("dp", "tensor", None),
        P("dp", None, None, "tensor"),
        P("dp", "tensor", None),
        P(None, "tensor", None),
        P("tensor", None, None),
        P(None, "tensor", None),
        P("tensor", None, None),
    )
    return jax.shard_map(
        on_device,
        mesh=mesh,
        in_specs=placed,
        out_specs=(
            P(None, ("dp", "tensor"), None),
            P(None, ("dp", "tensor"), None),
            P(None, "dp", "tensor"),
            P(None, "dp", "tensor"),
            P("dp", None, None, "tensor"),
            P(None, "tensor", None),
            P("tensor", "dp"),
            P("tensor", "dp"),
            P("dp", "tensor", None),
            P("tensor", None, None),
            P(None, "dp", "tensor"),
            P(None, "dp", "tensor"),
            P("dp", None, None, "tensor"),
            P(None, "tensor", None),
            P("tensor", "dp"),
            P("tensor", "dp"),
            P("dp", "tensor", None),
            P("tensor", None, None),
            P(),
            P(),
            P(None, None, "tensor"),
            P(None, None, "tensor"),
            P(None, "tensor"),
            P(None, "tensor"),
            P(None, "tensor"),
            P(None, "tensor"),
        ),
        check_vma=False,
    )
```

time: 2350 us -> 587 us (0.25)
  matrix products: 752 us -> 120 us
  other arithmetic: 565 us -> 14.1 us
  waiting for transfers between devices: 460 us -> 64.6 us
  local copies, waits for them, and re-layouts: 408 us -> 43.1 us
  Pallas kernels: 0 us -> 276 us
  blocking collectives: 107 us -> 0 us
  starting transfers between devices: 2.12 us -> 43.2 us
    dot_general x264 -> x38, matrix products: 752 us -> 120 us  [the longest x30 108 us: dot32(): return jnp.einsum(spec, a, b, preferred_element_type=jnp.float32)]
    pallas_call x0 -> x45, Pallas kernels: none -> 276 us  [the longest x8 140 us: mixer_call(): pl.pallas_call(body, grid=(1,), in_specs=in_specs, out_specs=out_specs, o...]
    reduce_sum x176 -> x1, other arithmetic: 266 us -> 0.28 us  [on_device(): scale = lax.rsqrt(jnp.mean(row * row, axis=1, keepdims=True) + tiny_eps)]
    all_gather x11 -> x2, waiting for transfers between devices: 198 us -> 22.8 us  [the longest x1 22.8 us: on_device(): weights_first = lax.all_gather(first, 'dp', axis=1, tiled=True)]
    reduce_scatter x8 -> x0, waiting for transfers between devices: 156 us -> none  [the longest x2 64.5 us: on_device(): lax.psum_scatter(ffn_term.astype(jnp.bfloat16), 'tensor', scatter_dimensi...]
    while x162 -> x0, local copies, waits for them, and re-layouts: 150 us -> none
    psum x2 -> x0, waiting for transfers between devices: 103 us -> none  [the longest x1 53.9 us: on_device(): lax.psum((project_left(merged_in, basis_in), project_left(merged_out, bas...]
    dynamic_update_slice x64 -> x0, other arithmetic: 86.2 us -> none  [mesa_head(): lax.scan(advance, (zero_state, zero_state), (keep_end, key_sums, value_su...]
  transfers between devices with their start and end apart: 21 -> 59, of which waited for: 15 -> 9; matrix products, arithmetic and copies ran while one was open for 19% -> 26% of each run, Pallas kernels for 0% -> 46%
where the time goes in v2:
time: 587 us; the launch traced here: 576 us
  Pallas kernels  276 us (47%)
  matrix products  120 us (20%)
  waiting for transfers between devices  64.6 us (11%)
  starting transfers between devices  43.2 us (7%)
  local copies, waits for them, and re-layouts  43.1 us (7%)
  between operations  15.7 us (3%)
  other arithmetic  14.1 us (2%)
    pallas_call x8, Pallas kernels, mixer_call(): pl.pallas_call(body, grid=(1,), in_specs=in_specs, out_specs=out_specs, o...  140 us
    pallas_call x31, Pallas kernels, call(): pl.pallas_call(kernel, grid=(1,), in_specs=kinds + any_specs(deps), out_s...  129 us
    dot_general x30, matrix products, dot32(): return jnp.einsum(spec, a, b, preferred_element_type=jnp.float32)  108 us
    ppermute x57, starting transfers between devices, swap(): return lax.ppermute(value, axis, [(i, i ^ flip) for i in range(count)])  43.1 us
    ppermute x57, waiting for transfers between devices, swap(): return lax.ppermute(value, axis, [(i, i ^ flip) for i in range(count)])  41.8 us
    unnamed x250, local copies, waits for them, and re-layouts  26.8 us
    all_gather x1, waiting for transfers between devices, on_device(): weights_first = lax.all_gather(first, 'dp', axis=1, tiled=True)  22.8 us
  transfers between devices with their start and end apart: 59, of which 9 were waited for; matrix products, arithmetic and copies ran while one was open for 26% of the time, Pallas kernels for 46%

profile of v2, /device:TPU:0, one launch (start us, length us, event | category | flops | bytes accessed | tf_op | source)
XLA Modules:
  0.0 576.2 jit_solution(9236839882110437158)
XLA Ops:
  12.5 2.9 collective-permute-start.1
  19.0 4.2 sketches.4.refs_7_
  23.1 5.9 %sketches.3.refs_6_ = f32[8,2752]{1,0:T(8,128)} custom-call(f32[2,704,1024]{2,1,0:T(8,128)} %bitcast.263, f32[1,704,1024]{2,1,0:T(8,128)} %refs_1_.1, f32[2,8,704]{2,1,0:T(8,128)} %bitcast.278, f32[1,8,1024]{2,1,0:T(8,128)} %bitcast.281), custom_call_target="tpu_custom_call" | custom-call | flops 1000000000 | bytes 3000000 | tf_op jit(solution)/shard_map/sketches/pallas_call | solution.py:604
  31.9 7.0 %collective-permute-done.5 = bf16[256,1024]{1,0:T(8,128)(2,1)} collective-permute-done((bf16[256,1024]{1,0:T(8,128)(2,1)}, bf16[256,1024]{1,0:T(8,128)(2,1)}, u32[]{:S(2)}, u32[]{:S(2)}) %collective-permute-start.5) | collective-permute-done | bytes 524320 | tf_op jit(solution)/shard_map/ppermute | solution.py:890
  38.9 3.9 fusion.55.refs_6_
  45.4 22.8 %all-gather.3.cloned.1.call-done = bf16[5,1024,256]{2,1,0:T(8,128)(2,1)} async-done(((bf16[5,128,256]{2,1,0:T(8,128)(2,1)}), bf16[5,1024,256]{2,1,0:T(8,128)(2,1)}) %all-gather.3.cloned.1.call-update) | async-done | bytes 2621456 | tf_op jit(solution)/shard_map/all_gather | solution.py:948
  68.2 6.6 %fusion.29.refs_0_ = f32[4,256,1024]{2,1,0:T(8,128)} fusion(bf16[5,1024,256]{2,1,0:T(8,128)(2,1)} %all-gather.3.cloned.1.call-done, bf16[1024,1024]{1,0:T(8,128)(2,1)} %copy-done.12), kind=kOutput, calls=%fused_computation.38 | convolution fusion | flops 2147483648 | bytes 8912896 | tf_op jit(solution)/shard_map/jdc,td->jct/dot_general | solution.py:905
  74.8 10.0 %mixer_forward.4.refs_1_ = bf16[128,1024]{1,0:T(8,128)(2,1)} custom-call(f32[4,256,1024]{2,1,0:T(8,128)} %fusion.29.refs_0_, f32[2,1,1024]{2,1,0:T(1,128)} %broadcast_in_dim.36.refs_1_, f32[3,256,4]{2,1,0:T(8,128)} %bitcast.268, f32[1,1024]{1,0:T(1,128)} %get-tuple-element.311.refs_3_, s32[3]{0:T(128)} %get-tuple-element.317.refs_4_.refs_8_, ...), custom_call_target="tpu_custom_call" | custom-call | flops 11000000512 | bytes 33000000 | tf_op jit(solution)/shard_map/mixer_forward/pallas_call | solution.py:565
  84.8 9.6 %mixer_forward.5.refs_1_ = bf16[128,1024]{1,0:T(8,128)(2,1)} custom-call(f32[4,256,1024]{2,1,0:T(8,128)} %fusion.29.refs_0_, f32[2,1,1024]{2,1,0:T(1,128)} %broadcast_in_dim.36.refs_1_, f32[3,256,4]{2,1,0:T(8,128)} %bitcast.269, f32[1,1024]{1,0:T(1,128)} %get-tuple-element.311.refs_3_, s32[3]{0:T(128)} %get-tuple-element.317.refs_4_.refs_8_, ...), custom_call_target="tpu_custom_call" | custom-call | flops 11000000512 | bytes 33000000 | tf_op jit(solution)/shard_map/mixer_forward/pallas_call | solution.py:565
  94.5 2.0 fusion.62
  97.3 2.0 convolution_convert_fusion.1
  100.8 3.9 fusion.56.refs_6_
  109.5 6.7 %fusion.27.refs_2_.refs_0_ = f32[4,256,1024]{2,1,0:T(8,128)} fusion(bf16[5,1024,256]{2,1,0:T(8,128)(2,1)} %all-gather.3.cloned.1.call-done, bf16[1024,1024]{1,0:T(8,128)(2,1)} %copy-done.11), kind=kOutput, calls=%fused_computation.36 | convolution fusion | flops 2147483648 | bytes 8912896 | tf_op jit(solution)/shard_map/jdc,td->jct/dot_general | solution.py:905
  116.2 6.1 %collective-permute-done.12.refs_6_ = bf16[256,1024]{1,0:T(8,128)(2,1)} collective-permute-done((bf16[256,1024]{1,0:T(8,128)(2,1)}, bf16[256,1024]{1,0:T(8,128)(2,1)}, u32[]{:S(2)}, u32[]{:S(2)}) %collective-permute-start.12) | collective-permute-done | bytes 524320 | tf_op jit(solution)/shard_map/ppermute | solution.py:890
  123.3 2.1 pass_on.8.refs_6_
  126.9 10.0 %mixer_forward.6.refs_5_ = bf16[128,1024]{1,0:T(8,128)(2,1)} custom-call(f32[4,256,1024]{2,1,0:T(8,128)} %fusion.27.refs_2_.refs_0_, f32[2,1,1024]{2,1,0:T(1,128)} %broadcast_in_dim.37.refs_1_, f32[3,256,4]{2,1,0:T(8,128)} %bitcast.270, f32[1,1024]{1,0:T(1,128)} %get-tuple-element.310.refs_3_, s32[3]{0:T(128)} %get-tuple-element.316.refs_4_.refs_8_, ...), custom_call_target="tpu_custom_call" | custom-call | flops 11000000512 | bytes 33000000 | tf_op jit(solution)/shard_map/mixer_forward/pallas_call | solution.py:565
  136.9 7.4 %collective-permute-done.7.refs_3_ = bf16[256,1024]{1,0:T(8,128)(2,1)S(1)} collective-permute-done((bf16[256,1024]{1,0:T(8,128)(2,1)}, bf16[256,1024]{1,0:T(8,128)(2,1)S(1)}, u32[]{:S(2)}, u32[]{:S(2)}) %collective-permute-start.7) | collective-permute-done | bytes 524320 | tf_op jit(solution)/shard_map/ppermute | solution.py:890
  145.1 3.0 second_norm.2
  149.5 9.6 %mixer_forward.7 = bf16[128,1024]{1,0:T(8,128)(2,1)} custom-call(f32[4,256,1024]{2,1,0:T(8,128)} %fusion.27.refs_2_.refs_0_, f32[2,1,1024]{2,1,0:T(1,128)} %broadcast_in_dim.37.refs_1_, f32[3,256,4]{2,1,0:T(8,128)} %bitcast.271, f32[1,1024]{1,0:T(1,128)} %get-tuple-element.310.refs_3_, s32[3]{0:T(128)} %get-tuple-element.316.refs_4_.refs_8_, ...), custom_call_target="tpu_custom_call" | custom-call | flops 11000000512 | bytes 33000000 | tf_op jit(solution)/shard_map/mixer_forward/pallas_call | solution.py:565
  159.1 2.0 fusion.63
  161.9 2.0 convolution_convert_fusion
  166.6 20.1 %ffn_pass.2 = (bf16[1024,704]{1,0:T(8,128)(2,1)}, bf16[2,1024,704]{2,1,0:T(8,128)(2,1)}, bf16[2,256,1024]{2,1,0:T(8,128)(2,1)}, bf16[2,256,1024]{2,1,0:T(8,128)(...) custom-call(bf16[256,1024]{1,0:T(8,128)(2,1)} %get-tuple-element.91., ...), custom_call_target="tpu_custom_call" | custom-call | flops 12000000000 | bytes 36000000 | tf_op jit(solution)/shard_map/ffn_pass/pallas_call | solution.py:604
  186.9 2.3 pass_on.9
  190.7 6.7 %fusion.25.refs_5_ = f32[2,704,1024]{2,1,0:T(8,128)} fusion(bf16[2,1024,704]{2,1,0:T(8,128)(2,1)S(1)} %copy-done.113, bf16[1024,1024]{1,0:T(8,128)(2,1)} %get-tuple-element.97), kind=kOutput, calls=%fused_computation.34 | convolution fusion | flops 2952790016 | bytes 10747904 | tf_op jit(solution)/shard_map/jth,td->jhd/dot_general | solution.py:905
  197.4 3.3 fusion.145.refs_6_
  200.7 2.9 collective-permute-done.17.refs_3_
  204.4 3.0 second_norm.3
  209.4 11.6 %collective-permute-done.18.refs_2_ = bf16[256,1024]{1,0:T(8,128)(2,1)} collective-permute-done((bf16[256,1024]{1,0:T(8,128)(2,1)}, bf16[256,1024]{1,0:T(8,128)(2,1)}, u32[]{:S(2)}, u32[]{:S(2)}) %collective-permute-start.18) | collective-permute-done | bytes 524320 | tf_op jit(solution)/shard_map/ppermute | solution.py:890
  224.4 2.2 pass_on.10.refs_11_
  228.0 20.3 %ffn_pass.3 = (bf16[1024,704]{1,0:T(8,128)(2,1)}, bf16[2,1024,704]{2,1,0:T(8,128)(2,1)}, bf16[2,256,1024]{2,1,0:T(8,128)(2,1)}, bf16[2,256,1024]{2,1,0:T(8,128)(...) custom-call(bf16[256,1024]{1,0:T(8,128)(2,1)} %get-tuple-element.100, ...), custom_call_target="tpu_custom_call" | custom-call | flops 12000000000 | bytes 36000000 | tf_op jit(solution)/shard_map/ffn_pass/pallas_call | solution.py:604
  249.4 3.8 norm_back.2
  254.9 10.1 %add_add_fusion.refs_2_.refs_3_ = f32[2,704,1024]{2,1,0:T(8,128)} fusion(f32[2,704,1024]{2,1,0:T(8,128)} %fusion.25.refs_5_, bf16[2,1024,704]{2,1,0:T(8,128)(2,1)} %get-tuple-element.107, bf16[1024,1024]{1,0:T(8,128)(2,1)} %get-tuple-element.108, f32[1,2,1024,704]{2,3,1,0:T(8,128)S(1)} %bitcast.265), kind=kOutput, calls=%fused_computation | convolution fusion | flops 2955673600 | bytes 22282240 | tf_op jit(solution)/shard_map/jth,td->jhd/dot_general | solution.py:905
  265.0 3.4 bitcast_add_fusion.3.refs_3_.refs_4_
  273.3 2.1 pass_on.11.refs_11_
  277.0 5.3 fusion.33.refs_4_
  282.3 25.1 %mixer_backward.4 = (bf16[4,128,1024]{2,1,0:T(8,128)(2,1)}, f32[1,1,1024]{2,1,0:T(1,128)}, f32[3,128,4]{2,1,0:T(8,128)}, f32[1,1,128]{2,1,0:T(1,128)}, f32[8,4096]{1,0:T(8,128)}) custom-call(f32[4,256,1024]{2,1,0:T(8,128)} %fusion.29.refs_0_, f32[2,1,1024]{2,1,0:T(1,128)} %broadcast_in_dim.36.refs_1_, f32[3,256,4]{2,1,0:T(8,128)} %bitcast.272, ...), custom_call_target="tpu_custom_call" | custom-call | flops 28000000000 | bytes 84000000 | tf_op jit(solution)/shard_map/mixer_backward/pallas_call | solution.py:565
  310.6 2.1 pass_on.12
  313.4 3.8 norm_back.3
  318.6 25.3 %mixer_backward.5 = (bf16[4,128,1024]{2,1,0:T(8,128)(2,1)}, f32[1,1,1024]{2,1,0:T(1,128)}, f32[3,128,4]{2,1,0:T(8,128)}, f32[1,1,128]{2,1,0:T(1,128)}, f32[8,4096]{1,0:T(8,128)}) custom-call(f32[4,256,1024]{2,1,0:T(8,128)} %fusion.29.refs_0_, f32[2,1,1024]{2,1,0:T(1,128)} %broadcast_in_dim.36.refs_1_, f32[3,256,4]{2,1,0:T(8,128)} %bitcast.273, ...), custom_call_target="tpu_custom_call" | custom-call | flops 28000000000 | bytes 84000000 | tf_op jit(solution)/shard_map/mixer_backward/pallas_call | solution.py:565
  345.5 3.9 fusion.50
  349.4 2.4 fusion.57
  354.7 5.9 %convolution_bitcast_fusion.refs_11_ = f32[4,1024,256]{2,1,0:T(8,128)} fusion(bf16[4,256,1024]{2,1,0:T(8,128)(2,1)S(1)} %fusion.50, bf16[256,1024]{1,0:T(8,128)(2,1)S(1)} %copy-done.94, bf16[256,1024]{1,0:T(8,128)(2,1)} %collective-permute-done.1, bf16[256,1024]{1,0:T(8,128)(2,1)} %collective-permute-done, bf16[256,1024]{1,0:T(8,128)(2,1)} %get-tuple-element.287), kind=kOutput, calls=%fused_computation.22 | convolution fusion | flops 2155872256 | bytes 8388608 | tf_op jit(solution)/shard_map/id,kci->kdc/dot_general | solution.py:905
  361.4 8.4 %frames_and_basis.2 = (f32[8,2752]{1,0:T(8,128)}, f32[8,2432]{1,0:T(8,128)}) custom-call(f32[8,2752]{1,0:T(8,128)} %add_after.10.refs_10_.refs_0_, f32[8,2752]{1,0:T(8,128)} %copy-done.55, f32[2,704,1024]{2,1,0:T(8,128)} %add_add_fusion.refs_2_.refs_3_, f32[1,704,1024]{2,1,0:T(8,128)} %bitcast_add_fusion.3.refs_3_.refs_4_, ...), custom_call_target="tpu_custom_call" | custom-call | flops 1000000000 | bytes 3000000 | tf_op jit(solution)/shard_map/frames_and_basis/pallas_call | solution.py:604
  371.3 2.1 pass_on.13
  375.6 2.1 pass_on.15
  381.8 2.3 sketches.5
  385.4 4.9 fusion.31.refs_4_
  390.3 25.1 %mixer_backward.6 = (bf16[4,128,1024]{2,1,0:T(8,128)(2,1)}, f32[1,1,1024]{2,1,0:T(1,128)}, f32[3,128,4]{2,1,0:T(8,128)}, f32[1,1,128]{2,1,0:T(1,128)}, f32[8,4352]{1,0:T(8,128)}) custom-call(f32[4,256,1024]{2,1,0:T(8,128)} %fusion.27.refs_2_.refs_0_, f32[2,1,1024]{2,1,0:T(1,128)} %broadcast_in_dim.37.refs_1_, f32[3,256,4]{2,1,0:T(8,128)} %bitcast.274, ...), custom_call_target="tpu_custom_call" | custom-call | flops 28000000000 | bytes 84000000 | tf_op jit(solution)/shard_map/mixer_backward/pallas_call | solution.py:565
  417.6 24.9 %mixer_backward.7 = (bf16[4,128,1024]{2,1,0:T(8,128)(2,1)}, f32[1,1,1024]{2,1,0:T(1,128)}, f32[3,128,4]{2,1,0:T(8,128)}, f32[1,1,128]{2,1,0:T(1,128)}, f32[8,4352]{1,0:T(8,128)}) custom-call(f32[4,256,1024]{2,1,0:T(8,128)} %fusion.27.refs_2_.refs_0_, f32[2,1,1024]{2,1,0:T(1,128)} %broadcast_in_dim.37.refs_1_, f32[3,256,4]{2,1,0:T(8,128)} %bitcast.275, ...), custom_call_target="tpu_custom_call" | custom-call | flops 28000000000 | bytes 84000000 | tf_op jit(solution)/shard_map/mixer_backward/pallas_call | solution.py:565
  444.7 2.8 fusion.147
  447.5 3.8 fusion.45.refs_2_.refs_0_
  451.3 2.0 fusion.134
  457.7 10.6 %multiply_reduce_fusion = (f32[1024]{0:T(1024)S(1)}, f32[4,1024,256]{2,1,0:T(8,128)}) fusion(bf16[5,1024,256]{2,1,0:T(8,128)(2,1)} %all-gather.3.cloned.1.call-done, f32[1,4,1024,256]{3,2,1,0:T(8,128)} %param.50, f32[4,1024,256]{2,1,0:T(8,128)} %convolution_bitcast_fusion.refs_11_, bf16[4,256,1024]{2,1,0:T(8,128)(2,1)} %gate.6.refs_0_, ...), kind=kOutput, calls=%fused_computation.6 | convolution fusion | flops 2161114112 | bytes 18878464 | tf_op jit(solution)/shard_map/id,kci->kdc/dot_general | solution.py:905
  473.2 2.6 collective-permute-done.48
  482.3 5.8 %fusion = bf16[1024,1024]{1,0:T(8,128)(2,1)S(1)} fusion(f32[1024,1024]{1,0:T(8,128)} %fusion.147, bf16[4,256,1024]{2,1,0:T(8,128)(2,1)} %gate.7, bf16[5,1024,256]{2,1,0:T(8,128)(2,1)} %all-gather.3.cloned.1.call-done), kind=kOutput, calls=%fused_computation.2 | convolution fusion | flops 2149580800 | bytes 10485760 | tf_op jit(solution)/shard_map/kci,kdc->id/dot_general | solution.py:905
  491.4 5.8 %frames_and_basis.3 = (f32[8,4352]{1,0:T(8,128)}, f32[8,2048]{1,0:T(8,128)}) custom-call(f32[8,4352]{1,0:T(8,128)} %add_after.13.refs_1_.refs_0_, f32[8,4352]{1,0:T(8,128)} %copy-done.49, f32[4,1024,256]{2,1,0:T(8,128)} %get-tuple-element.273.refs_2_.refs_3_, f32[1,256,1024]{2,1,0:T(8,128)} %fusion.61.refs_0_.refs_3_.refs_4_, bf16[2,2,256,1024]{3,2,1,0:T(8,128)(2,1)} %bitcast.262), custom_call_target="tpu_custom_call" | custom-call | flops 1000000000 | bytes 3000000 | tf_op jit(solution)/shard_map/frames_and_basis/pallas_call | solution.py:604
  501.5 3.9 add_rows.1.refs_7_
  510.8 8.0 %basis_and_errors.3 = (f32[8,2432]{1,0:T(8,128)}, f32[2,704,1024]{2,1,0:T(8,128)}, f32[1,704,1024]{2,1,0:T(8,128)}) custom-call(f32[8,2752]{1,0:T(8,128)} %get-tuple-element.149.refs_0_, f32[8,2432]{1,0:T(8,128)} %add_after.17.refs_1_, f32[8,2432]{1,0:T(8,128)} %copy-done.56, f32[2,704,1024]{2,1,0:T(8,128)} %add_add_fusion.refs_2_.refs_3_, ...), custom_call_target="tpu_custom_call" | custom-call | flops 1000000000 | bytes 3000000 | tf_op jit(solution)/shard_map/basis_and_errors/pallas_call | solution.py:604
  524.7 2.3 fusion.144
  532.9 3.6 norm_back_into.2.refs_0_.refs_6_
  542.2 2.1 pass_on.14.refs_5_
  545.0 5.7 basis_and_errors.2
  561.7 3.2 collective-permute-done.44.across_ref
  565.8 3.4 norm_back_into.3
  (462 shorter events, 129.5 us)
Async XLA Ops:
  7.2 61.0 %all-gather.3.cloned.1.call-start = ((), (), s32[]{:S(2)}) async-start(), calls=%async_computation | async-start | bytes 2949120 | tf_op jit(solution)/shard_map/all_gather | solution.py:948
  10.2 156.3 %all-gather.5.cloned.1.call-start = ((), (), s32[]{:S(2)}) async-start(), calls=%async_computation.1 | async-start | bytes 5308416 | tf_op jit(solution)/shard_map/all_gather | solution.py:951
  12.5 17.2 %collective-permute-start.1 = (bf16[256,1024]{1,0:T(8,128)(2,1)}, bf16[256,1024]{1,0:T(8,128)(2,1)}, u32[]{:S(2)}, u32[]{:S(2)}) collective-permute-start(bf16[256,1024]{1,0:T(8,128)(2,1)} %get-tuple-element.287), channel_id=1, source_target_pairs={{0,2},{1,3},{2,0},{3,1},{4,6},{5,7},{6,4},{7,5},{8,10},{9,11},{10,... | collective-permute-start | bytes 1572872 | tf_op jit(solution)/shard_map/ppermute | solution.py:890
  15.4 23.5 %collective-permute-start = (bf16[256,1024]{1,0:T(8,128)(2,1)}, bf16[256,1024]{1,0:T(8,128)(2,1)}, u32[]{:S(2)}, u32[]{:S(2)}) collective-permute-start(bf16[256,1024]{1,0:T(8,128)(2,1)} %get-tuple-element.287), channel_id=1, source_target_pairs={{0,1},{1,0},{2,3},{3,2},{4,5},{5,4},{6,7},{7,6},{8,9},{9,8},{10,11... | collective-permute-start | bytes 1572872 | tf_op jit(solution)/shard_map/ppermute | solution.py:890
  15.4 23.5 %collective-permute-start.5 = (bf16[256,1024]{1,0:T(8,128)(2,1)}, bf16[256,1024]{1,0:T(8,128)(2,1)}, u32[]{:S(2)}, u32[]{:S(2)}) collective-permute-start(bf16[256,1024]{1,0:T(8,128)(2,1)} %get-tuple-element.286), channel_id=1, source_target_pairs={{0,2},{1,3},{2,0},{3,1},{4,6},{5,7},{6,4},{7,5},{8,10},{9,11},{10,... | collective-permute-start | bytes 1572872 | tf_op jit(solution)/shard_map/ppermute | solution.py:890
  15.5 85.2 %collective-permute-start.4 = (bf16[256,1024]{1,0:T(8,128)(2,1)}, bf16[256,1024]{1,0:T(8,128)(2,1)}, u32[]{:S(2)}, u32[]{:S(2)}) collective-permute-start(bf16[256,1024]{1,0:T(8,128)(2,1)} %get-tuple-element.286), channel_id=1, source_target_pairs={{0,1},{1,0},{2,3},{3,2},{4,5},{5,4},{6,7},{7,6},{8,9},{9,8},{10,11... | collective-permute-start | bytes 1572872 | tf_op jit(solution)/shard_map/ppermute | solution.py:890
  17.4 87.3 %copy-start.52 = (bf16[1024,2]{0,1:T(2,128)(2,1)}, bf16[1024,2]{0,1:T(2,128)(2,1)S(1)}, u32[]{:S(2)}) copy-start(bf16[1024,2]{0,1:T(2,128)(2,1)S(1)} %convert_element_type.98) | copy-start | bytes 12292
  29.1 130.0 %copy-start.82 = (s32[1024]{0:T(1024)}, s32[1024]{0:T(1024)S(1)}, u32[]{:S(2)}) copy-start(s32[1024]{0:T(1024)S(1)} %fusion.93) | copy-start | bytes 12292
  29.7 9.2 %collective-permute-start.2 = (bf16[256,1024]{1,0:T(8,128)(2,1)}, bf16[256,1024]{1,0:T(8,128)(2,1)S(1)}, u32[]{:S(2)}, u32[]{:S(2)}) collective-permute-start(bf16[256,1024]{1,0:T(8,128)(2,1)} %collective-permute-done.1), channel_id=1, source_target_pairs={{0,1},{1,0},{2,3},{3,2},{4,5},{5,4},{6,7},{7,6},{8,9},{9,8},{10,11... | collective-permute-start | bytes 1572872 | tf_op jit(solution)/shard_map/ppermute | solution.py:890
  38.9 61.9 %collective-permute-start.6 = (bf16[256,1024]{1,0:T(8,128)(2,1)}, bf16[256,1024]{1,0:T(8,128)(2,1)}, u32[]{:S(2)}, u32[]{:S(2)}) collective-permute-start(bf16[256,1024]{1,0:T(8,128)(2,1)} %collective-permute-done.5), channel_id=1, source_target_pairs={{0,1},{1,0},{2,3},{3,2},{4,5},{5,4},{6,7},{7,6},{8,9},{9,8},{10,11... | collective-permute-start | bytes 1572872 | tf_op jit(solution)/shard_map/ppermute | solution.py:890
  100.8 21.5 %collective-permute-start.3 = (bf16[2,256,1024]{2,1,0:T(8,128)(2,1)}, bf16[2,256,1024]{2,1,0:T(8,128)(2,1)S(1)}, u32[]{:S(2)}, u32[]{:S(2)}) collective-permute-start(bf16[2,256,1024]{2,1,0:T(8,128)(2,1)} %get-tuple-element.284), channel_id=1, source_target_pairs={{0,1},{1,0},{2,3},{3,2},{4,5},{5,4},{6,7},{7,6},{8,9},{9,8},{10,11... | collective-permute-start | bytes 3145736 | tf_op jit(solution)/shard_map/ppermute | solution.py:890
  107.3 15.0 %collective-permute-start.12 = (bf16[256,1024]{1,0:T(8,128)(2,1)}, bf16[256,1024]{1,0:T(8,128)(2,1)}, u32[]{:S(2)}, u32[]{:S(2)}) collective-permute-start(bf16[256,1024]{1,0:T(8,128)(2,1)} %gate.4.refs_4_), channel_id=1, source_target_pairs={{0,2},{1,3},{2,0},{3,1},{4,6},{5,7},{6,4},{7,5},{8,10},{9,11},{10,... | collective-permute-start | bytes 1572872 | tf_op jit(solution)/shard_map/ppermute | solution.py:890
  108.7 56.7 %collective-permute-start.11 = (bf16[256,1024]{1,0:T(8,128)(2,1)}, bf16[256,1024]{1,0:T(8,128)(2,1)}, u32[]{:S(2)}, u32[]{:S(2)}) collective-permute-start(bf16[256,1024]{1,0:T(8,128)(2,1)} %gate.4.refs_4_), channel_id=1, source_target_pairs={{0,1},{1,0},{2,3},{3,2},{4,5},{5,4},{6,7},{7,6},{8,9},{9,8},{10,11... | collective-permute-start | bytes 1572872 | tf_op jit(solution)/shard_map/ppermute | solution.py:890
  109.0 99.9 %collective-permute-start.23 = (bf16[256,1024]{1,0:T(8,128)(2,1)}, bf16[256,1024]{1,0:T(8,128)(2,1)}, u32[]{:S(2)}, u32[]{:S(2)}) collective-permute-start(bf16[256,1024]{1,0:T(8,128)(2,1)} %gate.5.refs_4_), channel_id=1, source_target_pairs={{0,2},{1,3},{2,0},{3,1},{4,6},{5,7},{6,4},{7,5},{8,10},{9,11},{10,... | collective-permute-start | bytes 1572872 | tf_op jit(solution)/shard_map/ppermute | solution.py:890
  122.3 43.5 %collective-permute-start.13 = (bf16[256,1024]{1,0:T(8,128)(2,1)}, bf16[256,1024]{1,0:T(8,128)(2,1)}, u32[]{:S(2)}, u32[]{:S(2)}) collective-permute-start(bf16[256,1024]{1,0:T(8,128)(2,1)} %collective-permute-done.12.refs_6_), channel_id=1, source_target_pairs={{0,1},{1,0},{2,3},{3,2},{4,5},{5,4},{6,7},{7,6},{8,9},{9,8},{10,11... | collective-permute-start | bytes 1572872 | tf_op jit(solution)/shard_map/ppermute | solution.py:890
  125.4 18.9 %collective-permute-start.7 = (bf16[256,1024]{1,0:T(8,128)(2,1)}, bf16[256,1024]{1,0:T(8,128)(2,1)S(1)}, u32[]{:S(2)}, u32[]{:S(2)}) collective-permute-start(bf16[256,1024]{1,0:T(8,128)(2,1)} %pass_on.8.refs_6_), channel_id=1, source_target_pairs={{0,2},{1,3},{2,0},{3,1},{4,6},{5,7},{6,4},{7,5},{8,10},{9,11},{10,... | collective-permute-start | bytes 1572872 | tf_op jit(solution)/shard_map/ppermute | solution.py:890
  148.1 13.9 %collective-permute-start.9 = (bf16[256,1024]{1,0:T(8,128)(2,1)}, bf16[256,1024]{1,0:T(8,128)(2,1)S(1)}, u32[]{:S(2)}, u32[]{:S(2)}) collective-permute-start(bf16[256,1024]{1,0:T(8,128)(2,1)} %get-tuple-element.91.refs_6_.refs_0_), channel_id=1, source_target_pairs={{0,2},{1,3},{2,0},{3,1},{4,6},{5,7},{6,4},{7,5},{8,10},{9,11},{10,... | collective-permute-start | bytes 1572872 | tf_op jit(solution)/shard_map/ppermute | solution.py:890
  159.1 6.7 %collective-permute-start.8 = (bf16[256,1024]{1,0:T(8,128)(2,1)S(1)}, bf16[256,1024]{1,0:T(8,128)(2,1)S(1)}, u32[]{:S(2)}, u32[]{:S(2)}) collective-permute-start(bf16[256,1024]{1,0:T(8,128)(2,1)S(1)} %copy-done.96), channel_id=1, source_target_pairs={{0,1},{1,0},{2,3},{3,2},{4,5},{5,4},{6,7},{7,6},{8,9},{9,8},{10,11... | collective-permute-start | bytes 1572872 | tf_op jit(solution)/shard_map/ppermute | solution.py:890
  161.9 4.6 collective-permute-start.10
  165.4 21.5 %collective-permute-start.16 = (bf16[2,256,1024]{2,1,0:T(8,128)(2,1)}, bf16[2,256,1024]{2,1,0:T(8,128)(2,1)}, u32[]{:S(2)}, u32[]{:S(2)}) collective-permute-start(bf16[2,256,1024]{2,1,0:T(8,128)(2,1)} %get-tuple-element.283.refs_11_), channel_id=1, source_target_pairs={{0,1},{1,0},{2,3},{3,2},{4,5},{5,4},{6,7},{7,6},{8,9},{9,8},{10,11... | collective-permute-start | bytes 3145736 | tf_op jit(solution)/shard_map/ppermute | solution.py:890
  186.7 37.2 %collective-permute-start.15 = (bf16[2,256,1024]{2,1,0:T(8,128)(2,1)}, bf16[2,256,1024]{2,1,0:T(8,128)(2,1)}, u32[]{:S(2)}, u32[]{:S(2)}) collective-permute-start(bf16[2,256,1024]{2,1,0:T(8,128)(2,1)} %get-tuple-element.95.refs_2_), channel_id=1, source_target_pairs={{0,1},{1,0},{2,3},{3,2},{4,5},{5,4},{6,7},{7,6},{8,9},{9,8},{10,11... | collective-permute-start | bytes 3145736 | tf_op jit(solution)/shard_map/ppermute | solution.py:890
  189.2 14.4 %collective-permute-start.17 = (bf16[256,1024]{1,0:T(8,128)(2,1)}, bf16[256,1024]{1,0:T(8,128)(2,1)S(1)}, u32[]{:S(2)}, u32[]{:S(2)}) collective-permute-start(bf16[256,1024]{1,0:T(8,128)(2,1)} %pass_on.9), channel_id=1, source_target_pairs={{0,2},{1,3},{2,0},{3,1},{4,6},{5,7},{6,4},{7,5},{8,10},{9,11},{10,... | collective-permute-start | bytes 1572872 | tf_op jit(solution)/shard_map/ppermute | solution.py:890
  207.4 13.7 %collective-permute-start.18 = (bf16[256,1024]{1,0:T(8,128)(2,1)}, bf16[256,1024]{1,0:T(8,128)(2,1)}, u32[]{:S(2)}, u32[]{:S(2)}) collective-permute-start(bf16[256,1024]{1,0:T(8,128)(2,1)} %get-tuple-element.100.refs_0_), channel_id=1, source_target_pairs={{0,2},{1,3},{2,0},{3,1},{4,6},{5,7},{6,4},{7,5},{8,10},{9,11},{10,... | collective-permute-start | bytes 1572872 | tf_op jit(solution)/shard_map/ppermute | solution.py:890
  208.9 17.7 %collective-permute-start.22 = (bf16[256,1024]{1,0:T(8,128)(2,1)S(1)}, bf16[256,1024]{1,0:T(8,128)(2,1)}, u32[]{:S(2)}, u32[]{:S(2)}) collective-permute-start(bf16[256,1024]{1,0:T(8,128)(2,1)S(1)} %copy-done.14), channel_id=1, source_target_pairs={{0,1},{1,0},{2,3},{3,2},{4,5},{5,4},{6,7},{7,6},{8,9},{9,8},{10,11... | collective-permute-start | bytes 1572872 | tf_op jit(solution)/shard_map/ppermute | solution.py:890
  208.9 19.1 %collective-permute-start.24 = (bf16[256,1024]{1,0:T(8,128)(2,1)}, bf16[256,1024]{1,0:T(8,128)(2,1)}, u32[]{:S(2)}, u32[]{:S(2)}) collective-permute-start(bf16[256,1024]{1,0:T(8,128)(2,1)} %collective-permute-done.23.refs_6_), channel_id=1, source_target_pairs={{0,1},{1,0},{2,3},{3,2},{4,5},{5,4},{6,7},{7,6},{8,9},{9,8},{10,11... | collective-permute-start | bytes 1572872 | tf_op jit(solution)/shard_map/ppermute | solution.py:890
  209.4 18.6 %collective-permute-start.20 = (bf16[256,1024]{1,0:T(8,128)(2,1)}, bf16[256,1024]{1,0:T(8,128)(2,1)}, u32[]{:S(2)}, u32[]{:S(2)}) collective-permute-start(bf16[256,1024]{1,0:T(8,128)(2,1)} %get-tuple-element.100.refs_0_), channel_id=1, source_target_pairs={{0,1},{1,0},{2,3},{3,2},{4,5},{5,4},{6,7},{7,6},{8,9},{9,8},{10,11... | collective-permute-start | bytes 1572872 | tf_op jit(solution)/shard_map/ppermute | solution.py:890
  221.1 6.9 %collective-permute-start.21 = (bf16[256,1024]{1,0:T(8,128)(2,1)}, bf16[256,1024]{1,0:T(8,128)(2,1)}, u32[]{:S(2)}, u32[]{:S(2)}) collective-permute-start(bf16[256,1024]{1,0:T(8,128)(2,1)} %collective-permute-done.18.refs_2_), channel_id=1, source_target_pairs={{0,1},{1,0},{2,3},{3,2},{4,5},{5,4},{6,7},{7,6},{8,9},{9,8},{10,11... | collective-permute-start | bytes 1572872 | tf_op jit(solution)/shard_map/ppermute | solution.py:890
  222.4 32.4 %slice-start = ((s8[5767168]{0:T(1024)(128)(4,1)}), s8[4194304]{0:T(1024)(128)(4,1)S(1)}, s32[]{:S(2)}) async-start(s8[5767168]{0:T(1024)(128)(4,1)} %bitcast.264), calls=%async_computation.2 | async-start | bytes 8388608
  223.8 86.8 %collective-permute-start.14 = (bf16[2,256,1024]{2,1,0:T(8,128)(2,1)}, bf16[2,256,1024]{2,1,0:T(8,128)(2,1)}, u32[]{:S(2)}, u32[]{:S(2)}) collective-permute-start(bf16[2,256,1024]{2,1,0:T(8,128)(2,1)} %get-tuple-element.93), channel_id=1, source_target_pairs={{0,1},{1,0},{2,3},{3,2},{4,5},{5,4},{6,7},{7,6},{8,9},{9,8},{10,11... | collective-permute-start | bytes 3145736 | tf_op jit(solution)/shard_map/ppermute | solution.py:890
  226.5 28.3 %slice-start.1 = ((s8[5767168]{0:T(1024)(128)(4,1)}), s8[1572864]{0:T(1024)(128)(4,1)S(1)}, s32[]{:S(2)}) async-start(s8[5767168]{0:T(1024)(128)(4,1)} %bitcast.264), calls=%async_computation.3 | async-start | bytes 3145728
  226.5 22.0 %collective-permute-start.19 = (bf16[256,1024]{1,0:T(8,128)(2,1)}, bf16[256,1024]{1,0:T(8,128)(2,1)S(1)}, u32[]{:S(2)}, u32[]{:S(2)}) collective-permute-start(bf16[256,1024]{1,0:T(8,128)(2,1)} %pass_on.10.refs_11_), channel_id=1, source_target_pairs={{0,2},{1,3},{2,0},{3,1},{4,6},{5,7},{6,4},{7,5},{8,10},{9,11},{10,... | collective-permute-start | bytes 1572872 | tf_op jit(solution)/shard_map/ppermute | solution.py:890
  248.3 25.0 %collective-permute-start.29 = (bf16[2,256,1024]{2,1,0:T(8,128)(2,1)}, bf16[2,256,1024]{2,1,0:T(8,128)(2,1)}, u32[]{:S(2)}, u32[]{:S(2)}) collective-permute-start(bf16[2,256,1024]{2,1,0:T(8,128)(2,1)} %get-tuple-element.101.refs_6_), channel_id=1, source_target_pairs={{0,1},{1,0},{2,3},{3,2},{4,5},{5,4},{6,7},{7,6},{8,9},{9,8},{10,11... | collective-permute-start | bytes 3145736 | tf_op jit(solution)/shard_map/ppermute | solution.py:890
  253.2 17.5 %collective-permute-start.25 = (bf16[256,1024]{1,0:T(8,128)(2,1)}, bf16[256,1024]{1,0:T(8,128)(2,1)}, u32[]{:S(2)}, u32[]{:S(2)}) collective-permute-start(bf16[256,1024]{1,0:T(8,128)(2,1)} %get-tuple-element.102.refs_2_), channel_id=1, source_target_pairs={{0,1},{1,0},{2,3},{3,2},{4,5},{5,4},{6,7},{7,6},{8,9},{9,8},{10,11... | collective-permute-start | bytes 1572872 | tf_op jit(solution)/shard_map/ppermute | solution.py:890
  253.5 14.9 %collective-permute-start.26 = (bf16[256,1024]{1,0:T(8,128)(2,1)}, bf16[256,1024]{1,0:T(8,128)(2,1)S(1)}, u32[]{:S(2)}, u32[]{:S(2)}) collective-permute-start(bf16[256,1024]{1,0:T(8,128)(2,1)} %get-tuple-element.102.refs_2_), channel_id=1, source_target_pairs={{0,2},{1,3},{2,0},{3,1},{4,6},{5,7},{6,4},{7,5},{8,10},{9,11},{10,... | collective-permute-start | bytes 1572872 | tf_op jit(solution)/shard_map/ppermute | solution.py:890
  254.2 14.3 %collective-permute-start.28 = (f32[8,2752]{1,0:T(8,128)S(1)}, f32[8,2752]{1,0:T(8,128)S(1)}, u32[]{:S(2)}, u32[]{:S(2)}) collective-permute-start(f32[8,2752]{1,0:T(8,128)S(1)} %maximum_add_fusion.2.refs_0_), channel_id=1, source_target_pairs={{0,4},{4,0},{8,12},{12,8},{16,20},{20,16},{24,28},{28,24},{1,5},{5... | collective-permute-start | bytes 264200 | tf_op jit(solution)/shard_map/ppermute | solution.py:890
  268.4 8.5 %collective-permute-start.27 = (bf16[256,1024]{1,0:T(8,128)(2,1)S(1)}, bf16[256,1024]{1,0:T(8,128)(2,1)S(1)}, u32[]{:S(2)}, u32[]{:S(2)}) collective-permute-start(bf16[256,1024]{1,0:T(8,128)(2,1)S(1)} %collective-permute-done.26), channel_id=1, source_target_pairs={{0,1},{1,0},{2,3},{3,2},{4,5},{5,4},{6,7},{7,6},{8,9},{9,8},{10,11... | collective-permute-start | bytes 1572872 | tf_op jit(solution)/shard_map/ppermute | solution.py:890
  268.5 101.3 %collective-permute-start.31 = (bf16[2,256,1024]{2,1,0:T(8,128)(2,1)}, bf16[2,256,1024]{2,1,0:T(8,128)(2,1)}, u32[]{:S(2)}, u32[]{:S(2)}) collective-permute-start(bf16[2,256,1024]{2,1,0:T(8,128)(2,1)} %get-tuple-element.115), channel_id=1, source_target_pairs={{0,1},{1,0},{2,3},{3,2},{4,5},{5,4},{6,7},{7,6},{8,9},{9,8},{10,11... | collective-permute-start | bytes 3145736 | tf_op jit(solution)/shard_map/ppermute | solution.py:890
  270.7 36.6 %collective-permute-start.32 = (f32[8,2752]{1,0:T(8,128)}, f32[8,2752]{1,0:T(8,128)S(1)}, u32[]{:S(2)}, u32[]{:S(2)}) collective-permute-start(f32[8,2752]{1,0:T(8,128)} %add_after.9.refs_10_.refs_0_), channel_id=1, source_target_pairs={{0,8},{4,12},{8,0},{12,4},{16,24},{20,28},{24,16},{28,20},{1,9},{5... | collective-permute-start | bytes 264200 | tf_op jit(solution)/shard_map/ppermute | solution.py:890
  275.4 37.9 %collective-permute-start.33 = (bf16[256,1024]{1,0:T(8,128)(2,1)}, bf16[256,1024]{1,0:T(8,128)(2,1)}, u32[]{:S(2)}, u32[]{:S(2)}) collective-permute-start(bf16[256,1024]{1,0:T(8,128)(2,1)} %pass_on.11.refs_11_), channel_id=1, source_target_pairs={{0,2},{1,3},{2,0},{3,1},{4,6},{5,7},{6,4},{7,5},{8,10},{9,11},{10,... | collective-permute-start | bytes 1572872 | tf_op jit(solution)/shard_map/ppermute | solution.py:890
  309.6 51.2 %collective-permute-start.38 = (f32[8,2752]{1,0:T(8,128)}, f32[8,2752]{1,0:T(8,128)S(1)}, u32[]{:S(2)}, u32[]{:S(2)}) collective-permute-start(f32[8,2752]{1,0:T(8,128)} %add_after.10.refs_10_.refs_0_), channel_id=1, source_target_pairs={{0,16},{4,20},{8,24},{12,28},{16,0},{20,4},{24,8},{28,12},{1,17},{... | collective-permute-start | bytes 264200 | tf_op jit(solution)/shard_map/ppermute | solution.py:890
  312.8 186.6 %collective-permute-start.30 = (bf16[256,1024]{1,0:T(8,128)(2,1)}, bf16[256,1024]{1,0:T(8,128)(2,1)}, u32[]{:S(2)}, u32[]{:S(2)}) collective-permute-start(bf16[256,1024]{1,0:T(8,128)(2,1)} %pass_on.12), channel_id=1, source_target_pairs={{0,2},{1,3},{2,0},{3,1},{4,6},{5,7},{6,4},{7,5},{8,10},{9,11},{10,... | collective-permute-start | bytes 1572872 | tf_op jit(solution)/shard_map/ppermute | solution.py:890
  317.2 56.5 %collective-permute-start.36 = (bf16[256,1024]{1,0:T(8,128)(2,1)}, bf16[256,1024]{1,0:T(8,128)(2,1)}, u32[]{:S(2)}, u32[]{:S(2)}) collective-permute-start(bf16[256,1024]{1,0:T(8,128)(2,1)} %get-tuple-element.117.refs_11_), channel_id=1, source_target_pairs={{0,2},{1,3},{2,0},{3,1},{4,6},{5,7},{6,4},{7,5},{8,10},{9,11},{10,... | collective-permute-start | bytes 1572872 | tf_op jit(solution)/shard_map/ppermute | solution.py:890
  318.6 26.9 %copy-start.114 = (bf16[4,128,1024]{2,1,0:T(8,128)(2,1)S(1)}, bf16[4,128,1024]{2,1,0:T(8,128)(2,1)}, u32[]{:S(2)}) copy-start(bf16[4,128,1024]{2,1,0:T(8,128)(2,1)} %get-tuple-element.123) | copy-start | bytes 3145732
  354.6 21.0 %collective-permute-start.45 = (bf16[2,256,1024]{2,1,0:T(8,128)(2,1)}, bf16[2,256,1024]{2,1,0:T(8,128)(2,1)}, u32[]{:S(2)}, u32[]{:S(2)}) collective-permute-start(bf16[2,256,1024]{2,1,0:T(8,128)(2,1)} %get-tuple-element.274), channel_id=1, source_target_pairs={{0,1},{1,0},{2,3},{3,2},{4,5},{5,4},{6,7},{7,6},{8,9},{9,8},{10,11... | collective-permute-start | bytes 3145736 | tf_op jit(solution)/shard_map/ppermute | solution.py:890
  360.8 13.1 %collective-permute-start.35 = (bf16[256,1024]{1,0:T(8,128)(2,1)S(1)}, bf16[256,1024]{1,0:T(8,128)(2,1)S(1)}, u32[]{:S(2)}, u32[]{:S(2)}) collective-permute-start(bf16[256,1024]{1,0:T(8,128)(2,1)S(1)} %copy-done.32), channel_id=1, source_target_pairs={{0,1},{1,0},{2,3},{3,2},{4,5},{5,4},{6,7},{7,6},{8,9},{9,8},{10,11... | collective-permute-start | bytes 1572872 | tf_op jit(solution)/shard_map/ppermute | solution.py:890
  369.8 45.6 %collective-permute-start.39 = (f32[8,2432]{1,0:T(8,128)}, f32[8,2432]{1,0:T(8,128)S(1)}, u32[]{:S(2)}, u32[]{:S(2)}) collective-permute-start(f32[8,2432]{1,0:T(8,128)} %get-tuple-element.120.refs_10_.refs_0_), channel_id=1, source_target_pairs={{0,4},{4,0},{8,12},{12,8},{16,20},{20,16},{24,28},{28,24},{1,5},{5... | collective-permute-start | bytes 233480 | tf_op jit(solution)/shard_map/ppermute | solution.py:890
  373.7 5.5 collective-permute-start.37
  373.8 126.2 %collective-permute-start.34 = (bf16[256,1024]{1,0:T(8,128)(2,1)}, bf16[256,1024]{1,0:T(8,128)(2,1)}, u32[]{:S(2)}, u32[]{:S(2)}) collective-permute-start(bf16[256,1024]{1,0:T(8,128)(2,1)} %pass_on.13), channel_id=1, source_target_pairs={{0,2},{1,3},{2,0},{3,1},{4,6},{5,7},{6,4},{7,5},{8,10},{9,11},{10,... | collective-permute-start | bytes 1572872 | tf_op jit(solution)/shard_map/ppermute | solution.py:890
  377.7 154.3 %collective-permute-start.46 = (bf16[256,1024]{1,0:T(8,128)(2,1)}, bf16[256,1024]{1,0:T(8,128)(2,1)S(1)}, u32[]{:S(2)}, u32[]{:S(2)}) collective-permute-start(bf16[256,1024]{1,0:T(8,128)(2,1)} %pass_on.15), channel_id=1, source_target_pairs={{0,2},{1,3},{2,0},{3,1},{4,6},{5,7},{6,4},{7,5},{8,10},{9,11},{10,... | collective-permute-start | bytes 1572872 | tf_op jit(solution)/shard_map/ppermute | solution.py:890
  443.2 12.1 %collective-permute-start.40 = (f32[8,4352]{1,0:T(8,128)}, f32[8,4352]{1,0:T(8,128)S(1)}, u32[]{:S(2)}, u32[]{:S(2)}) collective-permute-start(f32[8,4352]{1,0:T(8,128)} %get-tuple-element.127.refs_0_), channel_id=1, source_target_pairs={{0,4},{4,0},{8,12},{12,8},{16,20},{20,16},{24,28},{28,24},{1,5},{5... | collective-permute-start | bytes 417800 | tf_op jit(solution)/shard_map/ppermute | solution.py:890
  468.4 1.6 collective-permute-start.47
  468.5 9.0 %collective-permute-start.41 = (f32[8,4352]{1,0:T(8,128)S(1)}, f32[8,4352]{1,0:T(8,128)S(1)}, u32[]{:S(2)}, u32[]{:S(2)}) collective-permute-start(f32[8,4352]{1,0:T(8,128)S(1)} %copy-done.25), channel_id=1, source_target_pairs={{0,8},{4,12},{8,0},{12,4},{16,24},{20,28},{24,16},{28,20},{1,9},{5... | collective-permute-start | bytes 417800 | tf_op jit(solution)/shard_map/ppermute | solution.py:890
  471.9 3.9 collective-permute-start.48
  475.8 21.4 %collective-permute-start.54 = (f32[8,2432]{1,0:T(8,128)S(1)}, f32[8,2432]{1,0:T(8,128)S(1)}, u32[]{:S(2)}, u32[]{:S(2)}) collective-permute-start(f32[8,2432]{1,0:T(8,128)S(1)} %copy-done.102), channel_id=1, source_target_pairs={{0,8},{4,12},{8,0},{12,4},{16,24},{20,28},{24,16},{28,20},{1,9},{5... | collective-permute-start | bytes 233480 | tf_op jit(solution)/shard_map/ppermute | solution.py:890
  480.8 9.0 %collective-permute-start.42 = (f32[8,4352]{1,0:T(8,128)S(1)}, f32[8,4352]{1,0:T(8,128)S(1)}, u32[]{:S(2)}, u32[]{:S(2)}) collective-permute-start(f32[8,4352]{1,0:T(8,128)S(1)} %copy-done.20), channel_id=1, source_target_pairs={{0,16},{4,20},{8,24},{12,28},{16,0},{20,4},{24,8},{28,12},{1,17},{... | collective-permute-start | bytes 417800 | tf_op jit(solution)/shard_map/ppermute | solution.py:890
  489.8 15.5 %collective-permute-start.50 = (f32[58,128]{1,0:T(8,128)S(1)}, f32[58,128]{1,0:T(8,128)S(1)}, u32[]{:S(2)}, u32[]{:S(2)}) collective-permute-start(f32[58,128]{1,0:T(8,128)S(1)} %pad_maximum_fusion.6.refs_1_), channel_id=1, source_target_pairs={{0,4},{4,0},{8,12},{12,8},{16,20},{20,16},{24,28},{28,24},{1,5},{5... | collective-permute-start | bytes 89096 | tf_op jit(solution)/shard_map/ppermute | solution.py:890
  497.2 44.1 %collective-permute-start.43 = (bf16[2,256,1024]{2,1,0:T(8,128)(2,1)S(1)}, bf16[2,256,1024]{2,1,0:T(8,128)(2,1)S(1)}, u32[]{:S(2)}, u32[]{:S(2)}) collective-permute-start(bf16[2,256,1024]{2,1,0:T(8,128)(2,1)S(1)} %get-tuple-element.276), channel_id=1, source_target_pairs={{0,1},{1,0},{2,3},{3,2},{4,5},{5,4},{6,7},{7,6},{8,9},{9,8},{10,11... | collective-permute-start | bytes 3145736 | tf_op jit(solution)/shard_map/ppermute | solution.py:890
  499.4 5.9 %collective-permute-start.49 = (f32[8,2048]{1,0:T(8,128)S(1)}, f32[8,2048]{1,0:T(8,128)S(1)}, u32[]{:S(2)}, u32[]{:S(2)}) collective-permute-start(f32[8,2048]{1,0:T(8,128)S(1)} %copy-done.41), channel_id=1, source_target_pairs={{0,4},{4,0},{8,12},{12,8},{16,20},{20,16},{24,28},{28,24},{1,5},{5... | collective-permute-start | bytes 196616 | tf_op jit(solution)/shard_map/ppermute | solution.py:890
  500.1 10.1 %collective-permute-start.55 = (f32[8,2432]{1,0:T(8,128)}, f32[8,2432]{1,0:T(8,128)S(1)}, u32[]{:S(2)}, u32[]{:S(2)}) collective-permute-start(f32[8,2432]{1,0:T(8,128)} %add_after.17.refs_1_), channel_id=1, source_target_pairs={{0,16},{4,20},{8,24},{12,28},{16,0},{20,4},{24,8},{28,12},{1,17},{... | collective-permute-start | bytes 233480 | tf_op jit(solution)/shard_map/ppermute | solution.py:890
  508.1 19.0 %collective-permute-start.51 = (f32[8,2048]{1,0:T(8,128)}, f32[8,2048]{1,0:T(8,128)S(1)}, u32[]{:S(2)}, u32[]{:S(2)}) collective-permute-start(f32[8,2048]{1,0:T(8,128)} %get-tuple-element.143.refs_0_), channel_id=1, source_target_pairs={{0,8},{4,12},{8,0},{12,4},{16,24},{20,28},{24,16},{28,20},{1,9},{5... | collective-permute-start | bytes 196616 | tf_op jit(solution)/shard_map/ppermute | solution.py:890
  509.1 18.0 %collective-permute-start.52 = (f32[58,128]{1,0:T(8,128)}, f32[58,128]{1,0:T(8,128)S(1)}, u32[]{:S(2)}, u32[]{:S(2)}) collective-permute-start(f32[58,128]{1,0:T(8,128)} %get-tuple-element.144.refs_1_), channel_id=1, source_target_pairs={{0,8},{4,12},{8,0},{12,4},{16,24},{20,28},{24,16},{28,20},{1,9},{5... | collective-permute-start | bytes 89096 | tf_op jit(solution)/shard_map/ppermute | solution.py:890
  529.9 8.1 %collective-permute-start.56 = (f32[58,128]{1,0:T(8,128)}, f32[58,128]{1,0:T(8,128)S(1)}, u32[]{:S(2)}, u32[]{:S(2)}) collective-permute-start(f32[58,128]{1,0:T(8,128)} %get-tuple-element.153), channel_id=1, source_target_pairs={{0,16},{4,20},{8,24},{12,28},{16,0},{20,4},{24,8},{28,12},{1,17},{... | collective-permute-start | bytes 89096 | tf_op jit(solution)/shard_map/ppermute | solution.py:890
  536.6 7.8 %collective-permute-start.53 = (f32[8,2048]{1,0:T(8,128)S(1)}, f32[8,2048]{1,0:T(8,128)S(1)}, u32[]{:S(2)}, u32[]{:S(2)}) collective-permute-start(f32[8,2048]{1,0:T(8,128)S(1)} %copy-done.57), channel_id=1, source_target_pairs={{0,16},{4,20},{8,24},{12,28},{16,0},{20,4},{24,8},{28,12},{1,17},{... | collective-permute-start | bytes 196616 | tf_op jit(solution)/shard_map/ppermute | solution.py:890
  552.8 12.1 %collective-permute-start.44 = (bf16[256,1024]{1,0:T(8,128)(2,1)S(1)}, bf16[256,1024]{1,0:T(8,128)(2,1)S(1)}, u32[]{:S(2)}, u32[]{:S(2)}) collective-permute-start(bf16[256,1024]{1,0:T(8,128)(2,1)S(1)} %copy-done.34), channel_id=1, source_target_pairs={{0,2},{1,3},{2,0},{3,1},{4,6},{5,7},{6,4},{7,5},{8,10},{9,11},{10,... | collective-permute-start | bytes 1572872 | tf_op jit(solution)/shard_map/ppermute | solution.py:890
  (114 other events, 567.8 us)
Sparse Core Ops, SparseCore 0:
  10.8 57.3 all-gather.2
  71.0 78.4 all-gather.4

commit v3 on v2

--- a/solution.py
+++ b/solution.py
@@ -711,12 +711,12 @@
         left_ff[...] = jnp.zeros_like(left_ff)
         left_down[...] = jnp.zeros_like(left_down)
 
-        def step(i, carry):
-            at = pl.ds(pl.multiple_of(i * tile, tile), tile)
+        def step(i):
+            at = slice(i * tile, (i + 1) * tile)
             x, dy = x_s[at, :], dy_s[at, :]
             gate = mm(x, ff_ref[0])
             up = mm(x, ff_ref[1])
-            sig = jax.nn.sigmoid(gate)
+            sig = sigmoid(gate)
             act = gate * sig
             hidden = (act * up).astype(BF)
             d_hidden = mm(dy, ff_ref[2])
@@ -736,9 +736,9 @@
                 left_ff[j] += halves(mm(high_low(inner), x))
             inner = halves(nt(high_low(bdown_ref[...]), dy))
             left_down[...] += halves(mm(high_low(inner), hidden))
-            return carry
-
-        lax.fori_loop(0, 2, step, 0)
+
+        for i in range(2):
+            step(i)
 
     pair = ((2, share, width), BF)
     return call(
@@ -749,6 +749,11 @@
         ],
         deps, cost=12,
     )
+
+
+momentum_decay = 0.5
+step_rate = 1.0
+small_rate = 0.05
 
 
 def add_steps(values, axis):
@@ -839,30 +844,38 @@
     return halves(by(both, high)) + by(both, low)[: few.shape[0]]
 
 
-def basis_and_errors(frame, left, right, groups, count, deps=()):
+def outer_terms(frame, basis, flipped):
+    high_f, high_b = frame.astype(BF).astype(F32), basis.astype(BF).astype(F32)
+    f = jnp.concatenate([high_f, frame - high_f, high_f, jnp.zeros_like(frame)], axis=0)
+    b = jnp.concatenate([high_b, high_b, basis - high_b, jnp.zeros_like(basis)], axis=0)
+    if flipped:
+        f, b = b, f
+    return f.T.astype(BF), b.astype(BF)
+
+
+def basis_and_errors(frame, left, right, groups, count, update, deps=()):
     blocks = each_block(groups)
-
-    def body(frame_ref, left_ref, right_ref, *refs):
-        basis_ref = refs[len(groups)]
-        out_refs = refs[len(groups) + 1 :]
+    total = len(groups)
+
+    def body(frame_ref, left_ref, right_ref, part_ref, weight_ref, moment_ref, *refs):
+        basis_ref, weight_out, moment_out = refs[total : total + 3]
+        out_refs = refs[total + 3 :]
         edge, edge_n = 0, 0
         for k, j, flipped, m, n in blocks:
             basis = (left_ref[:, edge_n : edge_n + n] + right_ref[:, edge_n : edge_n + n]) * (1.0 / count)
             basis_ref[:, edge_n : edge_n + n] = basis
-            frame = frame_ref[:, edge : edge + m]
-            high_f, high_b = frame.astype(BF).astype(F32), basis.astype(BF).astype(F32)
-            f = jnp.concatenate([high_f, frame - high_f, high_f, jnp.zeros_like(frame)], axis=0)
-            b = jnp.concatenate([high_b, high_b, basis - high_b, jnp.zeros_like(basis)], axis=0)
-            if flipped:
-                f, b = b, f
-            out_refs[k][j] = refs[k][j] - mm(f.T.astype(BF), b.astype(BF))
+            f, b = outer_terms(frame_ref[:, edge : edge + m], basis, flipped)
+            out_refs[k][j] = refs[k][j] - mm(f, b)
+            if k == 0:
+                f, b = outer_terms(part_ref[j], basis, flipped)
+                moment = momentum_decay * moment_ref[j] + mm(f, b)
+                moment_out[j] = moment
+                weight_out[j] = weight_ref[j] - step_rate * moment
             edge, edge_n = edge + m, edge_n + n
 
     arrays = [a for a, f in groups]
-    return call(
-        body, "basis_and_errors", [frame, left, right, *arrays],
-        [(left.shape, F32)] + [(a.shape, F32) for a in arrays], deps,
-    )
+    shapes = [(a.shape, F32) for a in (left, update[1], update[2], *arrays)]
+    return call(body, "basis_and_errors", [frame, left, right, *update, *arrays], shapes, deps)
 
 
 def sketches(groups, bases, deps=()):
@@ -878,11 +891,6 @@
     return call(
         body, "sketches", [a for a, f in groups] + bases, [((rank, sum(b[3] for b in blocks)), F32)], deps
     )[0]
-
-
-momentum_decay = 0.5
-step_rate = 1.0
-small_rate = 0.05
 
 
 def swap(value, axis, flip):
@@ -972,7 +980,6 @@
     resid, group_two, passed_mix, send_two, keep_mix, beside_mix = [], [], [], [], [], []
 
     def project(m):
-        packed.append(dot32("ji,id->jd", place[m], group_one[m]).astype(BF))
         proj.append(dot32("jdc,td->jct", weights_in, packed[m]))
         pre_decay.append(dot32("dh,td->ht", decay_low, packed[m])[:, None, :])
 
@@ -1000,10 +1007,11 @@
     err_ff_t = jnp.swapaxes(err_ff[0], 1, 2)
     err_left = sketches([(err_ff_t, True), (err_down, False)], [bases[2], bases[3]])
     left_in = sketches([(err_in[0], False)], [bases[0]])
+    for m in micros:
+        packed.append(dot32("ji,id->jd", place[m], group_one[m]).astype(BF))
+        pieces_dy.append(gather_rows(gate(cotangent[m].astype(BF), (pieces_one[last][2],))))
     project(0)
-    gated = [forward(0, h, (err_left, left_in)) for h in heads]
-    for m in micros:
-        pieces_dy.append(gather_rows(gate(cotangent[m].astype(BF), (gated[min(m, 1)],))))
+    gated = [forward(0, h, (err_left, left_in, packed[last])) for h in heads]
     sent = mix_out(0, gated)
     project(1)
     pass_mix(0, (proj[1],))
@@ -1064,11 +1072,18 @@
     left_ff = sum(left_ff)
     early = jnp.concatenate([left_ff[0], left_ff[1], sum(left_down)], axis=1) + err_left
 
+    def owned_frames(frame, blocks, rows, count):
+        starts = [j * rows + dp_index * count for j in range(blocks)]
+        return jnp.stack([lax.dynamic_slice_in_dim(frame, s, count, 1) for s in starts])
+
     def factor_steps():
         (left,), (right,), deps = yield from add_steps([early], "dp")
         frame, own = frames_and_basis(left, right, merged_early, dp_count, deps)
         (left,), (right,), deps = yield from add_steps([own], "dp")
-        return (frame,) + tuple(basis_and_errors(frame, left, right, merged_early, dp_count, deps))
+        update = (
+            owned_frames(frame, 2, width, w_ff.shape[1]), jnp.swapaxes(w_ff, 1, 2), jnp.swapaxes(mom_ff, 1, 2)
+        )
+        return (frame,) + tuple(basis_and_errors(frame, left, right, merged_early, dp_count, update, deps))
 
     steps = factor_steps()
     next(steps)
@@ -1141,7 +1156,7 @@
         while True:
             steps.send((own,))
     except StopIteration as end:
-        frame_early, basis_early, *errors_early = end.value
+        frame_early, basis_early, w_ff_new, mom_ff_new, *errors_early = end.value
     back_passed = [pass_on(*back_parts[m], (own,) if m == last else ()) for m in micros]
     (left, flat), (right, flat_moved), unused = finish_steps(add_steps([own, flat], "dp"))
     flat = (flat + flat_moved) / dp_count
@@ -1153,7 +1168,10 @@
     for m in micros:
         if m == last:
             deps = (back_passed[last], d_tokens, out_tokens)
-            basis_late, *errors_late = basis_and_errors(frame_late, left, right, merged, dp_count, deps)
+            update = (owned_frames(frame_late, 4, width, w_in.shape[1]), w_in, mom_in)
+            basis_late, w_in_new, mom_in_new, *errors_late = basis_and_errors(
+                frame_late, left, right, merged, dp_count, update, deps
+            )
         keep, beside = back_parts[m]
         d_tokens = norm_back_into(
             d_tokens, m, micro_count, d_resid[m], tokens, keep, beside, back_across[m], gain_one
@@ -1189,13 +1207,10 @@
     basis_down_new = rights[7].T[None]
     err_in_new, err_out_new = errors_late[0][None], errors_late[1]
     err_ff_new, err_down_new = jnp.swapaxes(errors_early[0], 1, 2)[None], errors_early[1]
-    owned_in = jnp.stack([outer(part(f, w_in.shape[1], 1), b) for f, b in zip(frames[:4], rights[:4])])
-    owned_ff = jnp.stack([outer(part(f, w_ff.shape[1], 1), b) for f, b in zip(frames[5:7], rights[5:7])])
+    w_ff_new, mom_ff_new = jnp.swapaxes(w_ff_new, 1, 2), jnp.swapaxes(mom_ff_new, 1, 2)
     owned_out = outer(frames[4], part(rights[4], w_out.shape[1], 1))
     owned_down = outer(frames[7], part(rights[7], w_down.shape[1], 1))
-    w_in_new, mom_in_new = advance_weight(w_in, mom_in, owned_in, step_rate)
     w_out_new, mom_out_new = advance_weight(w_out, mom_out, owned_out, step_rate)
-    w_ff_new, mom_ff_new = advance_weight(w_ff, mom_ff, owned_ff, step_rate)
     w_down_new, mom_down_new = advance_weight(w_down, mom_down, owned_down, step_rate)
     gains_new, mom_gains_new = advance_weight(norm_gains, mom_gains, gain_total, small_rate)
     conv_new, mom_conv_new = advance_weight(conv_taps, mom_conv, grad_conv, small_rate)

time: 587 us -> 568 us (0.968)
  waiting for transfers between devices: 64.6 us -> 47 us
  local copies, waits for them, and re-layouts: 43.1 us -> 49.9 us
  matrix products: 120 us -> 114 us
    ppermute x57, waiting for transfers between devices: 41.8 us -> 32 us  [swap(): return lax.ppermute(value, axis, [(i, i ^ flip) for i in range(count)])]
    all_gather x1, waiting for transfers between devices: 22.8 us -> 15 us  [on_device(): weights_first = lax.all_gather(first, 'dp', axis=1, tiled=True)]
    dot_general x8 -> x2, matrix products: 11.4 us -> 4.14 us  [outer(): return jnp.einsum('rm,rn->mn', frame, basis, precision=precise)]
    unnamed x250 -> x242, local copies, waits for them, and re-layouts: 26.8 us -> 31.3 us
  transfers between devices with their start and end apart: 59 -> 59, of which waited for: 9 -> 8; matrix products, arithmetic and copies ran while one was open for 26% -> 27% of each run, Pallas kernels for 46% -> 49%
where the time goes in v3:
time: 568 us; the launch traced here: 557 us
  Pallas kernels  276 us (49%)
  matrix products  114 us (20%)
  local copies, waits for them, and re-layouts  49.9 us (9%)
  waiting for transfers between devices  47 us (8%)
  starting transfers between devices  41 us (7%)
  between operations  15.6 us (3%)
  other arithmetic  12.9 us (2%)
    pallas_call x8, Pallas kernels, mixer_call(): pl.pallas_call(body, grid=(1,), in_specs=in_specs, out_specs=out_specs, o...  140 us
    pallas_call x31, Pallas kernels, call(): pl.pallas_call(kernel, grid=(1,), in_specs=kinds + any_specs(deps), out_s...  129 us
    dot_general x30, matrix products, dot32(): return jnp.einsum(spec, a, b, preferred_element_type=jnp.float32)  110 us
    ppermute x57, starting transfers between devices, swap(): return lax.ppermute(value, axis, [(i, i ^ flip) for i in range(count)])  41 us
    ppermute x57, waiting for transfers between devices, swap(): return lax.ppermute(value, axis, [(i, i ^ flip) for i in range(count)])  32 us
    unnamed x242, local copies, waits for them, and re-layouts  31.3 us
    all_gather x1, waiting for transfers between devices, on_device(): weights_first = lax.all_gather(first, 'dp', axis=1, tiled=True)  15 us
  transfers between devices with their start and end apart: 59, of which 8 were waited for; matrix products, arithmetic and copies ran while one was open for 27% of the time, Pallas kernels for 49%

profile of v3, /device:TPU:0, one launch (start us, length us, event | category | flops | bytes accessed | tf_op | source)
XLA Modules:
  0.0 556.8 jit_solution(7481820940972745332)
XLA Ops:
  12.5 2.9 collective-permute-start.1
  18.0 4.1 sketches.4.refs_7_
  22.1 6.4 %collective-permute-done.1 = bf16[256,1024]{1,0:T(8,128)(2,1)} collective-permute-done((bf16[256,1024]{1,0:T(8,128)(2,1)}, bf16[256,1024]{1,0:T(8,128)(2,1)}, u32[]{:S(2)}, u32[]{:S(2)}) %collective-permute-start.1) | collective-permute-done | bytes 524320 | tf_op jit(solution)/shard_map/ppermute | solution.py:898
  28.5 6.1 %sketches.3.refs_6_ = f32[8,2752]{1,0:T(8,128)} custom-call(f32[2,704,1024]{2,1,0:T(8,128)} %bitcast.267, f32[1,704,1024]{2,1,0:T(8,128)} %refs_1_.1, f32[2,8,704]{2,1,0:T(8,128)} %bitcast.284, f32[1,8,1024]{2,1,0:T(8,128)} %bitcast.287), custom_call_target="tpu_custom_call" | custom-call | flops 1000000000 | bytes 3000000 | tf_op jit(solution)/shard_map/sketches/pallas_call | solution.py:604
  40.6 4.2 fusion.55.refs_6_
  48.3 5.0 fusion.56.refs_8_.refs_6_
  53.3 15.0 %all-gather.3.cloned.1.call-done = bf16[5,1024,256]{2,1,0:T(8,128)(2,1)} async-done(((bf16[5,128,256]{2,1,0:T(8,128)(2,1)}), bf16[5,1024,256]{2,1,0:T(8,128)(2,1)}) %all-gather.3.cloned.1.call-update) | async-done | bytes 2621456 | tf_op jit(solution)/shard_map/all_gather | solution.py:956
  68.3 6.6 %fusion.29.refs_0_ = f32[4,256,1024]{2,1,0:T(8,128)} fusion(bf16[5,1024,256]{2,1,0:T(8,128)(2,1)} %all-gather.3.cloned.1.call-done, bf16[1024,1024]{1,0:T(8,128)(2,1)} %copy-done.10), kind=kOutput, calls=%fused_computation.38 | convolution fusion | flops 2147483648 | bytes 8912896 | tf_op jit(solution)/shard_map/jdc,td->jct/dot_general | solution.py:913
  74.9 9.9 %mixer_forward.4 = bf16[128,1024]{1,0:T(8,128)(2,1)} custom-call(f32[4,256,1024]{2,1,0:T(8,128)} %fusion.29.refs_0_, f32[2,1,1024]{2,1,0:T(1,128)} %broadcast_in_dim.36.refs_1_, f32[3,256,4]{2,1,0:T(8,128)} %bitcast.274, f32[1,1024]{1,0:T(1,128)} %get-tuple-element.315.refs_3_, s32[3]{0:T(128)} %get-tuple-element.321.refs_4_.refs_8_, f32[2,2]{1,0:T(2,128)} %refs_9_.7, ...), custom_call_target="tpu_custom_call" | custom-call | flops 11000000512 | bytes 33000000 | tf_op jit(solution)/shard_map/mixer_forward/pallas_call | solution.py:565
  84.8 9.8 %mixer_forward.5 = bf16[128,1024]{1,0:T(8,128)(2,1)} custom-call(f32[4,256,1024]{2,1,0:T(8,128)} %fusion.29.refs_0_, f32[2,1,1024]{2,1,0:T(1,128)} %broadcast_in_dim.36.refs_1_, f32[3,256,4]{2,1,0:T(8,128)} %bitcast.275, f32[1,1024]{1,0:T(1,128)} %get-tuple-element.315.refs_3_, s32[3]{0:T(128)} %get-tuple-element.321.refs_4_.refs_8_, f32[2,2]{1,0:T(2,128)} %refs_9_.7, ...), custom_call_target="tpu_custom_call" | custom-call | flops 11000000512 | bytes 33000000 | tf_op jit(solution)/shard_map/mixer_forward/pallas_call | solution.py:565
  94.6 2.0 fusion.62
  103.7 2.2 convolution_bitcast_fusion.1
  106.6 6.0 %fusion.27.refs_2_.refs_0_ = f32[4,256,1024]{2,1,0:T(8,128)} fusion(bf16[5,1024,256]{2,1,0:T(8,128)(2,1)} %all-gather.3.cloned.1.call-done, bf16[1024,1024]{1,0:T(8,128)(2,1)S(1)} %copy-done.9), kind=kOutput, calls=%fused_computation.36 | convolution fusion | flops 2147483648 | bytes 8912896 | tf_op jit(solution)/shard_map/jdc,td->jct/dot_general | solution.py:913
  112.6 2.1 pass_on.8.refs_6_
  115.6 9.8 %mixer_forward.6.refs_5_ = bf16[128,1024]{1,0:T(8,128)(2,1)} custom-call(f32[4,256,1024]{2,1,0:T(8,128)} %fusion.27.refs_2_.refs_0_, f32[2,1,1024]{2,1,0:T(1,128)} %broadcast_in_dim.37.refs_1_, f32[3,256,4]{2,1,0:T(8,128)} %bitcast.276, f32[1,1024]{1,0:T(1,128)} %get-tuple-element.314.refs_3_, s32[3]{0:T(128)} %get-tuple-element.320.refs_4_.refs_8_, ...), custom_call_target="tpu_custom_call" | custom-call | flops 11000000512 | bytes 33000000 | tf_op jit(solution)/shard_map/mixer_forward/pallas_call | solution.py:565
  125.4 3.9 collective-permute-done.7.refs_3_
  130.1 3.0 second_norm.2
  133.8 9.6 %mixer_forward.7 = bf16[128,1024]{1,0:T(8,128)(2,1)} custom-call(f32[4,256,1024]{2,1,0:T(8,128)} %fusion.27.refs_2_.refs_0_, f32[2,1,1024]{2,1,0:T(1,128)} %broadcast_in_dim.37.refs_1_, f32[3,256,4]{2,1,0:T(8,128)} %bitcast.277, f32[1,1024]{1,0:T(1,128)} %get-tuple-element.314.refs_3_, s32[3]{0:T(128)} %get-tuple-element.320.refs_4_.refs_8_, ...), custom_call_target="tpu_custom_call" | custom-call | flops 11000000512 | bytes 33000000 | tf_op jit(solution)/shard_map/mixer_forward/pallas_call | solution.py:565
  143.5 2.0 fusion.63
  146.9 2.0 convolution_convert_fusion
  151.8 19.2 %ffn_pass.2 = (bf16[1024,704]{1,0:T(8,128)(2,1)}, bf16[2,1024,704]{2,1,0:T(8,128)(2,1)}, bf16[2,256,1024]{2,1,0:T(8,128)(2,1)}, bf16[2,256,1024]{2,1,0:T(8,128)(...) custom-call(bf16[256,1024]{1,0:T(8,128)(2,1)} %get-tuple-element.95., ...), custom_call_target="tpu_custom_call" | custom-call | flops 12000000000 | bytes 36000000 | tf_op jit(solution)/shard_map/ffn_pass/pallas_call | solution.py:604
  171.2 2.3 pass_on.9
  174.3 6.9 %fusion.25.refs_5_ = f32[2,704,1024]{2,1,0:T(8,128)} fusion(bf16[2,1024,704]{2,1,0:T(8,128)(2,1)S(1)} %copy-done.109, bf16[1024,1024]{1,0:T(8,128)(2,1)} %get-tuple-element.101), kind=kOutput, calls=%fused_computation.34 | convolution fusion | flops 2952790016 | bytes 10747904 | tf_op jit(solution)/shard_map/jth,td->jhd/dot_general | solution.py:913
  181.2 3.3 fusion.123.refs_6_
  184.4 3.4 collective-permute-done.17.refs_3_
  188.7 3.0 second_norm.3
  192.9 12.4 %collective-permute-done.18.refs_2_ = bf16[256,1024]{1,0:T(8,128)(2,1)} collective-permute-done((bf16[256,1024]{1,0:T(8,128)(2,1)}, bf16[256,1024]{1,0:T(8,128)(2,1)}, u32[]{:S(2)}, u32[]{:S(2)}) %collective-permute-start.18) | collective-permute-done | bytes 524320 | tf_op jit(solution)/shard_map/ppermute | solution.py:898
  209.1 2.1 pass_on.10.refs_11_
  212.0 19.0 %ffn_pass.3 = (bf16[1024,704]{1,0:T(8,128)(2,1)}, bf16[2,1024,704]{2,1,0:T(8,128)(2,1)}, bf16[2,256,1024]{2,1,0:T(8,128)(2,1)}, bf16[2,256,1024]{2,1,0:T(8,128)(...) custom-call(bf16[256,1024]{1,0:T(8,128)(2,1)} %get-tuple-element.104, ...), custom_call_target="tpu_custom_call" | custom-call | flops 12000000000 | bytes 36000000 | tf_op jit(solution)/shard_map/ffn_pass/pallas_call | solution.py:604
  232.1 3.8 norm_back.2
  238.4 10.1 %add_add_fusion.refs_2_.refs_6_ = f32[2,704,1024]{2,1,0:T(8,128)} fusion(f32[2,704,1024]{2,1,0:T(8,128)} %fusion.25.refs_5_, bf16[2,1024,704]{2,1,0:T(8,128)(2,1)} %get-tuple-element.111, bf16[1024,1024]{1,0:T(8,128)(2,1)} %get-tuple-element.112, f32[1,2,1024,704]{2,3,1,0:T(8,128)S(1)} %bitcast.269), kind=kOutput, calls=%fused_computation | convolution fusion | flops 2955673600 | bytes 22282240 | tf_op jit(solution)/shard_map/jth,td->jhd/dot_general | solution.py:913
  248.5 3.4 bitcast_add_fusion.3.refs_3_.refs_7_
  258.9 2.1 pass_on.11.refs_11_
  262.1 5.3 fusion.33.refs_4_
  267.5 25.2 %mixer_backward.4 = (bf16[4,128,1024]{2,1,0:T(8,128)(2,1)}, f32[1,1,1024]{2,1,0:T(1,128)}, f32[3,128,4]{2,1,0:T(8,128)}, f32[1,1,128]{2,1,0:T(1,128)}, f32[8,4096]{1,0:T(8,128)}) custom-call(f32[4,256,1024]{2,1,0:T(8,128)} %fusion.29.refs_0_, f32[2,1,1024]{2,1,0:T(1,128)} %broadcast_in_dim.36.refs_1_, f32[3,256,4]{2,1,0:T(8,128)} %bitcast.278, ...), custom_call_target="tpu_custom_call" | custom-call | flops 28000000000 | bytes 84000000 | tf_op jit(solution)/shard_map/mixer_backward/pallas_call | solution.py:565
  295.6 2.1 pass_on.12
  300.0 3.8 norm_back.3
  304.4 25.4 %mixer_backward.5 = (bf16[4,128,1024]{2,1,0:T(8,128)(2,1)}, f32[1,1,1024]{2,1,0:T(1,128)}, f32[3,128,4]{2,1,0:T(8,128)}, f32[1,1,128]{2,1,0:T(1,128)}, f32[8,4096]{1,0:T(8,128)}) custom-call(f32[4,256,1024]{2,1,0:T(8,128)} %fusion.29.refs_0_, f32[2,1,1024]{2,1,0:T(1,128)} %broadcast_in_dim.36.refs_1_, f32[3,256,4]{2,1,0:T(8,128)} %bitcast.279, ...), custom_call_target="tpu_custom_call" | custom-call | flops 28000000000 | bytes 84000000 | tf_op jit(solution)/shard_map/mixer_backward/pallas_call | solution.py:565
  331.3 3.9 fusion.50
  335.2 2.4 fusion.57
  340.4 6.0 %convolution_bitcast_fusion.refs_11_ = f32[4,1024,256]{2,1,0:T(8,128)} fusion(bf16[4,256,1024]{2,1,0:T(8,128)(2,1)S(1)} %fusion.50, bf16[256,1024]{1,0:T(8,128)(2,1)} %collective-permute-done.2, bf16[256,1024]{1,0:T(8,128)(2,1)} %collective-permute-done.1, bf16[256,1024]{1,0:T(8,128)(2,1)} %collective-permute-done, bf16[256,1024]{1,0:T(8,128)(2,1)} %get-tuple-element.291), kind=kOutput, calls=%fused_computation.22 | convolution fusion | flops 2155872256 | bytes 8388608 | tf_op jit(solution)/shard_map/id,kci->kdc/dot_general | solution.py:913
  347.2 8.5 %frames_and_basis.2 = (f32[8,2752]{1,0:T(8,128)}, f32[8,2432]{1,0:T(8,128)}) custom-call(f32[8,2752]{1,0:T(8,128)} %add_after.10.refs_10_.refs_0_, f32[8,2752]{1,0:T(8,128)} %copy-done.49, f32[2,704,1024]{2,1,0:T(8,128)} %add_add_fusion.refs_2_.refs_6_, f32[1,704,1024]{2,1,0:T(8,128)} %bitcast_add_fusion.3.refs_3_.refs_7_, ...), custom_call_target="tpu_custom_call" | custom-call | flops 1000000000 | bytes 3000000 | tf_op jit(solution)/shard_map/frames_and_basis/pallas_call | solution.py:604
  359.1 2.1 pass_on.13
  365.8 2.2 pass_on.15
  370.0 1.8 fusion.61.refs_0_.refs_3_.refs_7_
  371.9 2.3 sketches.5
  375.5 4.9 fusion.31.refs_4_
  380.4 25.3 %mixer_backward.6 = (bf16[4,128,1024]{2,1,0:T(8,128)(2,1)}, f32[1,1,1024]{2,1,0:T(1,128)}, f32[3,128,4]{2,1,0:T(8,128)}, f32[1,1,128]{2,1,0:T(1,128)}, f32[8,4352]{1,0:T(8,128)}) custom-call(f32[4,256,1024]{2,1,0:T(8,128)} %fusion.27.refs_2_.refs_0_, f32[2,1,1024]{2,1,0:T(1,128)} %broadcast_in_dim.37.refs_1_, f32[3,256,4]{2,1,0:T(8,128)} %bitcast.280, ...), custom_call_target="tpu_custom_call" | custom-call | flops 28000000000 | bytes 84000000 | tf_op jit(solution)/shard_map/mixer_backward/pallas_call | solution.py:565
  407.9 24.8 %mixer_backward.7 = (bf16[4,128,1024]{2,1,0:T(8,128)(2,1)}, f32[1,1,1024]{2,1,0:T(1,128)}, f32[3,128,4]{2,1,0:T(8,128)}, f32[1,1,128]{2,1,0:T(1,128)}, f32[8,4352]{1,0:T(8,128)}) custom-call(f32[4,256,1024]{2,1,0:T(8,128)} %fusion.27.refs_2_.refs_0_, f32[2,1,1024]{2,1,0:T(1,128)} %broadcast_in_dim.37.refs_1_, f32[3,256,4]{2,1,0:T(8,128)} %bitcast.281, ...), custom_call_target="tpu_custom_call" | custom-call | flops 28000000000 | bytes 84000000 | tf_op jit(solution)/shard_map/mixer_backward/pallas_call | solution.py:565
  434.8 2.8 fusion.125
  437.6 3.8 fusion.45.refs_2_.refs_0_
  441.4 1.9 fusion.116
  443.4 2.0 fusion.80
  447.9 10.0 %multiply_reduce_fusion = (f32[1024]{0:T(1024)S(1)}, f32[4,1024,256]{2,1,0:T(8,128)}) fusion(bf16[5,1024,256]{2,1,0:T(8,128)(2,1)} %all-gather.3.cloned.1.call-done, f32[1,4,1024,256]{3,2,1,0:T(8,128)} %param.50, f32[4,1024,256]{2,1,0:T(8,128)} %convolution_bitcast_fusion.refs_11_, bf16[4,256,1024]{2,1,0:T(8,128)(2,1)} %gate.6.refs_0_, ...), kind=kOutput, calls=%fused_computation.6 | convolution fusion | flops 2161114112 | bytes 18878464 | tf_op jit(solution)/shard_map/id,kci->kdc/dot_general | solution.py:913
  462.8 2.8 collective-permute-done.48
  471.8 5.8 %fusion = bf16[1024,1024]{1,0:T(8,128)(2,1)S(1)} fusion(f32[1024,1024]{1,0:T(8,128)} %fusion.125, bf16[4,256,1024]{2,1,0:T(8,128)(2,1)} %gate.7, bf16[5,1024,256]{2,1,0:T(8,128)(2,1)} %all-gather.3.cloned.1.call-done), kind=kOutput, calls=%fused_computation.2 | convolution fusion | flops 2149580800 | bytes 10485760 | tf_op jit(solution)/shard_map/kci,kdc->id/dot_general | solution.py:913
  480.7 5.8 %frames_and_basis.3 = (f32[8,4352]{1,0:T(8,128)}, f32[8,2048]{1,0:T(8,128)}) custom-call(f32[8,4352]{1,0:T(8,128)} %add_after.13.refs_1_.refs_0_, f32[8,4352]{1,0:T(8,128)} %copy-done.43, f32[4,1024,256]{2,1,0:T(8,128)} %get-tuple-element.277.refs_2_.refs_6_, f32[1,256,1024]{2,1,0:T(8,128)} %fusion.61.refs_0_.refs_3_.refs_7_, bf16[2,2,256,1024]{3,2,1,0:T(8,128)(2,1)} %bitcast.266), custom_call_target="tpu_custom_call" | custom-call | flops 1000000000 | bytes 3000000 | tf_op jit(solution)/shard_map/frames_and_basis/pallas_call | solution.py:604
  492.4 3.9 add_rows.1.refs_10_
  501.8 9.1 %basis_and_errors.3 = (f32[8,2432]{1,0:T(8,128)}, f32[2,704,128]{2,1,0:T(8,128)}, f32[2,704,128]{2,1,0:T(8,128)}, f32[2,704,1024]{2,1,0:T(8,128)}, f32[1,704,1024]{2,1,0:T(8,128)}) custom-call(f32[8,2752]{1,0:T(8,128)} %get-tuple-element.155.refs_0_, f32[8,2432]{1,0:T(8,128)} %add_after.17.refs_1_, f32[8,2432]{1,0:T(8,128)} %copy-done.50, ...), custom_call_target="tpu_custom_call" | custom-call | flops 1000000000 | bytes 3000000 | tf_op jit(solution)/shard_map/basis_and_errors/pallas_call | solution.py:604
  512.2 2.3 fusion.122
  521.0 3.7 norm_back_into.2.refs_0_.refs_9_
  530.6 2.1 pass_on.14.refs_8_
  534.4 6.4 %basis_and_errors.2 = (f32[8,2048]{1,0:T(8,128)}, f32[4,128,256]{2,1,0:T(8,128)}, f32[4,128,256]{2,1,0:T(8,128)}, f32[4,1024,256]{2,1,0:T(8,128)}, f32[1,256,1024]{2,1,0:T(8,128)}) custom-call(f32[8,4352]{1,0:T(8,128)} %get-tuple-element.139.refs_0_, f32[8,2048]{1,0:T(8,128)} %get-tuple-element.149.refs_1_, f32[8,2048]{1,0:T(8,128)} %copy-done.52, ...), custom_call_target="tpu_custom_call" | custom-call | flops 1000000000 | bytes 3000000 | tf_op jit(solution)/shard_map/basis_and_errors/pallas_call | solution.py:604
  546.2 3.4 norm_back_into.3
  (448 shorter events, 125.5 us)
Async XLA Ops:
  7.2 61.0 %all-gather.3.cloned.1.call-start = ((), (), s32[]{:S(2)}) async-start(), calls=%async_computation | async-start | bytes 2949120 | tf_op jit(solution)/shard_map/all_gather | solution.py:956
  10.2 141.4 %all-gather.5.cloned.1.call-start = ((), (), s32[]{:S(2)}) async-start(), calls=%async_computation.1 | async-start | bytes 5308416 | tf_op jit(solution)/shard_map/all_gather | solution.py:959
  12.5 16.0 %collective-permute-start.1 = (bf16[256,1024]{1,0:T(8,128)(2,1)}, bf16[256,1024]{1,0:T(8,128)(2,1)}, u32[]{:S(2)}, u32[]{:S(2)}) collective-permute-start(bf16[256,1024]{1,0:T(8,128)(2,1)} %get-tuple-element.291), channel_id=1, source_target_pairs={{0,2},{1,3},{2,0},{3,1},{4,6},{5,7},{6,4},{7,5},{8,10},{9,11},{10,... | collective-permute-start | bytes 1572872 | tf_op jit(solution)/shard_map/ppermute | solution.py:898
  15.4 25.2 %collective-permute-start = (bf16[256,1024]{1,0:T(8,128)(2,1)}, bf16[256,1024]{1,0:T(8,128)(2,1)}, u32[]{:S(2)}, u32[]{:S(2)}) collective-permute-start(bf16[256,1024]{1,0:T(8,128)(2,1)} %get-tuple-element.291), channel_id=1, source_target_pairs={{0,1},{1,0},{2,3},{3,2},{4,5},{5,4},{6,7},{7,6},{8,9},{9,8},{10,11... | collective-permute-start | bytes 1572872 | tf_op jit(solution)/shard_map/ppermute | solution.py:898
  15.4 23.5 %collective-permute-start.4 = (bf16[256,1024]{1,0:T(8,128)(2,1)}, bf16[256,1024]{1,0:T(8,128)(2,1)}, u32[]{:S(2)}, u32[]{:S(2)}) collective-permute-start(bf16[256,1024]{1,0:T(8,128)(2,1)} %get-tuple-element.290), channel_id=1, source_target_pairs={{0,2},{1,3},{2,0},{3,1},{4,6},{5,7},{6,4},{7,5},{8,10},{9,11},{10,... | collective-permute-start | bytes 1572872 | tf_op jit(solution)/shard_map/ppermute | solution.py:898
  15.5 31.9 %collective-permute-start.3 = (bf16[256,1024]{1,0:T(8,128)(2,1)}, bf16[256,1024]{1,0:T(8,128)(2,1)}, u32[]{:S(2)}, u32[]{:S(2)}) collective-permute-start(bf16[256,1024]{1,0:T(8,128)(2,1)} %get-tuple-element.290), channel_id=1, source_target_pairs={{0,1},{1,0},{2,3},{3,2},{4,5},{5,4},{6,7},{7,6},{8,9},{9,8},{10,11... | collective-permute-start | bytes 1572872 | tf_op jit(solution)/shard_map/ppermute | solution.py:898
  22.0 121.4 %copy-start.76 = (s32[1024]{0:T(1024)}, s32[1024]{0:T(1024)S(1)}, u32[]{:S(2)}) copy-start(s32[1024]{0:T(1024)S(1)} %fusion.87) | copy-start | bytes 12292
  28.5 12.2 %collective-permute-start.2 = (bf16[256,1024]{1,0:T(8,128)(2,1)}, bf16[256,1024]{1,0:T(8,128)(2,1)}, u32[]{:S(2)}, u32[]{:S(2)}) collective-permute-start(bf16[256,1024]{1,0:T(8,128)(2,1)} %collective-permute-done.1), channel_id=1, source_target_pairs={{0,1},{1,0},{2,3},{3,2},{4,5},{5,4},{6,7},{7,6},{8,9},{9,8},{10,11... | collective-permute-start | bytes 1572872 | tf_op jit(solution)/shard_map/ppermute | solution.py:898
  34.6 69.1 %copy-start.46 = (bf16[1024,2]{0,1:T(2,128)(2,1)}, bf16[1024,2]{0,1:T(2,128)(2,1)S(1)}, u32[]{:S(2)}) copy-start(bf16[1024,2]{0,1:T(2,128)(2,1)S(1)} %convert_element_type.98) | copy-start | bytes 12292
  38.9 67.7 %collective-permute-start.12 = (bf16[256,1024]{1,0:T(8,128)(2,1)}, bf16[256,1024]{1,0:T(8,128)(2,1)}, u32[]{:S(2)}, u32[]{:S(2)}) collective-permute-start(bf16[256,1024]{1,0:T(8,128)(2,1)} %gate.4.refs_4_), channel_id=1, source_target_pairs={{0,2},{1,3},{2,0},{3,1},{4,6},{5,7},{6,4},{7,5},{8,10},{9,11},{10,... | collective-permute-start | bytes 1572872 | tf_op jit(solution)/shard_map/ppermute | solution.py:898
  40.6 6.8 %collective-permute-start.5 = (bf16[256,1024]{1,0:T(8,128)(2,1)}, bf16[256,1024]{1,0:T(8,128)(2,1)S(1)}, u32[]{:S(2)}, u32[]{:S(2)}) collective-permute-start(bf16[256,1024]{1,0:T(8,128)(2,1)} %collective-permute-done.4.refs_1_), channel_id=1, source_target_pairs={{0,1},{1,0},{2,3},{3,2},{4,5},{5,4},{6,7},{7,6},{8,9},{9,8},{10,11... | collective-permute-start | bytes 1572872 | tf_op jit(solution)/shard_map/ppermute | solution.py:898
  100.7 11.9 %collective-permute-start.6 = (bf16[2,256,1024]{2,1,0:T(8,128)(2,1)}, bf16[2,256,1024]{2,1,0:T(8,128)(2,1)}, u32[]{:S(2)}, u32[]{:S(2)}) collective-permute-start(bf16[2,256,1024]{2,1,0:T(8,128)(2,1)} %get-tuple-element.288), channel_id=1, source_target_pairs={{0,1},{1,0},{2,3},{3,2},{4,5},{5,4},{6,7},{7,6},{8,9},{9,8},{10,11... | collective-permute-start | bytes 3145736 | tf_op jit(solution)/shard_map/ppermute | solution.py:898
  101.7 48.7 %collective-permute-start.11 = (bf16[256,1024]{1,0:T(8,128)(2,1)}, bf16[256,1024]{1,0:T(8,128)(2,1)S(1)}, u32[]{:S(2)}, u32[]{:S(2)}) collective-permute-start(bf16[256,1024]{1,0:T(8,128)(2,1)} %gate.4.refs_4_), channel_id=1, source_target_pairs={{0,1},{1,0},{2,3},{3,2},{4,5},{5,4},{6,7},{7,6},{8,9},{9,8},{10,11... | collective-permute-start | bytes 1572872 | tf_op jit(solution)/shard_map/ppermute | solution.py:898
  102.2 90.2 %collective-permute-start.23 = (bf16[256,1024]{1,0:T(8,128)(2,1)}, bf16[256,1024]{1,0:T(8,128)(2,1)}, u32[]{:S(2)}, u32[]{:S(2)}) collective-permute-start(bf16[256,1024]{1,0:T(8,128)(2,1)} %gate.5.refs_4_), channel_id=1, source_target_pairs={{0,2},{1,3},{2,0},{3,1},{4,6},{5,7},{6,4},{7,5},{8,10},{9,11},{10,... | collective-permute-start | bytes 1572872 | tf_op jit(solution)/shard_map/ppermute | solution.py:898
  106.6 44.2 %collective-permute-start.13 = (bf16[256,1024]{1,0:T(8,128)(2,1)}, bf16[256,1024]{1,0:T(8,128)(2,1)S(1)}, u32[]{:S(2)}, u32[]{:S(2)}) collective-permute-start(bf16[256,1024]{1,0:T(8,128)(2,1)} %collective-permute-done.12.refs_6_), channel_id=1, source_target_pairs={{0,1},{1,0},{2,3},{3,2},{4,5},{5,4},{6,7},{7,6},{8,9},{9,8},{10,11... | collective-permute-start | bytes 1572872 | tf_op jit(solution)/shard_map/ppermute | solution.py:898
  114.7 14.5 %collective-permute-start.7 = (bf16[256,1024]{1,0:T(8,128)(2,1)}, bf16[256,1024]{1,0:T(8,128)(2,1)S(1)}, u32[]{:S(2)}, u32[]{:S(2)}) collective-permute-start(bf16[256,1024]{1,0:T(8,128)(2,1)} %pass_on.8.refs_6_), channel_id=1, source_target_pairs={{0,2},{1,3},{2,0},{3,1},{4,6},{5,7},{6,4},{7,5},{8,10},{9,11},{10,... | collective-permute-start | bytes 1572872 | tf_op jit(solution)/shard_map/ppermute | solution.py:898
  133.0 13.9 %collective-permute-start.9 = (bf16[256,1024]{1,0:T(8,128)(2,1)}, bf16[256,1024]{1,0:T(8,128)(2,1)S(1)}, u32[]{:S(2)}, u32[]{:S(2)}) collective-permute-start(bf16[256,1024]{1,0:T(8,128)(2,1)} %get-tuple-element.95.refs_6_.refs_0_), channel_id=1, source_target_pairs={{0,2},{1,3},{2,0},{3,1},{4,6},{5,7},{6,4},{7,5},{8,10},{9,11},{10,... | collective-permute-start | bytes 1572872 | tf_op jit(solution)/shard_map/ppermute | solution.py:898
  143.5 7.3 %collective-permute-start.8 = (bf16[256,1024]{1,0:T(8,128)(2,1)S(1)}, bf16[256,1024]{1,0:T(8,128)(2,1)S(1)}, u32[]{:S(2)}, u32[]{:S(2)}) collective-permute-start(bf16[256,1024]{1,0:T(8,128)(2,1)S(1)} %copy-done.91), channel_id=1, source_target_pairs={{0,1},{1,0},{2,3},{3,2},{4,5},{5,4},{6,7},{7,6},{8,9},{9,8},{10,11... | collective-permute-start | bytes 1572872 | tf_op jit(solution)/shard_map/ppermute | solution.py:898
  146.9 4.7 collective-permute-start.10
  150.4 20.9 %collective-permute-start.16 = (bf16[2,256,1024]{2,1,0:T(8,128)(2,1)}, bf16[2,256,1024]{2,1,0:T(8,128)(2,1)}, u32[]{:S(2)}, u32[]{:S(2)}) collective-permute-start(bf16[2,256,1024]{2,1,0:T(8,128)(2,1)} %get-tuple-element.287.refs_11_), channel_id=1, source_target_pairs={{0,1},{1,0},{2,3},{3,2},{4,5},{5,4},{6,7},{7,6},{8,9},{9,8},{10,11... | collective-permute-start | bytes 3145736 | tf_op jit(solution)/shard_map/ppermute | solution.py:898
  171.0 37.2 %collective-permute-start.15 = (bf16[2,256,1024]{2,1,0:T(8,128)(2,1)}, bf16[2,256,1024]{2,1,0:T(8,128)(2,1)S(1)}, u32[]{:S(2)}, u32[]{:S(2)}) collective-permute-start(bf16[2,256,1024]{2,1,0:T(8,128)(2,1)} %get-tuple-element.99.refs_2_), channel_id=1, source_target_pairs={{0,1},{1,0},{2,3},{3,2},{4,5},{5,4},{6,7},{7,6},{8,9},{9,8},{10,11... | collective-permute-start | bytes 3145736 | tf_op jit(solution)/shard_map/ppermute | solution.py:898
  173.5 14.4 %collective-permute-start.17 = (bf16[256,1024]{1,0:T(8,128)(2,1)}, bf16[256,1024]{1,0:T(8,128)(2,1)S(1)}, u32[]{:S(2)}, u32[]{:S(2)}) collective-permute-start(bf16[256,1024]{1,0:T(8,128)(2,1)} %pass_on.9), channel_id=1, source_target_pairs={{0,2},{1,3},{2,0},{3,1},{4,6},{5,7},{6,4},{7,5},{8,10},{9,11},{10,... | collective-permute-start | bytes 1572872 | tf_op jit(solution)/shard_map/ppermute | solution.py:898
  191.7 13.7 %collective-permute-start.18 = (bf16[256,1024]{1,0:T(8,128)(2,1)}, bf16[256,1024]{1,0:T(8,128)(2,1)}, u32[]{:S(2)}, u32[]{:S(2)}) collective-permute-start(bf16[256,1024]{1,0:T(8,128)(2,1)} %get-tuple-element.104.refs_0_), channel_id=1, source_target_pairs={{0,2},{1,3},{2,0},{3,1},{4,6},{5,7},{6,4},{7,5},{8,10},{9,11},{10,... | collective-permute-start | bytes 1572872 | tf_op jit(solution)/shard_map/ppermute | solution.py:898
  192.4 18.8 %collective-permute-start.22 = (bf16[256,1024]{1,0:T(8,128)(2,1)}, bf16[256,1024]{1,0:T(8,128)(2,1)}, u32[]{:S(2)}, u32[]{:S(2)}) collective-permute-start(bf16[256,1024]{1,0:T(8,128)(2,1)} %gate.5.refs_4_), channel_id=1, source_target_pairs={{0,1},{1,0},{2,3},{3,2},{4,5},{5,4},{6,7},{7,6},{8,9},{9,8},{10,11... | collective-permute-start | bytes 1572872 | tf_op jit(solution)/shard_map/ppermute | solution.py:898
  192.4 19.6 %collective-permute-start.24 = (bf16[256,1024]{1,0:T(8,128)(2,1)}, bf16[256,1024]{1,0:T(8,128)(2,1)}, u32[]{:S(2)}, u32[]{:S(2)}) collective-permute-start(bf16[256,1024]{1,0:T(8,128)(2,1)} %collective-permute-done.23.refs_6_), channel_id=1, source_target_pairs={{0,1},{1,0},{2,3},{3,2},{4,5},{5,4},{6,7},{7,6},{8,9},{9,8},{10,11... | collective-permute-start | bytes 1572872 | tf_op jit(solution)/shard_map/ppermute | solution.py:898
  192.9 19.1 %collective-permute-start.20 = (bf16[256,1024]{1,0:T(8,128)(2,1)}, bf16[256,1024]{1,0:T(8,128)(2,1)}, u32[]{:S(2)}, u32[]{:S(2)}) collective-permute-start(bf16[256,1024]{1,0:T(8,128)(2,1)} %get-tuple-element.104.refs_0_), channel_id=1, source_target_pairs={{0,1},{1,0},{2,3},{3,2},{4,5},{5,4},{6,7},{7,6},{8,9},{9,8},{10,11... | collective-permute-start | bytes 1572872 | tf_op jit(solution)/shard_map/ppermute | solution.py:898
  205.4 6.6 %collective-permute-start.21 = (bf16[256,1024]{1,0:T(8,128)(2,1)}, bf16[256,1024]{1,0:T(8,128)(2,1)}, u32[]{:S(2)}, u32[]{:S(2)}) collective-permute-start(bf16[256,1024]{1,0:T(8,128)(2,1)} %collective-permute-done.18.refs_2_), channel_id=1, source_target_pairs={{0,1},{1,0},{2,3},{3,2},{4,5},{5,4},{6,7},{7,6},{8,9},{9,8},{10,11... | collective-permute-start | bytes 1572872 | tf_op jit(solution)/shard_map/ppermute | solution.py:898
  206.7 31.7 %slice-start = ((s8[5767168]{0:T(1024)(128)(4,1)}), s8[4194304]{0:T(1024)(128)(4,1)S(1)}, s32[]{:S(2)}) async-start(s8[5767168]{0:T(1024)(128)(4,1)} %bitcast.268), calls=%async_computation.2 | async-start | bytes 8388608
  208.1 87.4 %collective-permute-start.14 = (bf16[2,256,1024]{2,1,0:T(8,128)(2,1)}, bf16[2,256,1024]{2,1,0:T(8,128)(2,1)}, u32[]{:S(2)}, u32[]{:S(2)}) collective-permute-start(bf16[2,256,1024]{2,1,0:T(8,128)(2,1)} %get-tuple-element.97), channel_id=1, source_target_pairs={{0,1},{1,0},{2,3},{3,2},{4,5},{5,4},{6,7},{7,6},{8,9},{9,8},{10,11... | collective-permute-start | bytes 3145736 | tf_op jit(solution)/shard_map/ppermute | solution.py:898
  211.2 27.1 %slice-start.1 = ((s8[5767168]{0:T(1024)(128)(4,1)}), s8[1572864]{0:T(1024)(128)(4,1)S(1)}, s32[]{:S(2)}) async-start(s8[5767168]{0:T(1024)(128)(4,1)} %bitcast.268), calls=%async_computation.3 | async-start | bytes 3145728
  211.2 20.0 %collective-permute-start.19 = (bf16[256,1024]{1,0:T(8,128)(2,1)}, bf16[256,1024]{1,0:T(8,128)(2,1)S(1)}, u32[]{:S(2)}, u32[]{:S(2)}) collective-permute-start(bf16[256,1024]{1,0:T(8,128)(2,1)} %pass_on.10.refs_11_), channel_id=1, source_target_pairs={{0,2},{1,3},{2,0},{3,1},{4,6},{5,7},{6,4},{7,5},{8,10},{9,11},{10,... | collective-permute-start | bytes 1572872 | tf_op jit(solution)/shard_map/ppermute | solution.py:898
  231.0 26.9 %collective-permute-start.29 = (bf16[2,256,1024]{2,1,0:T(8,128)(2,1)}, bf16[2,256,1024]{2,1,0:T(8,128)(2,1)S(1)}, u32[]{:S(2)}, u32[]{:S(2)}) collective-permute-start(bf16[2,256,1024]{2,1,0:T(8,128)(2,1)} %get-tuple-element.105.refs_6_), channel_id=1, source_target_pairs={{0,1},{1,0},{2,3},{3,2},{4,5},{5,4},{6,7},{7,6},{8,9},{9,8},{10,11... | collective-permute-start | bytes 3145736 | tf_op jit(solution)/shard_map/ppermute | solution.py:898
  235.9 18.3 %collective-permute-start.25 = (bf16[256,1024]{1,0:T(8,128)(2,1)}, bf16[256,1024]{1,0:T(8,128)(2,1)}, u32[]{:S(2)}, u32[]{:S(2)}) collective-permute-start(bf16[256,1024]{1,0:T(8,128)(2,1)} %get-tuple-element.106.refs_2_), channel_id=1, source_target_pairs={{0,1},{1,0},{2,3},{3,2},{4,5},{5,4},{6,7},{7,6},{8,9},{9,8},{10,11... | collective-permute-start | bytes 1572872 | tf_op jit(solution)/shard_map/ppermute | solution.py:898
  236.2 15.8 %collective-permute-start.26 = (bf16[256,1024]{1,0:T(8,128)(2,1)}, bf16[256,1024]{1,0:T(8,128)(2,1)}, u32[]{:S(2)}, u32[]{:S(2)}) collective-permute-start(bf16[256,1024]{1,0:T(8,128)(2,1)} %get-tuple-element.106.refs_2_), channel_id=1, source_target_pairs={{0,2},{1,3},{2,0},{3,1},{4,6},{5,7},{6,4},{7,5},{8,10},{9,11},{10,... | collective-permute-start | bytes 1572872 | tf_op jit(solution)/shard_map/ppermute | solution.py:898
  237.6 14.4 %collective-permute-start.28 = (f32[8,2752]{1,0:T(8,128)S(1)}, f32[8,2752]{1,0:T(8,128)S(1)}, u32[]{:S(2)}, u32[]{:S(2)}) collective-permute-start(f32[8,2752]{1,0:T(8,128)S(1)} %maximum_add_fusion.refs_0_), channel_id=1, source_target_pairs={{0,4},{4,0},{8,12},{12,8},{16,20},{20,16},{24,28},{28,24},{1,5},{5... | collective-permute-start | bytes 264200 | tf_op jit(solution)/shard_map/ppermute | solution.py:898
  252.0 10.1 %collective-permute-start.27 = (bf16[256,1024]{1,0:T(8,128)(2,1)}, bf16[256,1024]{1,0:T(8,128)(2,1)S(1)}, u32[]{:S(2)}, u32[]{:S(2)}) collective-permute-start(bf16[256,1024]{1,0:T(8,128)(2,1)} %collective-permute-done.26), channel_id=1, source_target_pairs={{0,1},{1,0},{2,3},{3,2},{4,5},{5,4},{6,7},{7,6},{8,9},{9,8},{10,11... | collective-permute-start | bytes 1572872 | tf_op jit(solution)/shard_map/ppermute | solution.py:898
  252.0 105.1 %collective-permute-start.31 = (bf16[2,256,1024]{2,1,0:T(8,128)(2,1)}, bf16[2,256,1024]{2,1,0:T(8,128)(2,1)}, u32[]{:S(2)}, u32[]{:S(2)}) collective-permute-start(bf16[2,256,1024]{2,1,0:T(8,128)(2,1)} %get-tuple-element.119), channel_id=1, source_target_pairs={{0,1},{1,0},{2,3},{3,2},{4,5},{5,4},{6,7},{7,6},{8,9},{9,8},{10,11... | collective-permute-start | bytes 3145736 | tf_op jit(solution)/shard_map/ppermute | solution.py:898
  254.2 38.5 %collective-permute-start.32 = (f32[8,2752]{1,0:T(8,128)}, f32[8,2752]{1,0:T(8,128)S(1)}, u32[]{:S(2)}, u32[]{:S(2)}) collective-permute-start(f32[8,2752]{1,0:T(8,128)} %add_after.9.refs_10_.refs_0_), channel_id=1, source_target_pairs={{0,8},{4,12},{8,0},{12,4},{16,24},{20,28},{24,16},{28,20},{1,9},{5... | collective-permute-start | bytes 264200 | tf_op jit(solution)/shard_map/ppermute | solution.py:898
  261.0 38.2 %collective-permute-start.33 = (bf16[256,1024]{1,0:T(8,128)(2,1)}, bf16[256,1024]{1,0:T(8,128)(2,1)S(1)}, u32[]{:S(2)}, u32[]{:S(2)}) collective-permute-start(bf16[256,1024]{1,0:T(8,128)(2,1)} %pass_on.11.refs_11_), channel_id=1, source_target_pairs={{0,2},{1,3},{2,0},{3,1},{4,6},{5,7},{6,4},{7,5},{8,10},{9,11},{10,... | collective-permute-start | bytes 1572872 | tf_op jit(solution)/shard_map/ppermute | solution.py:898
  295.0 51.6 %collective-permute-start.38 = (f32[8,2752]{1,0:T(8,128)}, f32[8,2752]{1,0:T(8,128)S(1)}, u32[]{:S(2)}, u32[]{:S(2)}) collective-permute-start(f32[8,2752]{1,0:T(8,128)} %add_after.10.refs_10_.refs_0_), channel_id=1, source_target_pairs={{0,16},{4,20},{8,24},{12,28},{16,0},{20,4},{24,8},{28,12},{1,17},{... | collective-permute-start | bytes 264200 | tf_op jit(solution)/shard_map/ppermute | solution.py:898
  297.7 192.3 %collective-permute-start.30 = (bf16[256,1024]{1,0:T(8,128)(2,1)}, bf16[256,1024]{1,0:T(8,128)(2,1)}, u32[]{:S(2)}, u32[]{:S(2)}) collective-permute-start(bf16[256,1024]{1,0:T(8,128)(2,1)} %pass_on.12), channel_id=1, source_target_pairs={{0,2},{1,3},{2,0},{3,1},{4,6},{5,7},{6,4},{7,5},{8,10},{9,11},{10,... | collective-permute-start | bytes 1572872 | tf_op jit(solution)/shard_map/ppermute | solution.py:898
  303.8 55.1 %collective-permute-start.36 = (bf16[256,1024]{1,0:T(8,128)(2,1)}, bf16[256,1024]{1,0:T(8,128)(2,1)}, u32[]{:S(2)}, u32[]{:S(2)}) collective-permute-start(bf16[256,1024]{1,0:T(8,128)(2,1)} %get-tuple-element.121.refs_11_), channel_id=1, source_target_pairs={{0,2},{1,3},{2,0},{3,1},{4,6},{5,7},{6,4},{7,5},{8,10},{9,11},{10,... | collective-permute-start | bytes 1572872 | tf_op jit(solution)/shard_map/ppermute | solution.py:898
  304.4 26.9 %copy-start.110 = (bf16[4,128,1024]{2,1,0:T(8,128)(2,1)S(1)}, bf16[4,128,1024]{2,1,0:T(8,128)(2,1)}, u32[]{:S(2)}) copy-start(bf16[4,128,1024]{2,1,0:T(8,128)(2,1)} %get-tuple-element.127) | copy-start | bytes 3145732
  340.4 24.4 %collective-permute-start.45 = (bf16[2,256,1024]{2,1,0:T(8,128)(2,1)}, bf16[2,256,1024]{2,1,0:T(8,128)(2,1)S(1)}, u32[]{:S(2)}, u32[]{:S(2)}) collective-permute-start(bf16[2,256,1024]{2,1,0:T(8,128)(2,1)} %get-tuple-element.278), channel_id=1, source_target_pairs={{0,1},{1,0},{2,3},{3,2},{4,5},{5,4},{6,7},{7,6},{8,9},{9,8},{10,11... | collective-permute-start | bytes 3145736 | tf_op jit(solution)/shard_map/ppermute | solution.py:898
  346.6 15.8 %collective-permute-start.35 = (bf16[256,1024]{1,0:T(8,128)(2,1)}, bf16[256,1024]{1,0:T(8,128)(2,1)S(1)}, u32[]{:S(2)}, u32[]{:S(2)}) collective-permute-start(bf16[256,1024]{1,0:T(8,128)(2,1)} %get-tuple-element.121.refs_11_), channel_id=1, source_target_pairs={{0,1},{1,0},{2,3},{3,2},{4,5},{5,4},{6,7},{7,6},{8,9},{9,8},{10,11... | collective-permute-start | bytes 1572872 | tf_op jit(solution)/shard_map/ppermute | solution.py:898
  357.1 48.6 %collective-permute-start.39 = (f32[8,2432]{1,0:T(8,128)}, f32[8,2432]{1,0:T(8,128)S(1)}, u32[]{:S(2)}, u32[]{:S(2)}) collective-permute-start(f32[8,2432]{1,0:T(8,128)} %get-tuple-element.124.refs_10_.refs_0_), channel_id=1, source_target_pairs={{0,4},{4,0},{8,12},{12,8},{16,20},{20,16},{24,28},{28,24},{1,5},{5... | collective-permute-start | bytes 233480 | tf_op jit(solution)/shard_map/ppermute | solution.py:898
  358.9 9.9 %collective-permute-start.37 = (bf16[256,1024]{1,0:T(8,128)(2,1)}, bf16[256,1024]{1,0:T(8,128)(2,1)S(1)}, u32[]{:S(2)}, u32[]{:S(2)}) collective-permute-start(bf16[256,1024]{1,0:T(8,128)(2,1)} %collective-permute-done.36), channel_id=1, source_target_pairs={{0,1},{1,0},{2,3},{3,2},{4,5},{5,4},{6,7},{7,6},{8,9},{9,8},{10,11... | collective-permute-start | bytes 1572872 | tf_op jit(solution)/shard_map/ppermute | solution.py:898
  362.3 128.5 %collective-permute-start.34 = (bf16[256,1024]{1,0:T(8,128)(2,1)}, bf16[256,1024]{1,0:T(8,128)(2,1)}, u32[]{:S(2)}, u32[]{:S(2)}) collective-permute-start(bf16[256,1024]{1,0:T(8,128)(2,1)} %pass_on.13), channel_id=1, source_target_pairs={{0,2},{1,3},{2,0},{3,1},{4,6},{5,7},{6,4},{7,5},{8,10},{9,11},{10,... | collective-permute-start | bytes 1572872 | tf_op jit(solution)/shard_map/ppermute | solution.py:898
  368.0 152.1 %collective-permute-start.46 = (bf16[256,1024]{1,0:T(8,128)(2,1)}, bf16[256,1024]{1,0:T(8,128)(2,1)S(1)}, u32[]{:S(2)}, u32[]{:S(2)}) collective-permute-start(bf16[256,1024]{1,0:T(8,128)(2,1)} %pass_on.15), channel_id=1, source_target_pairs={{0,2},{1,3},{2,0},{3,1},{4,6},{5,7},{6,4},{7,5},{8,10},{9,11},{10,... | collective-permute-start | bytes 1572872 | tf_op jit(solution)/shard_map/ppermute | solution.py:898
  433.4 12.2 %collective-permute-start.40 = (f32[8,4352]{1,0:T(8,128)}, f32[8,4352]{1,0:T(8,128)S(1)}, u32[]{:S(2)}, u32[]{:S(2)}) collective-permute-start(f32[8,4352]{1,0:T(8,128)} %get-tuple-element.131.refs_0_), channel_id=1, source_target_pairs={{0,4},{4,0},{8,12},{12,8},{16,20},{20,16},{24,28},{28,24},{1,5},{5... | collective-permute-start | bytes 417800 | tf_op jit(solution)/shard_map/ppermute | solution.py:898
  458.1 1.7 collective-permute-start.47
  458.2 9.2 %collective-permute-start.41 = (f32[8,4352]{1,0:T(8,128)S(1)}, f32[8,4352]{1,0:T(8,128)S(1)}, u32[]{:S(2)}, u32[]{:S(2)}) collective-permute-start(f32[8,4352]{1,0:T(8,128)S(1)} %copy-done.25), channel_id=1, source_target_pairs={{0,8},{4,12},{8,0},{12,4},{16,24},{20,28},{24,16},{28,20},{1,9},{5... | collective-permute-start | bytes 417800 | tf_op jit(solution)/shard_map/ppermute | solution.py:898
  461.7 3.9 collective-permute-start.48
  465.6 21.0 %collective-permute-start.54 = (f32[8,2432]{1,0:T(8,128)S(1)}, f32[8,2432]{1,0:T(8,128)S(1)}, u32[]{:S(2)}, u32[]{:S(2)}) collective-permute-start(f32[8,2432]{1,0:T(8,128)S(1)} %copy-done.97), channel_id=1, source_target_pairs={{0,8},{4,12},{8,0},{12,4},{16,24},{20,28},{24,16},{28,20},{1,9},{5... | collective-permute-start | bytes 233480 | tf_op jit(solution)/shard_map/ppermute | solution.py:898
  470.6 8.8 %collective-permute-start.42 = (f32[8,4352]{1,0:T(8,128)S(1)}, f32[8,4352]{1,0:T(8,128)S(1)}, u32[]{:S(2)}, u32[]{:S(2)}) collective-permute-start(f32[8,4352]{1,0:T(8,128)S(1)} %copy-done.19), channel_id=1, source_target_pairs={{0,16},{4,20},{8,24},{12,28},{16,0},{20,4},{24,8},{28,12},{1,17},{... | collective-permute-start | bytes 417800 | tf_op jit(solution)/shard_map/ppermute | solution.py:898
  479.4 16.9 %collective-permute-start.50 = (f32[58,128]{1,0:T(8,128)S(1)}, f32[58,128]{1,0:T(8,128)S(1)}, u32[]{:S(2)}, u32[]{:S(2)}) collective-permute-start(f32[58,128]{1,0:T(8,128)S(1)} %pad_maximum_fusion.6.refs_1_), channel_id=1, source_target_pairs={{0,4},{4,0},{8,12},{12,8},{16,20},{20,16},{24,28},{28,24},{1,5},{5... | collective-permute-start | bytes 89096 | tf_op jit(solution)/shard_map/ppermute | solution.py:898
  486.5 43.1 %collective-permute-start.43 = (bf16[2,256,1024]{2,1,0:T(8,128)(2,1)S(1)}, bf16[2,256,1024]{2,1,0:T(8,128)(2,1)S(1)}, u32[]{:S(2)}, u32[]{:S(2)}) collective-permute-start(bf16[2,256,1024]{2,1,0:T(8,128)(2,1)S(1)} %get-tuple-element.280), channel_id=1, source_target_pairs={{0,1},{1,0},{2,3},{3,2},{4,5},{5,4},{6,7},{7,6},{8,9},{9,8},{10,11... | collective-permute-start | bytes 3145736 | tf_op jit(solution)/shard_map/ppermute | solution.py:898
  490.0 6.3 %collective-permute-start.49 = (f32[8,2048]{1,0:T(8,128)S(1)}, f32[8,2048]{1,0:T(8,128)S(1)}, u32[]{:S(2)}, u32[]{:S(2)}) collective-permute-start(f32[8,2048]{1,0:T(8,128)S(1)} %copy-done.37), channel_id=1, source_target_pairs={{0,4},{4,0},{8,12},{12,8},{16,20},{20,16},{24,28},{28,24},{1,5},{5... | collective-permute-start | bytes 196616 | tf_op jit(solution)/shard_map/ppermute | solution.py:898
  490.8 10.3 %collective-permute-start.55 = (f32[8,2432]{1,0:T(8,128)}, f32[8,2432]{1,0:T(8,128)S(1)}, u32[]{:S(2)}, u32[]{:S(2)}) collective-permute-start(f32[8,2432]{1,0:T(8,128)} %add_after.17.refs_1_), channel_id=1, source_target_pairs={{0,16},{4,20},{8,24},{12,28},{16,0},{20,4},{24,8},{28,12},{1,17},{... | collective-permute-start | bytes 233480 | tf_op jit(solution)/shard_map/ppermute | solution.py:898
  499.1 16.4 %collective-permute-start.51 = (f32[8,2048]{1,0:T(8,128)}, f32[8,2048]{1,0:T(8,128)S(1)}, u32[]{:S(2)}, u32[]{:S(2)}) collective-permute-start(f32[8,2048]{1,0:T(8,128)} %get-tuple-element.147.refs_0_), channel_id=1, source_target_pairs={{0,8},{4,12},{8,0},{12,4},{16,24},{20,28},{24,16},{28,20},{1,9},{5... | collective-permute-start | bytes 196616 | tf_op jit(solution)/shard_map/ppermute | solution.py:898
  500.1 15.4 %collective-permute-start.52 = (f32[58,128]{1,0:T(8,128)}, f32[58,128]{1,0:T(8,128)S(1)}, u32[]{:S(2)}, u32[]{:S(2)}) collective-permute-start(f32[58,128]{1,0:T(8,128)} %get-tuple-element.148.refs_1_), channel_id=1, source_target_pairs={{0,8},{4,12},{8,0},{12,4},{16,24},{20,28},{24,16},{28,20},{1,9},{5... | collective-permute-start | bytes 89096 | tf_op jit(solution)/shard_map/ppermute | solution.py:898
  518.2 8.2 %collective-permute-start.56 = (f32[58,128]{1,0:T(8,128)}, f32[58,128]{1,0:T(8,128)S(1)}, u32[]{:S(2)}, u32[]{:S(2)}) collective-permute-start(f32[58,128]{1,0:T(8,128)} %get-tuple-element.161), channel_id=1, source_target_pairs={{0,16},{4,20},{8,24},{12,28},{16,0},{20,4},{24,8},{28,12},{1,17},{... | collective-permute-start | bytes 89096 | tf_op jit(solution)/shard_map/ppermute | solution.py:898
  524.7 9.0 %collective-permute-start.53 = (f32[8,2048]{1,0:T(8,128)S(1)}, f32[8,2048]{1,0:T(8,128)S(1)}, u32[]{:S(2)}, u32[]{:S(2)}) collective-permute-start(f32[8,2048]{1,0:T(8,128)S(1)} %copy-done.51), channel_id=1, source_target_pairs={{0,16},{4,20},{8,24},{12,28},{16,0},{20,4},{24,8},{28,12},{1,17},{... | collective-permute-start | bytes 196616 | tf_op jit(solution)/shard_map/ppermute | solution.py:898
  532.8 12.6 %collective-permute-start.44 = (bf16[256,1024]{1,0:T(8,128)(2,1)}, bf16[256,1024]{1,0:T(8,128)(2,1)S(1)}, u32[]{:S(2)}, u32[]{:S(2)}) collective-permute-start(bf16[256,1024]{1,0:T(8,128)(2,1)} %pass_on.14.refs_8_), channel_id=1, source_target_pairs={{0,2},{1,3},{2,0},{3,1},{4,6},{5,7},{6,4},{7,5},{8,10},{9,11},{10,... | collective-permute-start | bytes 1572872 | tf_op jit(solution)/shard_map/ppermute | solution.py:898
  (110 other events, 511.2 us)
Sparse Core Ops, SparseCore 0:
  10.8 57.4 all-gather.2
  71.0 78.4 all-gather.4

commit v4 on v3

--- a/solution.py
+++ b/solution.py
@@ -694,22 +694,29 @@
     return call(body, "add_rows", inputs, [(shape, BF)], deps)[0]
 
 
-def ffn_pass(rows, grads, w_ff, basis_ff, basis_down, deps=()):
+def ffn_pass(rows, grads, w_ff, basis_ff, basis_down, old=None, deps=()):
     share, width = rows[0].shape
     total = 4 * share
     hidden_width = w_ff.shape[2]
     rank = basis_ff.shape[1]
     tile = 2 * share
+    pieces = len(rows)
+    steps = pieces // 2
+    first = 0 if old is None else 1
 
     def body(*refs):
-        row_refs, grad_refs = refs[:4], refs[4:8]
-        ff_ref, bff_ref, bdown_ref = refs[8:11]
-        hidden_ref, dgu_ref, two_keep, two_send, ffn_keep, ffn_send, left_ff, left_down, x_s, dy_s = refs[11:]
-        for k in range(4):
+        row_refs, grad_refs = refs[:pieces], refs[pieces : 2 * pieces]
+        ff_ref, bff_ref, bdown_ref = refs[2 * pieces : 2 * pieces + 3]
+        left_ff, left_down, hidden_ref, dgu_ref, two_keep, two_send, ffn_keep, ffn_send, x_s, dy_s = refs[-10:]
+        for k in range(pieces):
             x_s[k * share : (k + 1) * share, :] = row_refs[k][...]
             dy_s[k * share : (k + 1) * share, :] = grad_refs[k][...]
-        left_ff[...] = jnp.zeros_like(left_ff)
-        left_down[...] = jnp.zeros_like(left_down)
+        if old is None:
+            left_ff[...] = jnp.zeros_like(left_ff)
+            left_down[...] = jnp.zeros_like(left_down)
+        else:
+            left_ff[...] = refs[2 * pieces + 3][...]
+            left_down[...] = refs[2 * pieces + 4][...]
 
         def step(i):
             at = slice(i * tile, (i + 1) * tile)
@@ -737,18 +744,41 @@
             inner = halves(nt(high_low(bdown_ref[...]), dy))
             left_down[...] += halves(mm(high_low(inner), hidden))
 
-        for i in range(2):
+        for i in range(steps):
             step(i)
 
+    whole = pl.BlockSpec(memory_space=pltpu.VMEM)
     pair = ((2, share, width), BF)
-    return call(
-        body, "ffn_pass", [*rows, *grads, w_ff, basis_ff, basis_down],
-        [
-            ((total, hidden_width), BF), ((2, total, hidden_width), BF), pair, pair, pair, pair,
-            ((2, rank, width), F32), ((rank, hidden_width), F32), ((total, width), BF), ((total, width), BF),
-        ],
-        deps, cost=12,
-    )
+    outs = [
+        ((2, rank, width), F32), ((rank, hidden_width), F32),
+        ((total, hidden_width), BF), ((2, total, hidden_width), BF), pair, pair, pair, pair,
+        ((total, width), BF), ((total, width), BF),
+    ]
+    tall = pl.BlockSpec((steps * tile, width), lambda g: (first, 0))
+    part = pl.BlockSpec((steps, share, width), lambda g: (first, 0, 0))
+    out_specs = [
+        whole, whole,
+        pl.BlockSpec((steps * tile, hidden_width), lambda g: (first, 0)),
+        pl.BlockSpec((2, steps * tile, hidden_width), lambda g: (0, first, 0)),
+        part, part, part, part, tall, tall,
+    ]
+    inputs = [*rows, *grads, w_ff, basis_ff, basis_down]
+    kept, aliases = [], {}
+    if old is not None:
+        inputs += old[:2]
+        kept = list(old[2:])
+        aliases = {len(inputs) + k: 2 + k for k in range(len(kept))}
+    return pl.pallas_call(
+        body,
+        grid=(1,),
+        in_specs=[whole] * len(inputs) + any_specs(kept) + any_specs(deps),
+        out_specs=out_specs,
+        out_shape=[jax.ShapeDtypeStruct(*o) for o in outs],
+        input_output_aliases=aliases,
+        compiler_params=pltpu.CompilerParams(vmem_limit_bytes=56 * 2**20),
+        cost_estimate=pl.CostEstimate(flops=6 * steps * 10**9, bytes_accessed=18 * steps * 10**6, transcendentals=0),
+        name="ffn_pass",
+    )(*inputs, *kept, *deps)
 
 
 momentum_decay = 0.5
@@ -1023,10 +1053,13 @@
     hidden, d_gate_up, two_keep, two_beside, two_passed, ffn_parts, left_ff, left_down = [[] for i in range(8)]
     rows_of_two, rows_of_dy = [], []
 
-    def feed_forward(m, deps):
-        h, dgu, keep, send, ffn_keep, ffn_send, lf, ld, rows_two, rows_dy = ffn_pass(
-            group_two[m], pieces_dy[m], weights_ff, bases[2], bases[3][0], deps
-        )
+    def feed_forward(m, deps, early=None):
+        if early is None:
+            parts = ffn_pass(group_two[m], pieces_dy[m], weights_ff, bases[2], bases[3][0], None, deps)
+        else:
+            parts = ffn_pass(group_two[m][:2], pieces_dy[m][:2], weights_ff, bases[2], bases[3][0], None, early)
+            parts = ffn_pass(group_two[m][2:], pieces_dy[m][2:], weights_ff, bases[2], bases[3][0], parts, deps)
+        lf, ld, h, dgu, keep, send, ffn_keep, ffn_send, rows_two, rows_dy = parts
         hidden.append(h)
         d_gate_up.append(dgu)
         two_keep.append(keep)
@@ -1061,7 +1094,7 @@
     grads_first = weight_grads(0)
     norm_two(1, grads_first)
     pass_two(0, (group_two[1][2],))
-    sent = feed_forward(1, (two_passed[0],))
+    sent = feed_forward(1, (two_passed[0],), (send_two[1],))
     back_two(0, (sent,))
     pass_two(1, (send_back[0],))
     grads_last = weight_grads(1)

time: 568 us -> 572 us (level)
  Pallas kernels: 276 us -> 283 us
    pallas_call x0 -> x3, Pallas kernels: none -> 45.3 us  [ffn_pass(): pl.pallas_call(body, grid=(1,), in_specs=[whole] * len(inputs) + any_spec...]
    pallas_call x31 -> x29, Pallas kernels: 129 us -> 90.9 us  [call(): pl.pallas_call(kernel, grid=(1,), in_specs=kinds + any_specs(deps), out_s...]
    unnamed x242 -> x246, local copies, waits for them, and re-layouts: 31.3 us -> 32.2 us
  transfers between devices with their start and end apart: 59 -> 59, of which waited for: 8 -> 8; matrix products, arithmetic and copies ran while one was open for 27% -> 27% of each run, Pallas kernels for 49% -> 50%
where the time goes in v4:
time: 572 us; the launch traced here: 561 us
  Pallas kernels  283 us (49%)
  matrix products  114 us (20%)
  local copies, waits for them, and re-layouts  50.7 us (9%)
  waiting for transfers between devices  43.4 us (8%)
  starting transfers between devices  40.5 us (7%)
  between operations  15.7 us (3%)
  other arithmetic  13 us (2%)
    pallas_call x8, Pallas kernels, mixer_call(): pl.pallas_call(body, grid=(1,), in_specs=in_specs, out_specs=out_specs, o...  140 us
    dot_general x30, matrix products, dot32(): return jnp.einsum(spec, a, b, preferred_element_type=jnp.float32)  110 us
    pallas_call x29, Pallas kernels, call(): pl.pallas_call(kernel, grid=(1,), in_specs=kinds + any_specs(deps), out_s...  90.9 us
    pallas_call x3, Pallas kernels, ffn_pass(): pl.pallas_call(body, grid=(1,), in_specs=[whole] * len(inputs) + any_spec...  45.3 us
    ppermute x57, starting transfers between devices, swap(): return lax.ppermute(value, axis, [(i, i ^ flip) for i in range(count)])  40.5 us
    unnamed x246, local copies, waits for them, and re-layouts  32.2 us
    ppermute x57, waiting for transfers between devices, swap(): return lax.ppermute(value, axis, [(i, i ^ flip) for i in range(count)])  28.6 us
    all_gather x1, waiting for transfers between devices, on_device(): weights_first = lax.all_gather(first, 'dp', axis=1, tiled=True)  14.8 us
  transfers between devices with their start and end apart: 59, of which 8 were waited for; matrix products, arithmetic and copies ran while one was open for 27% of the time, Pallas kernels for 50%

profile of v4, /device:TPU:0, one launch (start us, length us, event | category | flops | bytes accessed | tf_op | source)
XLA Modules:
  0.0 560.7 jit_solution(11210803072072191558)
XLA Ops:
  12.5 2.9 collective-permute-start.1
  18.0 4.1 sketches.4.refs_7_
  22.1 6.4 %collective-permute-done.1 = bf16[256,1024]{1,0:T(8,128)(2,1)} collective-permute-done((bf16[256,1024]{1,0:T(8,128)(2,1)}, bf16[256,1024]{1,0:T(8,128)(2,1)}, u32[]{:S(2)}, u32[]{:S(2)}) %collective-permute-start.1) | collective-permute-done | bytes 524320 | tf_op jit(solution)/shard_map/ppermute | solution.py:928
  28.6 6.1 %sketches.3.refs_6_ = f32[8,2752]{1,0:T(8,128)} custom-call(f32[2,704,1024]{2,1,0:T(8,128)} %bitcast.267, f32[1,704,1024]{2,1,0:T(8,128)} %refs_1_.1, f32[2,8,704]{2,1,0:T(8,128)} %bitcast.284, f32[1,8,1024]{2,1,0:T(8,128)} %bitcast.288), custom_call_target="tpu_custom_call" | custom-call | flops 1000000000 | bytes 3000000 | tf_op jit(solution)/shard_map/sketches/pallas_call | solution.py:604
  40.7 4.2 fusion.55.refs_6_
  48.3 5.0 fusion.56.refs_8_.refs_6_
  53.4 14.8 %all-gather.3.cloned.1.call-done = bf16[5,1024,256]{2,1,0:T(8,128)(2,1)} async-done(((bf16[5,128,256]{2,1,0:T(8,128)(2,1)}), bf16[5,1024,256]{2,1,0:T(8,128)(2,1)}) %all-gather.3.cloned.1.call-update) | async-done | bytes 2621456 | tf_op jit(solution)/shard_map/all_gather | solution.py:986
  68.2 6.6 %fusion.29.refs_0_ = f32[4,256,1024]{2,1,0:T(8,128)} fusion(bf16[5,1024,256]{2,1,0:T(8,128)(2,1)} %all-gather.3.cloned.1.call-done, bf16[1024,1024]{1,0:T(8,128)(2,1)} %copy-done.10), kind=kOutput, calls=%fused_computation.38 | convolution fusion | flops 2147483648 | bytes 8912896 | tf_op jit(solution)/shard_map/jdc,td->jct/dot_general | solution.py:943
  74.8 9.9 %mixer_forward.4 = bf16[128,1024]{1,0:T(8,128)(2,1)} custom-call(f32[4,256,1024]{2,1,0:T(8,128)} %fusion.29.refs_0_, f32[2,1,1024]{2,1,0:T(1,128)} %broadcast_in_dim.36.refs_1_, f32[3,256,4]{2,1,0:T(8,128)} %bitcast.274, f32[1,1024]{1,0:T(1,128)} %get-tuple-element.335.refs_3_, s32[3]{0:T(128)} %get-tuple-element.341.refs_4_.refs_8_, f32[2,2]{1,0:T(2,128)} %refs_9_.7, ...), custom_call_target="tpu_custom_call" | custom-call | flops 11000000512 | bytes 33000000 | tf_op jit(solution)/shard_map/mixer_forward/pallas_call | solution.py:565
  84.7 9.8 %mixer_forward.5 = bf16[128,1024]{1,0:T(8,128)(2,1)} custom-call(f32[4,256,1024]{2,1,0:T(8,128)} %fusion.29.refs_0_, f32[2,1,1024]{2,1,0:T(1,128)} %broadcast_in_dim.36.refs_1_, f32[3,256,4]{2,1,0:T(8,128)} %bitcast.275, f32[1,1024]{1,0:T(1,128)} %get-tuple-element.335.refs_3_, s32[3]{0:T(128)} %get-tuple-element.341.refs_4_.refs_8_, f32[2,2]{1,0:T(2,128)} %refs_9_.7, ...), custom_call_target="tpu_custom_call" | custom-call | flops 11000000512 | bytes 33000000 | tf_op jit(solution)/shard_map/mixer_forward/pallas_call | solution.py:565
  94.5 2.0 fusion.62
  103.6 2.2 convolution_bitcast_fusion.1
  106.5 6.0 %fusion.27.refs_2_.refs_0_ = f32[4,256,1024]{2,1,0:T(8,128)} fusion(bf16[5,1024,256]{2,1,0:T(8,128)(2,1)} %all-gather.3.cloned.1.call-done, bf16[1024,1024]{1,0:T(8,128)(2,1)S(1)} %copy-done.9), kind=kOutput, calls=%fused_computation.36 | convolution fusion | flops 2147483648 | bytes 8912896 | tf_op jit(solution)/shard_map/jdc,td->jct/dot_general | solution.py:943
  112.6 2.1 pass_on.8.refs_6_
  115.5 9.8 %mixer_forward.6.refs_5_ = bf16[128,1024]{1,0:T(8,128)(2,1)} custom-call(f32[4,256,1024]{2,1,0:T(8,128)} %fusion.27.refs_2_.refs_0_, f32[2,1,1024]{2,1,0:T(1,128)} %broadcast_in_dim.37.refs_1_, f32[3,256,4]{2,1,0:T(8,128)} %bitcast.276, f32[1,1024]{1,0:T(1,128)} %get-tuple-element.334.refs_3_, s32[3]{0:T(128)} %get-tuple-element.340.refs_4_.refs_8_, ...), custom_call_target="tpu_custom_call" | custom-call | flops 11000000512 | bytes 33000000 | tf_op jit(solution)/shard_map/mixer_forward/pallas_call | solution.py:565
  125.3 3.9 collective-permute-done.7.refs_3_
  130.0 2.9 second_norm.2
  133.8 9.6 %mixer_forward.7 = bf16[128,1024]{1,0:T(8,128)(2,1)} custom-call(f32[4,256,1024]{2,1,0:T(8,128)} %fusion.27.refs_2_.refs_0_, f32[2,1,1024]{2,1,0:T(1,128)} %broadcast_in_dim.37.refs_1_, f32[3,256,4]{2,1,0:T(8,128)} %bitcast.277, f32[1,1024]{1,0:T(1,128)} %get-tuple-element.334.refs_3_, s32[3]{0:T(128)} %get-tuple-element.340.refs_4_.refs_8_, ...), custom_call_target="tpu_custom_call" | custom-call | flops 11000000512 | bytes 33000000 | tf_op jit(solution)/shard_map/mixer_forward/pallas_call | solution.py:565
  143.4 2.0 fusion.63
  146.8 2.0 convolution_convert_fusion
  151.2 19.6 %ffn_pass.3 = (f32[2,8,1024]{2,1,0:T(8,128)}, f32[8,704]{1,0:T(8,128)}, bf16[1024,704]{1,0:T(8,128)(2,1)}, bf16[2,1024,704]{2,1,0:T(8,128)(2,1)}, bf16[2,256,102...) custom-call(bf16[256,1024]{1,0:T(8,128)(2,1)} %get-tuple-element.105, ...), custom_call_target="tpu_custom_call" | custom-call | flops 12000000000 | bytes 36000000 | tf_op jit(solution)/shard_map/ffn_pass/pallas_call | solution.py:771
  171.2 2.3 pass_on.9
  174.2 6.9 %fusion.25.refs_5_ = f32[2,704,1024]{2,1,0:T(8,128)} fusion(bf16[2,1024,704]{2,1,0:T(8,128)(2,1)S(1)} %copy-done.111, bf16[1024,1024]{1,0:T(8,128)(2,1)} %get-tuple-element.111), kind=kOutput, calls=%fused_computation.34 | convolution fusion | flops 2952790016 | bytes 10747904 | tf_op jit(solution)/shard_map/jth,td->jhd/dot_general | solution.py:943
  181.1 3.3 fusion.123.refs_6_
  184.4 3.3 collective-permute-done.17.refs_3_
  188.5 3.0 second_norm.3
  196.1 8.9 %collective-permute-done.18.refs_2_.refs_0_ = bf16[256,1024]{1,0:T(8,128)(2,1)S(1)} collective-permute-done((bf16[256,1024]{1,0:T(8,128)(2,1)}, bf16[256,1024]{1,0:T(8,128)(2,1)S(1)}, u32[]{:S(2)}, u32[]{:S(2)}) %collective-permute-start.18) | collective-permute-done | bytes 524320 | tf_op jit(solution)/shard_map/ppermute | solution.py:928
  205.8 2.1 pass_on.10.refs_17_
  208.7 12.6 %ffn_pass.4 = (f32[2,8,1024]{2,1,0:T(8,128)}, f32[8,704]{1,0:T(8,128)}, bf16[1024,704]{1,0:T(8,128)(2,1)}, bf16[2,1024,704]{2,1,0:T(8,128)(2,1)}, bf16[2,256,102...) custom-call(bf16[256,1024]{1,0:T(8,128)(2,1)} %get-tuple-element.114, ...), custom_call_target="tpu_custom_call" | custom-call | flops 6000000000 | bytes 18000000 | tf_op jit(solution)/shard_map/ffn_pass/pallas_call | solution.py:771
  222.3 13.0 %ffn_pass.5 = (f32[2,8,1024]{2,1,0:T(8,128)}, f32[8,704]{1,0:T(8,128)}, bf16[1024,704]{1,0:T(8,128)(2,1)}, bf16[2,1024,704]{2,1,0:T(8,128)(2,1)}, bf16[2,256,102...) custom-call(bf16[256,1024]{1,0:T(8,128)(2,1)} %copy-done.90, ...), custom_call_target="tpu_custom_call", output_to_operand_aliasing={{2}: (9, {}), {3}: (10, {}), {4}: (11, {}), {5}: (12, {}), ... | custom-call | flops 6000000000 | bytes 18000000 | tf_op jit(solution)/shard_map/ffn_pass/pallas_call | solution.py:771
  236.5 3.8 norm_back.2
  242.6 10.1 %add_add_fusion.refs_2_.refs_6_ = f32[2,704,1024]{2,1,0:T(8,128)} fusion(f32[2,704,1024]{2,1,0:T(8,128)} %fusion.25.refs_5_, bf16[2,1024,704]{2,1,0:T(8,128)(2,1)} %get-tuple-element.131, bf16[1024,1024]{1,0:T(8,128)(2,1)} %get-tuple-element.132, f32[1,2,1024,704]{2,3,1,0:T(8,128)S(1)} %bitcast.269), kind=kOutput, calls=%fused_computation | convolution fusion | flops 2955673600 | bytes 22282240 | tf_op jit(solution)/shard_map/jth,td->jhd/dot_general | solution.py:943
  252.8 3.4 bitcast_add_fusion.3.refs_3_.refs_7_
  263.1 2.1 pass_on.11.refs_11_
  266.3 5.3 fusion.33.refs_4_
  271.7 25.2 %mixer_backward.4 = (bf16[4,128,1024]{2,1,0:T(8,128)(2,1)}, f32[1,1,1024]{2,1,0:T(1,128)}, f32[3,128,4]{2,1,0:T(8,128)}, f32[1,1,128]{2,1,0:T(1,128)}, f32[8,4096]{1,0:T(8,128)}) custom-call(f32[4,256,1024]{2,1,0:T(8,128)} %fusion.29.refs_0_, f32[2,1,1024]{2,1,0:T(1,128)} %broadcast_in_dim.36.refs_1_, f32[3,256,4]{2,1,0:T(8,128)} %bitcast.278, ...), custom_call_target="tpu_custom_call" | custom-call | flops 28000000000 | bytes 84000000 | tf_op jit(solution)/shard_map/mixer_backward/pallas_call | solution.py:565
  299.6 2.1 pass_on.12
  304.1 3.8 norm_back.3
  308.4 25.4 %mixer_backward.5 = (bf16[4,128,1024]{2,1,0:T(8,128)(2,1)}, f32[1,1,1024]{2,1,0:T(1,128)}, f32[3,128,4]{2,1,0:T(8,128)}, f32[1,1,128]{2,1,0:T(1,128)}, f32[8,4096]{1,0:T(8,128)}) custom-call(f32[4,256,1024]{2,1,0:T(8,128)} %fusion.29.refs_0_, f32[2,1,1024]{2,1,0:T(1,128)} %broadcast_in_dim.36.refs_1_, f32[3,256,4]{2,1,0:T(8,128)} %bitcast.279, ...), custom_call_target="tpu_custom_call" | custom-call | flops 28000000000 | bytes 84000000 | tf_op jit(solution)/shard_map/mixer_backward/pallas_call | solution.py:565
  335.3 3.9 fusion.50
  339.2 2.4 fusion.57
  344.4 6.0 %convolution_bitcast_fusion.refs_11_ = f32[4,1024,256]{2,1,0:T(8,128)} fusion(bf16[4,256,1024]{2,1,0:T(8,128)(2,1)S(1)} %fusion.50, bf16[256,1024]{1,0:T(8,128)(2,1)} %collective-permute-done.2, bf16[256,1024]{1,0:T(8,128)(2,1)} %collective-permute-done.1, bf16[256,1024]{1,0:T(8,128)(2,1)} %collective-permute-done, bf16[256,1024]{1,0:T(8,128)(2,1)} %get-tuple-element.311), kind=kOutput, calls=%fused_computation.22 | convolution fusion | flops 2155872256 | bytes 8388608 | tf_op jit(solution)/shard_map/id,kci->kdc/dot_general | solution.py:943
  351.2 8.5 %frames_and_basis.2 = (f32[8,2752]{1,0:T(8,128)}, f32[8,2432]{1,0:T(8,128)}) custom-call(f32[8,2752]{1,0:T(8,128)} %add_after.10.refs_10_.refs_0_, f32[8,2752]{1,0:T(8,128)} %copy-done.50, f32[2,704,1024]{2,1,0:T(8,128)} %add_add_fusion.refs_2_.refs_6_, f32[1,704,1024]{2,1,0:T(8,128)} %bitcast_add_fusion.3.refs_3_.refs_7_, ...), custom_call_target="tpu_custom_call" | custom-call | flops 1000000000 | bytes 3000000 | tf_op jit(solution)/shard_map/frames_and_basis/pallas_call | solution.py:604
  363.1 2.1 pass_on.13
  369.9 2.2 pass_on.15
  374.1 1.8 fusion.61.refs_0_.refs_3_.refs_7_
  375.9 2.3 sketches.5
  379.5 4.9 fusion.31.refs_4_
  384.5 25.3 %mixer_backward.6 = (bf16[4,128,1024]{2,1,0:T(8,128)(2,1)}, f32[1,1,1024]{2,1,0:T(1,128)}, f32[3,128,4]{2,1,0:T(8,128)}, f32[1,1,128]{2,1,0:T(1,128)}, f32[8,4352]{1,0:T(8,128)}) custom-call(f32[4,256,1024]{2,1,0:T(8,128)} %fusion.27.refs_2_.refs_0_, f32[2,1,1024]{2,1,0:T(1,128)} %broadcast_in_dim.37.refs_1_, f32[3,256,4]{2,1,0:T(8,128)} %bitcast.280, ...), custom_call_target="tpu_custom_call" | custom-call | flops 28000000000 | bytes 84000000 | tf_op jit(solution)/shard_map/mixer_backward/pallas_call | solution.py:565
  411.9 24.8 %mixer_backward.7 = (bf16[4,128,1024]{2,1,0:T(8,128)(2,1)}, f32[1,1,1024]{2,1,0:T(1,128)}, f32[3,128,4]{2,1,0:T(8,128)}, f32[1,1,128]{2,1,0:T(1,128)}, f32[8,4352]{1,0:T(8,128)}) custom-call(f32[4,256,1024]{2,1,0:T(8,128)} %fusion.27.refs_2_.refs_0_, f32[2,1,1024]{2,1,0:T(1,128)} %broadcast_in_dim.37.refs_1_, f32[3,256,4]{2,1,0:T(8,128)} %bitcast.281, ...), custom_call_target="tpu_custom_call" | custom-call | flops 28000000000 | bytes 84000000 | tf_op jit(solution)/shard_map/mixer_backward/pallas_call | solution.py:565
  438.9 2.8 fusion.125
  441.6 4.0 fusion.45.refs_2_.refs_0_
  447.4 2.0 fusion.80
  452.0 10.0 %multiply_reduce_fusion = (f32[1024]{0:T(1024)S(1)}, f32[4,1024,256]{2,1,0:T(8,128)}) fusion(bf16[5,1024,256]{2,1,0:T(8,128)(2,1)} %all-gather.3.cloned.1.call-done, f32[1,4,1024,256]{3,2,1,0:T(8,128)} %param.50, f32[4,1024,256]{2,1,0:T(8,128)} %convolution_bitcast_fusion.refs_11_, bf16[4,256,1024]{2,1,0:T(8,128)(2,1)} %gate.6.refs_0_, ...), kind=kOutput, calls=%fused_computation.6 | convolution fusion | flops 2161114112 | bytes 18878464 | tf_op jit(solution)/shard_map/id,kci->kdc/dot_general | solution.py:943
  466.6 3.0 collective-permute-done.48
  475.9 5.8 %fusion = bf16[1024,1024]{1,0:T(8,128)(2,1)S(1)} fusion(f32[1024,1024]{1,0:T(8,128)} %fusion.125, bf16[4,256,1024]{2,1,0:T(8,128)(2,1)} %gate.7, bf16[5,1024,256]{2,1,0:T(8,128)(2,1)} %all-gather.3.cloned.1.call-done), kind=kOutput, calls=%fused_computation.2 | convolution fusion | flops 2149580800 | bytes 10485760 | tf_op jit(solution)/shard_map/kci,kdc->id/dot_general | solution.py:943
  484.8 5.8 %frames_and_basis.3 = (f32[8,4352]{1,0:T(8,128)}, f32[8,2048]{1,0:T(8,128)}) custom-call(f32[8,4352]{1,0:T(8,128)} %add_after.13.refs_1_.refs_0_, f32[8,4352]{1,0:T(8,128)} %copy-done.44, f32[4,1024,256]{2,1,0:T(8,128)} %get-tuple-element.297.refs_2_.refs_6_, f32[1,256,1024]{2,1,0:T(8,128)} %fusion.61.refs_0_.refs_3_.refs_7_, bf16[2,2,256,1024]{3,2,1,0:T(8,128)(2,1)} %bitcast.266), custom_call_target="tpu_custom_call" | custom-call | flops 1000000000 | bytes 3000000 | tf_op jit(solution)/shard_map/frames_and_basis/pallas_call | solution.py:604
  496.4 3.9 add_rows.1.refs_10_
  505.7 9.1 %basis_and_errors.3 = (f32[8,2432]{1,0:T(8,128)}, f32[2,704,128]{2,1,0:T(8,128)}, f32[2,704,128]{2,1,0:T(8,128)}, f32[2,704,1024]{2,1,0:T(8,128)}, f32[1,704,1024]{2,1,0:T(8,128)}) custom-call(f32[8,2752]{1,0:T(8,128)} %get-tuple-element.175.refs_0_, f32[8,2432]{1,0:T(8,128)} %add_after.17.refs_1_, f32[8,2432]{1,0:T(8,128)} %copy-done.51, ...), custom_call_target="tpu_custom_call" | custom-call | flops 1000000000 | bytes 3000000 | tf_op jit(solution)/shard_map/basis_and_errors/pallas_call | solution.py:604
  516.2 2.3 fusion.122
  525.0 3.7 norm_back_into.2.refs_0_.refs_9_
  534.6 2.1 pass_on.14.refs_8_
  538.2 6.4 %basis_and_errors.2 = (f32[8,2048]{1,0:T(8,128)}, f32[4,128,256]{2,1,0:T(8,128)}, f32[4,128,256]{2,1,0:T(8,128)}, f32[4,1024,256]{2,1,0:T(8,128)}, f32[1,256,1024]{2,1,0:T(8,128)}) custom-call(f32[8,4352]{1,0:T(8,128)} %get-tuple-element.159.refs_0_, f32[8,2048]{1,0:T(8,128)} %get-tuple-element.169.refs_1_, f32[8,2048]{1,0:T(8,128)} %copy-done.53, ...), custom_call_target="tpu_custom_call" | custom-call | flops 1000000000 | bytes 3000000 | tf_op jit(solution)/shard_map/basis_and_errors/pallas_call | solution.py:604
  550.0 3.4 norm_back_into.3
  (453 shorter events, 127.4 us)
Async XLA Ops:
  7.2 61.0 %all-gather.3.cloned.1.call-start = ((), (), s32[]{:S(2)}) async-start(), calls=%async_computation | async-start | bytes 2949120 | tf_op jit(solution)/shard_map/all_gather | solution.py:986
  10.2 140.9 %all-gather.5.cloned.1.call-start = ((), (), s32[]{:S(2)}) async-start(), calls=%async_computation.1 | async-start | bytes 5308416 | tf_op jit(solution)/shard_map/all_gather | solution.py:989
  12.5 16.0 %collective-permute-start.1 = (bf16[256,1024]{1,0:T(8,128)(2,1)}, bf16[256,1024]{1,0:T(8,128)(2,1)}, u32[]{:S(2)}, u32[]{:S(2)}) collective-permute-start(bf16[256,1024]{1,0:T(8,128)(2,1)} %get-tuple-element.311), channel_id=1, source_target_pairs={{0,2},{1,3},{2,0},{3,1},{4,6},{5,7},{6,4},{7,5},{8,10},{9,11},{10,... | collective-permute-start | bytes 1572872 | tf_op jit(solution)/shard_map/ppermute | solution.py:928
  15.5 25.2 %collective-permute-start = (bf16[256,1024]{1,0:T(8,128)(2,1)}, bf16[256,1024]{1,0:T(8,128)(2,1)}, u32[]{:S(2)}, u32[]{:S(2)}) collective-permute-start(bf16[256,1024]{1,0:T(8,128)(2,1)} %get-tuple-element.311), channel_id=1, source_target_pairs={{0,1},{1,0},{2,3},{3,2},{4,5},{5,4},{6,7},{7,6},{8,9},{9,8},{10,11... | collective-permute-start | bytes 1572872 | tf_op jit(solution)/shard_map/ppermute | solution.py:928
  15.5 23.5 %collective-permute-start.4 = (bf16[256,1024]{1,0:T(8,128)(2,1)}, bf16[256,1024]{1,0:T(8,128)(2,1)}, u32[]{:S(2)}, u32[]{:S(2)}) collective-permute-start(bf16[256,1024]{1,0:T(8,128)(2,1)} %get-tuple-element.310), channel_id=1, source_target_pairs={{0,2},{1,3},{2,0},{3,1},{4,6},{5,7},{6,4},{7,5},{8,10},{9,11},{10,... | collective-permute-start | bytes 1572872 | tf_op jit(solution)/shard_map/ppermute | solution.py:928
  15.6 31.9 %collective-permute-start.3 = (bf16[256,1024]{1,0:T(8,128)(2,1)}, bf16[256,1024]{1,0:T(8,128)(2,1)}, u32[]{:S(2)}, u32[]{:S(2)}) collective-permute-start(bf16[256,1024]{1,0:T(8,128)(2,1)} %get-tuple-element.310), channel_id=1, source_target_pairs={{0,1},{1,0},{2,3},{3,2},{4,5},{5,4},{6,7},{7,6},{8,9},{9,8},{10,11... | collective-permute-start | bytes 1572872 | tf_op jit(solution)/shard_map/ppermute | solution.py:928
  22.1 121.3 %copy-start.77 = (s32[1024]{0:T(1024)}, s32[1024]{0:T(1024)S(1)}, u32[]{:S(2)}) copy-start(s32[1024]{0:T(1024)S(1)} %fusion.87) | copy-start | bytes 12292
  28.5 12.2 %collective-permute-start.2 = (bf16[256,1024]{1,0:T(8,128)(2,1)}, bf16[256,1024]{1,0:T(8,128)(2,1)}, u32[]{:S(2)}, u32[]{:S(2)}) collective-permute-start(bf16[256,1024]{1,0:T(8,128)(2,1)} %collective-permute-done.1), channel_id=1, source_target_pairs={{0,1},{1,0},{2,3},{3,2},{4,5},{5,4},{6,7},{7,6},{8,9},{9,8},{10,11... | collective-permute-start | bytes 1572872 | tf_op jit(solution)/shard_map/ppermute | solution.py:928
  34.7 69.0 %copy-start.47 = (bf16[1024,2]{0,1:T(2,128)(2,1)}, bf16[1024,2]{0,1:T(2,128)(2,1)S(1)}, u32[]{:S(2)}) copy-start(bf16[1024,2]{0,1:T(2,128)(2,1)S(1)} %convert_element_type.98) | copy-start | bytes 12292
  38.9 67.6 %collective-permute-start.12 = (bf16[256,1024]{1,0:T(8,128)(2,1)}, bf16[256,1024]{1,0:T(8,128)(2,1)}, u32[]{:S(2)}, u32[]{:S(2)}) collective-permute-start(bf16[256,1024]{1,0:T(8,128)(2,1)} %gate.4.refs_4_), channel_id=1, source_target_pairs={{0,2},{1,3},{2,0},{3,1},{4,6},{5,7},{6,4},{7,5},{8,10},{9,11},{10,... | collective-permute-start | bytes 1572872 | tf_op jit(solution)/shard_map/ppermute | solution.py:928
  40.7 6.8 %collective-permute-start.5 = (bf16[256,1024]{1,0:T(8,128)(2,1)}, bf16[256,1024]{1,0:T(8,128)(2,1)S(1)}, u32[]{:S(2)}, u32[]{:S(2)}) collective-permute-start(bf16[256,1024]{1,0:T(8,128)(2,1)} %collective-permute-done.4.refs_1_), channel_id=1, source_target_pairs={{0,1},{1,0},{2,3},{3,2},{4,5},{5,4},{6,7},{7,6},{8,9},{9,8},{10,11... | collective-permute-start | bytes 1572872 | tf_op jit(solution)/shard_map/ppermute | solution.py:928
  100.6 11.9 %collective-permute-start.6 = (bf16[2,256,1024]{2,1,0:T(8,128)(2,1)}, bf16[2,256,1024]{2,1,0:T(8,128)(2,1)}, u32[]{:S(2)}, u32[]{:S(2)}) collective-permute-start(bf16[2,256,1024]{2,1,0:T(8,128)(2,1)} %get-tuple-element.308), channel_id=1, source_target_pairs={{0,1},{1,0},{2,3},{3,2},{4,5},{5,4},{6,7},{7,6},{8,9},{9,8},{10,11... | collective-permute-start | bytes 3145736 | tf_op jit(solution)/shard_map/ppermute | solution.py:928
  101.7 48.3 %collective-permute-start.11 = (bf16[256,1024]{1,0:T(8,128)(2,1)}, bf16[256,1024]{1,0:T(8,128)(2,1)}, u32[]{:S(2)}, u32[]{:S(2)}) collective-permute-start(bf16[256,1024]{1,0:T(8,128)(2,1)} %gate.4.refs_4_), channel_id=1, source_target_pairs={{0,1},{1,0},{2,3},{3,2},{4,5},{5,4},{6,7},{7,6},{8,9},{9,8},{10,11... | collective-permute-start | bytes 1572872 | tf_op jit(solution)/shard_map/ppermute | solution.py:928
  102.2 93.4 %collective-permute-start.21 = (bf16[256,1024]{1,0:T(8,128)(2,1)}, bf16[256,1024]{1,0:T(8,128)(2,1)}, u32[]{:S(2)}, u32[]{:S(2)}) collective-permute-start(bf16[256,1024]{1,0:T(8,128)(2,1)} %gate.5.refs_2_), channel_id=1, source_target_pairs={{0,2},{1,3},{2,0},{3,1},{4,6},{5,7},{6,4},{7,5},{8,10},{9,11},{10,... | collective-permute-start | bytes 1572872 | tf_op jit(solution)/shard_map/ppermute | solution.py:928
  106.5 43.9 %collective-permute-start.13 = (bf16[256,1024]{1,0:T(8,128)(2,1)}, bf16[256,1024]{1,0:T(8,128)(2,1)}, u32[]{:S(2)}, u32[]{:S(2)}) collective-permute-start(bf16[256,1024]{1,0:T(8,128)(2,1)} %collective-permute-done.12.refs_6_), channel_id=1, source_target_pairs={{0,1},{1,0},{2,3},{3,2},{4,5},{5,4},{6,7},{7,6},{8,9},{9,8},{10,11... | collective-permute-start | bytes 1572872 | tf_op jit(solution)/shard_map/ppermute | solution.py:928
  114.7 14.5 %collective-permute-start.7 = (bf16[256,1024]{1,0:T(8,128)(2,1)}, bf16[256,1024]{1,0:T(8,128)(2,1)S(1)}, u32[]{:S(2)}, u32[]{:S(2)}) collective-permute-start(bf16[256,1024]{1,0:T(8,128)(2,1)} %pass_on.8.refs_6_), channel_id=1, source_target_pairs={{0,2},{1,3},{2,0},{3,1},{4,6},{5,7},{6,4},{7,5},{8,10},{9,11},{10,... | collective-permute-start | bytes 1572872 | tf_op jit(solution)/shard_map/ppermute | solution.py:928
  133.0 13.9 %collective-permute-start.9 = (bf16[256,1024]{1,0:T(8,128)(2,1)}, bf16[256,1024]{1,0:T(8,128)(2,1)S(1)}, u32[]{:S(2)}, u32[]{:S(2)}) collective-permute-start(bf16[256,1024]{1,0:T(8,128)(2,1)} %get-tuple-element.105.refs_6_.refs_0_), channel_id=1, source_target_pairs={{0,2},{1,3},{2,0},{3,1},{4,6},{5,7},{6,4},{7,5},{8,10},{9,11},{10,... | collective-permute-start | bytes 1572872 | tf_op jit(solution)/shard_map/ppermute | solution.py:928
  143.4 7.0 %collective-permute-start.8 = (bf16[256,1024]{1,0:T(8,128)(2,1)S(1)}, bf16[256,1024]{1,0:T(8,128)(2,1)S(1)}, u32[]{:S(2)}, u32[]{:S(2)}) collective-permute-start(bf16[256,1024]{1,0:T(8,128)(2,1)S(1)} %copy-done.91), channel_id=1, source_target_pairs={{0,1},{1,0},{2,3},{3,2},{4,5},{5,4},{6,7},{7,6},{8,9},{9,8},{10,11... | collective-permute-start | bytes 1572872 | tf_op jit(solution)/shard_map/ppermute | solution.py:928
  146.8 4.3 collective-permute-start.10
  150.0 21.2 %collective-permute-start.16 = (bf16[2,256,1024]{2,1,0:T(8,128)(2,1)S(1)}, bf16[2,256,1024]{2,1,0:T(8,128)(2,1)}, u32[]{:S(2)}, u32[]{:S(2)}) collective-permute-start(bf16[2,256,1024]{2,1,0:T(8,128)(2,1)S(1)} %get-tuple-element.307.refs_11_), channel_id=1, source_target_pairs={{0,1},{1,0},{2,3},{3,2},{4,5},{5,4},{6,7},{7,6},{8,9},{9,8},{10,11... | collective-permute-start | bytes 3145736 | tf_op jit(solution)/shard_map/ppermute | solution.py:928
  170.8 24.7 %collective-permute-start.15 = (bf16[2,256,1024]{2,1,0:T(8,128)(2,1)}, bf16[2,256,1024]{2,1,0:T(8,128)(2,1)}, u32[]{:S(2)}, u32[]{:S(2)}) collective-permute-start(bf16[2,256,1024]{2,1,0:T(8,128)(2,1)} %get-tuple-element.109.refs_2_), channel_id=1, source_target_pairs={{0,1},{1,0},{2,3},{3,2},{4,5},{5,4},{6,7},{7,6},{8,9},{9,8},{10,11... | collective-permute-start | bytes 3145736 | tf_op jit(solution)/shard_map/ppermute | solution.py:928
  173.5 14.3 %collective-permute-start.17 = (bf16[256,1024]{1,0:T(8,128)(2,1)}, bf16[256,1024]{1,0:T(8,128)(2,1)S(1)}, u32[]{:S(2)}, u32[]{:S(2)}) collective-permute-start(bf16[256,1024]{1,0:T(8,128)(2,1)} %pass_on.9), channel_id=1, source_target_pairs={{0,2},{1,3},{2,0},{3,1},{4,6},{5,7},{6,4},{7,5},{8,10},{9,11},{10,... | collective-permute-start | bytes 1572872 | tf_op jit(solution)/shard_map/ppermute | solution.py:928
  191.5 13.4 %collective-permute-start.18 = (bf16[256,1024]{1,0:T(8,128)(2,1)}, bf16[256,1024]{1,0:T(8,128)(2,1)S(1)}, u32[]{:S(2)}, u32[]{:S(2)}) collective-permute-start(bf16[256,1024]{1,0:T(8,128)(2,1)} %get-tuple-element.114.refs_0_.refs_7_), channel_id=1, source_target_pairs={{0,2},{1,3},{2,0},{3,1},{4,6},{5,7},{6,4},{7,5},{8,10},{9,11},{10,... | collective-permute-start | bytes 1572872 | tf_op jit(solution)/shard_map/ppermute | solution.py:928
  192.3 16.4 %collective-permute-start.24 = (bf16[256,1024]{1,0:T(8,128)(2,1)S(1)}, bf16[256,1024]{1,0:T(8,128)(2,1)}, u32[]{:S(2)}, u32[]{:S(2)}) collective-permute-start(bf16[256,1024]{1,0:T(8,128)(2,1)S(1)} %copy-done.14), channel_id=1, source_target_pairs={{0,1},{1,0},{2,3},{3,2},{4,5},{5,4},{6,7},{7,6},{8,9},{9,8},{10,11... | collective-permute-start | bytes 1572872 | tf_op jit(solution)/shard_map/ppermute | solution.py:928
  192.3 16.4 %collective-permute-start.23 = (bf16[256,1024]{1,0:T(8,128)(2,1)}, bf16[256,1024]{1,0:T(8,128)(2,1)}, u32[]{:S(2)}, u32[]{:S(2)}) collective-permute-start(bf16[256,1024]{1,0:T(8,128)(2,1)} %get-tuple-element.114.refs_0_.refs_7_), channel_id=1, source_target_pairs={{0,1},{1,0},{2,3},{3,2},{4,5},{5,4},{6,7},{7,6},{8,9},{9,8},{10,11... | collective-permute-start | bytes 1572872 | tf_op jit(solution)/shard_map/ppermute | solution.py:928
  195.5 25.8 %collective-permute-start.22 = (bf16[256,1024]{1,0:T(8,128)(2,1)}, bf16[256,1024]{1,0:T(8,128)(2,1)S(1)}, u32[]{:S(2)}, u32[]{:S(2)}) collective-permute-start(bf16[256,1024]{1,0:T(8,128)(2,1)} %collective-permute-done.21.refs_2_), channel_id=1, source_target_pairs={{0,1},{1,0},{2,3},{3,2},{4,5},{5,4},{6,7},{7,6},{8,9},{9,8},{10,11... | collective-permute-start | bytes 1572872 | tf_op jit(solution)/shard_map/ppermute | solution.py:928
  195.5 104.1 %collective-permute-start.14 = (bf16[2,256,1024]{2,1,0:T(8,128)(2,1)}, bf16[2,256,1024]{2,1,0:T(8,128)(2,1)}, u32[]{:S(2)}, u32[]{:S(2)}) collective-permute-start(bf16[2,256,1024]{2,1,0:T(8,128)(2,1)} %get-tuple-element.107), channel_id=1, source_target_pairs={{0,1},{1,0},{2,3},{3,2},{4,5},{5,4},{6,7},{7,6},{8,9},{9,8},{10,11... | collective-permute-start | bytes 3145736 | tf_op jit(solution)/shard_map/ppermute | solution.py:928
  207.9 27.8 %collective-permute-start.19 = (bf16[256,1024]{1,0:T(8,128)(2,1)}, bf16[256,1024]{1,0:T(8,128)(2,1)S(1)}, u32[]{:S(2)}, u32[]{:S(2)}) collective-permute-start(bf16[256,1024]{1,0:T(8,128)(2,1)} %pass_on.10.refs_17_), channel_id=1, source_target_pairs={{0,2},{1,3},{2,0},{3,1},{4,6},{5,7},{6,4},{7,5},{8,10},{9,11},{10,... | collective-permute-start | bytes 1572872 | tf_op jit(solution)/shard_map/ppermute | solution.py:928
  208.6 12.7 %collective-permute-start.20 = (bf16[256,1024]{1,0:T(8,128)(2,1)}, bf16[256,1024]{1,0:T(8,128)(2,1)S(1)}, u32[]{:S(2)}, u32[]{:S(2)}) collective-permute-start(bf16[256,1024]{1,0:T(8,128)(2,1)} %copy-done.90), channel_id=1, source_target_pairs={{0,1},{1,0},{2,3},{3,2},{4,5},{5,4},{6,7},{7,6},{8,9},{9,8},{10,11... | collective-permute-start | bytes 1572872 | tf_op jit(solution)/shard_map/ppermute | solution.py:928
  208.6 34.0 %slice-start = ((s8[5767168]{0:T(1024)(128)(4,1)}), s8[4194304]{0:T(1024)(128)(4,1)S(1)}, s32[]{:S(2)}) async-start(s8[5767168]{0:T(1024)(128)(4,1)} %bitcast.268), calls=%async_computation.2 | async-start | bytes 8388608
  235.2 26.8 %collective-permute-start.29 = (bf16[2,256,1024]{2,1,0:T(8,128)(2,1)}, bf16[2,256,1024]{2,1,0:T(8,128)(2,1)S(1)}, u32[]{:S(2)}, u32[]{:S(2)}) collective-permute-start(bf16[2,256,1024]{2,1,0:T(8,128)(2,1)} %get-tuple-element.125.refs_6_), channel_id=1, source_target_pairs={{0,1},{1,0},{2,3},{3,2},{4,5},{5,4},{6,7},{7,6},{8,9},{9,8},{10,11... | collective-permute-start | bytes 3145736 | tf_op jit(solution)/shard_map/ppermute | solution.py:928
  240.4 18.1 %collective-permute-start.25 = (bf16[256,1024]{1,0:T(8,128)(2,1)}, bf16[256,1024]{1,0:T(8,128)(2,1)}, u32[]{:S(2)}, u32[]{:S(2)}) collective-permute-start(bf16[256,1024]{1,0:T(8,128)(2,1)} %get-tuple-element.126.refs_2_), channel_id=1, source_target_pairs={{0,1},{1,0},{2,3},{3,2},{4,5},{5,4},{6,7},{7,6},{8,9},{9,8},{10,11... | collective-permute-start | bytes 1572872 | tf_op jit(solution)/shard_map/ppermute | solution.py:928
  240.4 15.8 %collective-permute-start.26 = (bf16[256,1024]{1,0:T(8,128)(2,1)}, bf16[256,1024]{1,0:T(8,128)(2,1)}, u32[]{:S(2)}, u32[]{:S(2)}) collective-permute-start(bf16[256,1024]{1,0:T(8,128)(2,1)} %get-tuple-element.126.refs_2_), channel_id=1, source_target_pairs={{0,2},{1,3},{2,0},{3,1},{4,6},{5,7},{6,4},{7,5},{8,10},{9,11},{10,... | collective-permute-start | bytes 1572872 | tf_op jit(solution)/shard_map/ppermute | solution.py:928
  241.8 14.4 %collective-permute-start.28 = (f32[8,2752]{1,0:T(8,128)S(1)}, f32[8,2752]{1,0:T(8,128)S(1)}, u32[]{:S(2)}, u32[]{:S(2)}) collective-permute-start(f32[8,2752]{1,0:T(8,128)S(1)} %maximum_add_fusion.refs_0_), channel_id=1, source_target_pairs={{0,4},{4,0},{8,12},{12,8},{16,20},{20,16},{24,28},{28,24},{1,5},{5... | collective-permute-start | bytes 264200 | tf_op jit(solution)/shard_map/ppermute | solution.py:928
  256.2 10.1 %collective-permute-start.27 = (bf16[256,1024]{1,0:T(8,128)(2,1)}, bf16[256,1024]{1,0:T(8,128)(2,1)S(1)}, u32[]{:S(2)}, u32[]{:S(2)}) collective-permute-start(bf16[256,1024]{1,0:T(8,128)(2,1)} %collective-permute-done.26), channel_id=1, source_target_pairs={{0,1},{1,0},{2,3},{3,2},{4,5},{5,4},{6,7},{7,6},{8,9},{9,8},{10,11... | collective-permute-start | bytes 1572872 | tf_op jit(solution)/shard_map/ppermute | solution.py:928
  256.3 104.9 %collective-permute-start.31 = (bf16[2,256,1024]{2,1,0:T(8,128)(2,1)}, bf16[2,256,1024]{2,1,0:T(8,128)(2,1)}, u32[]{:S(2)}, u32[]{:S(2)}) collective-permute-start(bf16[2,256,1024]{2,1,0:T(8,128)(2,1)} %get-tuple-element.139), channel_id=1, source_target_pairs={{0,1},{1,0},{2,3},{3,2},{4,5},{5,4},{6,7},{7,6},{8,9},{9,8},{10,11... | collective-permute-start | bytes 3145736 | tf_op jit(solution)/shard_map/ppermute | solution.py:928
  258.5 38.4 %collective-permute-start.32 = (f32[8,2752]{1,0:T(8,128)}, f32[8,2752]{1,0:T(8,128)S(1)}, u32[]{:S(2)}, u32[]{:S(2)}) collective-permute-start(f32[8,2752]{1,0:T(8,128)} %add_after.9.refs_10_.refs_0_), channel_id=1, source_target_pairs={{0,8},{4,12},{8,0},{12,4},{16,24},{20,28},{24,16},{28,20},{1,9},{5... | collective-permute-start | bytes 264200 | tf_op jit(solution)/shard_map/ppermute | solution.py:928
  265.2 38.2 %collective-permute-start.33 = (bf16[256,1024]{1,0:T(8,128)(2,1)}, bf16[256,1024]{1,0:T(8,128)(2,1)S(1)}, u32[]{:S(2)}, u32[]{:S(2)}) collective-permute-start(bf16[256,1024]{1,0:T(8,128)(2,1)} %pass_on.11.refs_11_), channel_id=1, source_target_pairs={{0,2},{1,3},{2,0},{3,1},{4,6},{5,7},{6,4},{7,5},{8,10},{9,11},{10,... | collective-permute-start | bytes 1572872 | tf_op jit(solution)/shard_map/ppermute | solution.py:928
  299.1 51.5 %collective-permute-start.38 = (f32[8,2752]{1,0:T(8,128)}, f32[8,2752]{1,0:T(8,128)S(1)}, u32[]{:S(2)}, u32[]{:S(2)}) collective-permute-start(f32[8,2752]{1,0:T(8,128)} %add_after.10.refs_10_.refs_0_), channel_id=1, source_target_pairs={{0,16},{4,20},{8,24},{12,28},{16,0},{20,4},{24,8},{28,12},{1,17},{... | collective-permute-start | bytes 264200 | tf_op jit(solution)/shard_map/ppermute | solution.py:928
  301.8 192.3 %collective-permute-start.30 = (bf16[256,1024]{1,0:T(8,128)(2,1)}, bf16[256,1024]{1,0:T(8,128)(2,1)}, u32[]{:S(2)}, u32[]{:S(2)}) collective-permute-start(bf16[256,1024]{1,0:T(8,128)(2,1)} %pass_on.12), channel_id=1, source_target_pairs={{0,2},{1,3},{2,0},{3,1},{4,6},{5,7},{6,4},{7,5},{8,10},{9,11},{10,... | collective-permute-start | bytes 1572872 | tf_op jit(solution)/shard_map/ppermute | solution.py:928
  307.9 55.0 %collective-permute-start.36 = (bf16[256,1024]{1,0:T(8,128)(2,1)}, bf16[256,1024]{1,0:T(8,128)(2,1)}, u32[]{:S(2)}, u32[]{:S(2)}) collective-permute-start(bf16[256,1024]{1,0:T(8,128)(2,1)} %get-tuple-element.141.refs_11_), channel_id=1, source_target_pairs={{0,2},{1,3},{2,0},{3,1},{4,6},{5,7},{6,4},{7,5},{8,10},{9,11},{10,... | collective-permute-start | bytes 1572872 | tf_op jit(solution)/shard_map/ppermute | solution.py:928
  308.4 26.9 %copy-start.112 = (bf16[4,128,1024]{2,1,0:T(8,128)(2,1)S(1)}, bf16[4,128,1024]{2,1,0:T(8,128)(2,1)}, u32[]{:S(2)}) copy-start(bf16[4,128,1024]{2,1,0:T(8,128)(2,1)} %get-tuple-element.147) | copy-start | bytes 3145732
  344.4 24.5 %collective-permute-start.45 = (bf16[2,256,1024]{2,1,0:T(8,128)(2,1)}, bf16[2,256,1024]{2,1,0:T(8,128)(2,1)S(1)}, u32[]{:S(2)}, u32[]{:S(2)}) collective-permute-start(bf16[2,256,1024]{2,1,0:T(8,128)(2,1)} %get-tuple-element.298), channel_id=1, source_target_pairs={{0,1},{1,0},{2,3},{3,2},{4,5},{5,4},{6,7},{7,6},{8,9},{9,8},{10,11... | collective-permute-start | bytes 3145736 | tf_op jit(solution)/shard_map/ppermute | solution.py:928
  350.6 15.7 %collective-permute-start.35 = (bf16[256,1024]{1,0:T(8,128)(2,1)}, bf16[256,1024]{1,0:T(8,128)(2,1)S(1)}, u32[]{:S(2)}, u32[]{:S(2)}) collective-permute-start(bf16[256,1024]{1,0:T(8,128)(2,1)} %get-tuple-element.141.refs_11_), channel_id=1, source_target_pairs={{0,1},{1,0},{2,3},{3,2},{4,5},{5,4},{6,7},{7,6},{8,9},{9,8},{10,11... | collective-permute-start | bytes 1572872 | tf_op jit(solution)/shard_map/ppermute | solution.py:928
  361.2 48.6 %collective-permute-start.39 = (f32[8,2432]{1,0:T(8,128)}, f32[8,2432]{1,0:T(8,128)S(1)}, u32[]{:S(2)}, u32[]{:S(2)}) collective-permute-start(f32[8,2432]{1,0:T(8,128)} %get-tuple-element.144.refs_10_.refs_0_), channel_id=1, source_target_pairs={{0,4},{4,0},{8,12},{12,8},{16,20},{20,16},{24,28},{28,24},{1,5},{5... | collective-permute-start | bytes 233480 | tf_op jit(solution)/shard_map/ppermute | solution.py:928
  362.9 9.8 %collective-permute-start.37 = (bf16[256,1024]{1,0:T(8,128)(2,1)}, bf16[256,1024]{1,0:T(8,128)(2,1)S(1)}, u32[]{:S(2)}, u32[]{:S(2)}) collective-permute-start(bf16[256,1024]{1,0:T(8,128)(2,1)} %collective-permute-done.36), channel_id=1, source_target_pairs={{0,1},{1,0},{2,3},{3,2},{4,5},{5,4},{6,7},{7,6},{8,9},{9,8},{10,11... | collective-permute-start | bytes 1572872 | tf_op jit(solution)/shard_map/ppermute | solution.py:928
  366.3 128.5 %collective-permute-start.34 = (bf16[256,1024]{1,0:T(8,128)(2,1)}, bf16[256,1024]{1,0:T(8,128)(2,1)}, u32[]{:S(2)}, u32[]{:S(2)}) collective-permute-start(bf16[256,1024]{1,0:T(8,128)(2,1)} %pass_on.13), channel_id=1, source_target_pairs={{0,2},{1,3},{2,0},{3,1},{4,6},{5,7},{6,4},{7,5},{8,10},{9,11},{10,... | collective-permute-start | bytes 1572872 | tf_op jit(solution)/shard_map/ppermute | solution.py:928
  372.0 152.1 %collective-permute-start.46 = (bf16[256,1024]{1,0:T(8,128)(2,1)}, bf16[256,1024]{1,0:T(8,128)(2,1)S(1)}, u32[]{:S(2)}, u32[]{:S(2)}) collective-permute-start(bf16[256,1024]{1,0:T(8,128)(2,1)} %pass_on.15), channel_id=1, source_target_pairs={{0,2},{1,3},{2,0},{3,1},{4,6},{5,7},{6,4},{7,5},{8,10},{9,11},{10,... | collective-permute-start | bytes 1572872 | tf_op jit(solution)/shard_map/ppermute | solution.py:928
  411.9 25.5 %copy-start.79 = (f32[1,1,1024]{2,1,0:T(1,128)S(1)}, f32[1,1,1024]{2,1,0:T(1,128)}, u32[]{:S(2)}) copy-start(f32[1,1,1024]{2,1,0:T(1,128)} %get-tuple-element.154) | copy-start | bytes 12292
  437.5 12.1 %collective-permute-start.40 = (f32[8,4352]{1,0:T(8,128)}, f32[8,4352]{1,0:T(8,128)S(1)}, u32[]{:S(2)}, u32[]{:S(2)}) collective-permute-start(f32[8,4352]{1,0:T(8,128)} %get-tuple-element.151.refs_0_), channel_id=1, source_target_pairs={{0,4},{4,0},{8,12},{12,8},{16,20},{20,16},{24,28},{28,24},{1,5},{5... | collective-permute-start | bytes 417800 | tf_op jit(solution)/shard_map/ppermute | solution.py:928
  462.1 1.7 collective-permute-start.47
  462.2 9.1 %collective-permute-start.41 = (f32[8,4352]{1,0:T(8,128)S(1)}, f32[8,4352]{1,0:T(8,128)S(1)}, u32[]{:S(2)}, u32[]{:S(2)}) collective-permute-start(f32[8,4352]{1,0:T(8,128)S(1)} %copy-done.26), channel_id=1, source_target_pairs={{0,8},{4,12},{8,0},{12,4},{16,24},{20,28},{24,16},{28,20},{1,9},{5... | collective-permute-start | bytes 417800 | tf_op jit(solution)/shard_map/ppermute | solution.py:928
  465.7 3.9 collective-permute-start.48
  469.5 21.1 %collective-permute-start.54 = (f32[8,2432]{1,0:T(8,128)S(1)}, f32[8,2432]{1,0:T(8,128)S(1)}, u32[]{:S(2)}, u32[]{:S(2)}) collective-permute-start(f32[8,2432]{1,0:T(8,128)S(1)} %copy-done.99), channel_id=1, source_target_pairs={{0,8},{4,12},{8,0},{12,4},{16,24},{20,28},{24,16},{28,20},{1,9},{5... | collective-permute-start | bytes 233480 | tf_op jit(solution)/shard_map/ppermute | solution.py:928
  474.6 8.9 %collective-permute-start.42 = (f32[8,4352]{1,0:T(8,128)S(1)}, f32[8,4352]{1,0:T(8,128)S(1)}, u32[]{:S(2)}, u32[]{:S(2)}) collective-permute-start(f32[8,4352]{1,0:T(8,128)S(1)} %copy-done.20), channel_id=1, source_target_pairs={{0,16},{4,20},{8,24},{12,28},{16,0},{20,4},{24,8},{28,12},{1,17},{... | collective-permute-start | bytes 417800 | tf_op jit(solution)/shard_map/ppermute | solution.py:928
  483.4 16.9 %collective-permute-start.50 = (f32[58,128]{1,0:T(8,128)S(1)}, f32[58,128]{1,0:T(8,128)S(1)}, u32[]{:S(2)}, u32[]{:S(2)}) collective-permute-start(f32[58,128]{1,0:T(8,128)S(1)} %pad_maximum_fusion.6.refs_1_), channel_id=1, source_target_pairs={{0,4},{4,0},{8,12},{12,8},{16,20},{20,16},{24,28},{28,24},{1,5},{5... | collective-permute-start | bytes 89096 | tf_op jit(solution)/shard_map/ppermute | solution.py:928
  490.6 43.0 %collective-permute-start.43 = (bf16[2,256,1024]{2,1,0:T(8,128)(2,1)S(1)}, bf16[2,256,1024]{2,1,0:T(8,128)(2,1)S(1)}, u32[]{:S(2)}, u32[]{:S(2)}) collective-permute-start(bf16[2,256,1024]{2,1,0:T(8,128)(2,1)S(1)} %get-tuple-element.300), channel_id=1, source_target_pairs={{0,1},{1,0},{2,3},{3,2},{4,5},{5,4},{6,7},{7,6},{8,9},{9,8},{10,11... | collective-permute-start | bytes 3145736 | tf_op jit(solution)/shard_map/ppermute | solution.py:928
  494.1 6.2 %collective-permute-start.49 = (f32[8,2048]{1,0:T(8,128)S(1)}, f32[8,2048]{1,0:T(8,128)S(1)}, u32[]{:S(2)}, u32[]{:S(2)}) collective-permute-start(f32[8,2048]{1,0:T(8,128)S(1)} %copy-done.38), channel_id=1, source_target_pairs={{0,4},{4,0},{8,12},{12,8},{16,20},{20,16},{24,28},{28,24},{1,5},{5... | collective-permute-start | bytes 196616 | tf_op jit(solution)/shard_map/ppermute | solution.py:928
  494.8 10.3 %collective-permute-start.55 = (f32[8,2432]{1,0:T(8,128)}, f32[8,2432]{1,0:T(8,128)S(1)}, u32[]{:S(2)}, u32[]{:S(2)}) collective-permute-start(f32[8,2432]{1,0:T(8,128)} %add_after.17.refs_1_), channel_id=1, source_target_pairs={{0,16},{4,20},{8,24},{12,28},{16,0},{20,4},{24,8},{28,12},{1,17},{... | collective-permute-start | bytes 233480 | tf_op jit(solution)/shard_map/ppermute | solution.py:928
  503.1 16.4 %collective-permute-start.51 = (f32[8,2048]{1,0:T(8,128)}, f32[8,2048]{1,0:T(8,128)S(1)}, u32[]{:S(2)}, u32[]{:S(2)}) collective-permute-start(f32[8,2048]{1,0:T(8,128)} %get-tuple-element.167.refs_0_), channel_id=1, source_target_pairs={{0,8},{4,12},{8,0},{12,4},{16,24},{20,28},{24,16},{28,20},{1,9},{5... | collective-permute-start | bytes 196616 | tf_op jit(solution)/shard_map/ppermute | solution.py:928
  504.0 15.4 %collective-permute-start.52 = (f32[58,128]{1,0:T(8,128)}, f32[58,128]{1,0:T(8,128)S(1)}, u32[]{:S(2)}, u32[]{:S(2)}) collective-permute-start(f32[58,128]{1,0:T(8,128)} %get-tuple-element.168.refs_1_), channel_id=1, source_target_pairs={{0,8},{4,12},{8,0},{12,4},{16,24},{20,28},{24,16},{28,20},{1,9},{5... | collective-permute-start | bytes 89096 | tf_op jit(solution)/shard_map/ppermute | solution.py:928
  522.2 8.2 %collective-permute-start.56 = (f32[58,128]{1,0:T(8,128)}, f32[58,128]{1,0:T(8,128)S(1)}, u32[]{:S(2)}, u32[]{:S(2)}) collective-permute-start(f32[58,128]{1,0:T(8,128)} %get-tuple-element.181), channel_id=1, source_target_pairs={{0,16},{4,20},{8,24},{12,28},{16,0},{20,4},{24,8},{28,12},{1,17},{... | collective-permute-start | bytes 89096 | tf_op jit(solution)/shard_map/ppermute | solution.py:928
  528.8 8.8 %collective-permute-start.53 = (f32[8,2048]{1,0:T(8,128)S(1)}, f32[8,2048]{1,0:T(8,128)S(1)}, u32[]{:S(2)}, u32[]{:S(2)}) collective-permute-start(f32[8,2048]{1,0:T(8,128)S(1)} %copy-done.52), channel_id=1, source_target_pairs={{0,16},{4,20},{8,24},{12,28},{16,0},{20,4},{24,8},{28,12},{1,17},{... | collective-permute-start | bytes 196616 | tf_op jit(solution)/shard_map/ppermute | solution.py:928
  536.8 12.4 %collective-permute-start.44 = (bf16[256,1024]{1,0:T(8,128)(2,1)}, bf16[256,1024]{1,0:T(8,128)(2,1)S(1)}, u32[]{:S(2)}, u32[]{:S(2)}) collective-permute-start(bf16[256,1024]{1,0:T(8,128)(2,1)} %pass_on.14.refs_8_), channel_id=1, source_target_pairs={{0,2},{1,3},{2,0},{3,1},{4,6},{5,7},{6,4},{7,5},{8,10},{9,11},{10,... | collective-permute-start | bytes 1572872 | tf_op jit(solution)/shard_map/ppermute | solution.py:928
  (112 other events, 482.1 us)
Sparse Core Ops, SparseCore 0:
  10.8 57.3 all-gather.2
  71.0 78.4 all-gather.4
